TPU v7x, 128 devices: a whole 4x4x4 slice. The times are simulated.
128 devices in a mesh: chan: 8 (over y_hi, z), bin: 16 (over y_lo, x, core).
Axes of the slice: x: 4, y: 4 (y_hi: 2, y_lo: 2; y = y_hi * 2 + y_lo), z: 4, core: 2. Of those that a mesh axis runs over, the one named last changes fastest.
Arguments:
- spectra: bfloat16 [128, 2, 512, 2048], P('bin', None, None, 'chan')
- valid: int32 [16, 512], P('chan'), may hold values from 0 to 1, as said below
Outputs:
- stacked: bfloat16 [16, 9, 128, 2, 128, 128], P('chan', None, 'bin')
Inputs may be any that keep to these rules, and one draw needn't show every extreme that they name: `valid`: each entry is 0 or 1; in every draw exactly one channel block, drawn from the seed, has no usable segment at all.
All inputs are finite; a program needn't handle non-finite values.
Results may differ from a plain program's by a relative error of at most 0.0043.
Values may be sent and summed in bfloat16 or wider, within the bound.
No kernel may reach another device: no remote copies, remote signals or barrier semaphores. Data moves between devices by JAX's collectives and lax.ppermute only.
A program may use at most 128 MiB of HBM per device.

v0:
```python
import jax
import jax.numpy as jnp
from jax import lax
from jax.sharding import PartitionSpec as P


def shifted(block, axis, distance):
    devices = range(lax.axis_size(axis))
    route = [((i - distance) % len(devices), i) for i in devices]
    return lax.ppermute(block, axis, route)


def cross_block(left, right, left_mask, right_mask):
    total = jnp.maximum(jnp.sum(left_mask * right_mask), 1.0)
    real_part = jnp.einsum(
        "fsa,fsb->fab", left[:, 0], right[:, 0], preferred_element_type=jnp.float32
    )
    real_part = real_part + jnp.einsum(
        "fsa,fsb->fab", left[:, 1], right[:, 1], preferred_element_type=jnp.float32
    )
    imag_part = jnp.einsum(
        "fsa,fsb->fab", left[:, 1], right[:, 0], preferred_element_type=jnp.float32
    )
    imag_part = imag_part - jnp.einsum(
        "fsa,fsb->fab", left[:, 0], right[:, 1], preferred_element_type=jnp.float32
    )
    return (jnp.stack([real_part, imag_part], axis=1) / total).astype(jnp.bfloat16)


def shards(spectra, valid):
    bin_devices = lax.axis_size("bin")
    chan_devices = lax.axis_size("chan")
    bins_here = spectra.shape[0]
    blocks_here = valid.shape[0]
    width = spectra.shape[3] // blocks_here
    block_count = blocks_here * chan_devices
    offsets = block_count // 2 + 1
    spectra32 = spectra.astype(jnp.float32)
    partial_value = jnp.sum(jnp.sqrt(spectra32[:, 0] ** 2 + spectra32[:, 1] ** 2), axis=0)
    amplitude = lax.psum(partial_value, "bin")
    keep = jnp.repeat(valid.astype(jnp.float32).T, width, axis=1)
    white = (spectra32 / (amplitude / (bins_here * bin_devices) + 1e-06) * keep).astype(
        jnp.bfloat16
    )
    own_mask = valid.astype(jnp.float32)
    results = [[None] * offsets for row_block in range(blocks_here)]

    def fill(blocks, masks, offset):
        masks_float = masks.astype(jnp.float32)
        for row_block in range(blocks_here):
            for col_block in range(blocks_here):
                lag = offset * blocks_here + col_block - row_block
                if 0 <= lag < offsets:
                    left = white[..., row_block * width : (row_block + 1) * width]
                    right = blocks[..., col_block * width : (col_block + 1) * width]
                    results[row_block][lag] = cross_block(
                        left, right, own_mask[row_block], masks_float[col_block]
                    )

    fill(white, valid, 0)
    farthest = (blocks_here - 1 + block_count // 2) // blocks_here
    moving = (white, valid)
    for offset in range(1, farthest + 1):
        moving = shifted((moving[0], moving[1]), "chan", -1)
        fill(moving[0], moving[1], offset)
    return jnp.stack([jnp.stack(row_list) for row_list in results])


def solution(mesh):
    return jax.shard_map(
        shards,
        mesh=mesh,
        in_specs=(P("bin", None, None, "chan"), P("chan", None)),
        out_specs=P("chan", None, "bin", None, None, None),
        check_vma=False,
    )
```

profile of v0, /device:TPU:6, one launch (start us, length us, event | category | flops | bytes accessed | tf_op | source)
XLA Modules:
  0.0 633.6 jit_solution(6455354421108233897)
XLA Ops:
  6.5 3.1 copy_convert_fusion
  9.6 2.3 fusion.2
  12.8 116.6 %all-reduce.2.cloned.1.call-done = f32[512,256]{1,0:T(8,128)} async-done(((f32[512,256]{1,0:T(8,128)}), f32[512,256]{1,0:T(8,128)}) %all-reduce.2.cloned.1.call-update) | async-done | bytes 524304 | tf_op jit(solution)/shard_map/psum | solution.py:40
  130.5 4.2 multiply_convert_fusion
  134.7 5.1 collective-permute-start
  140.5 88.1 %collective-permute-done.1 = s32[2,512]{1,0:T(2,128)S(1)} collective-permute-done((s32[2,512]{1,0:T(2,128)S(1)}, s32[2,512]{1,0:T(2,128)S(1)}, u32[]{:S(2)}, u32[]{:S(2)}) %collective-permute-start.1) | collective-permute-done | bytes 4128 | tf_op jit(solution)/shard_map/ppermute | solution.py:10
  228.6 6.1 collective-permute-start.3
  236.0 5.9 collective-permute-start.5
  243.3 6.1 collective-permute-start.7
  262.6 2.1 fusion.108
  264.7 2.1 fusion.38
  266.8 2.0 fusion.107
  268.9 2.0 fusion.37
  271.8 2.1 fusion.111
  273.9 2.1 fusion.20
  276.0 2.0 fusion.110
  278.0 2.0 fusion.19
  280.2 2.0 fusion.109
  282.2 2.0 fusion.35
  284.3 2.0 fusion.106
  286.3 2.0 fusion.36
  289.2 2.0 fusion.60
  291.3 2.0 fusion.59
  293.3 6.2 collective-permute-start.2
  299.5 2.0 fusion.18
  301.5 2.0 fusion.17
  303.7 2.0 fusion.64
  305.8 2.0 fusion.16
  307.8 2.0 fusion.63
  309.8 2.0 fusion.15
  312.0 2.0 fusion.61
  314.1 2.0 fusion.33
  316.1 2.0 fusion.62
  318.1 2.0 fusion.34
  321.1 2.0 fusion.65
  323.1 2.0 fusion.31
  325.2 2.0 fusion.66
  327.2 2.0 fusion.32
  330.2 58.6 %collective-permute-done.2 = bf16[8,2,512,256]{3,2,0,1:T(8,128)(2,1)S(1)} collective-permute-done((bf16[8,2,512,256]{3,2,0,1:T(8,128)(2,1)}, bf16[8,2,512,256]{3,2,0,1:T(8,128)(2,1)S(1)}, u32[]{:S(2)}, u32[]{:S(2)}) %collective-permute-start.2) | collective-permute-done | bytes 4194336 | tf_op jit(solution)/shard_map/ppermute | solution.py:10
  392.2 6.5 %collective-permute-start.4 = (bf16[8,2,512,256]{3,2,0,1:T(8,128)(2,1)S(1)}, bf16[8,2,512,256]{3,2,0,1:T(8,128)(2,1)S(1)}, u32[]{:S(2)}, u32[]{:S(2)}) collective-permute-start(bf16[8,2,512,256]{3,2,0,1:T(8,128)(2,1)S(1)} %collective-permute-done.2), channel_id=1, source_target_pairs={{16,0},{32,16},{48,32},{64,48},{80,64},{96,80},{112,96},{0,112},{1... | collective-permute-start | bytes 12582920 | tf_op jit(solution)/shard_map/ppermute | solution.py:10
  400.5 1.7 fusion.13
  402.4 1.7 fusion.72
  404.1 1.7 fusion.12
  407.5 1.7 fusion.11
  411.2 1.7 fusion.29
  414.6 1.7 fusion.30
  419.0 1.7 fusion.27
  422.4 1.7 fusion.28
  425.1 61.7 %collective-permute-done.4 = bf16[8,2,512,256]{3,2,0,1:T(8,128)(2,1)S(1)} collective-permute-done((bf16[8,2,512,256]{3,2,0,1:T(8,128)(2,1)S(1)}, bf16[8,2,512,256]{3,2,0,1:T(8,128)(2,1)S(1)}, u32[]{:S(2)}, u32[]{:S(2)}) %collective-permute-start.4) | collective-permute-done | bytes 4194336 | tf_op jit(solution)/shard_map/ppermute | solution.py:10
  490.2 6.3 collective-permute-start.6
  496.5 1.7 fusion.10
  498.3 1.7 fusion.9
  500.2 1.7 fusion.80
  501.9 1.7 fusion.8
  507.3 1.7 fusion.77
  509.0 1.7 fusion.25
  512.4 1.7 fusion.26
  520.3 1.7 fusion.24
  523.0 60.7 %collective-permute-done.6 = bf16[8,2,512,256]{3,2,0,1:T(8,128)(2,1)S(1)} collective-permute-done((bf16[8,2,512,256]{3,2,0,1:T(8,128)(2,1)S(1)}, bf16[8,2,512,256]{3,2,0,1:T(8,128)(2,1)S(1)}, u32[]{:S(2)}, u32[]{:S(2)}) %collective-permute-start.6) | collective-permute-done | bytes 4194336 | tf_op jit(solution)/shard_map/ppermute | solution.py:10
  587.1 1.7 fusion.6
  597.8 2.5 fusion.85
  603.8 1.9 fusion.22
  606.6 8.3 %pad_maximum_fusion = bf16[2,9,8,2,128,128]{5,4,2,3,1,0:T(8,128)(2,1)} fusion(bf16[1,9,8,2,128,128]{5,4,2,3,1,0:T(8,128)(2,1)} %bitcast.260, bf16[1,9,8,2,128,128]{5,4,2,3,1,0:T(8,128)(2,1)} %bitcast.37), kind=kLoop, calls=%fused_computation | loop fusion | flops 4718592 | bytes 18874368 | tf_op jit(solution)/shard_map/stack | solution.py:66
  614.9 11.7 %copy.77 = bf16[2,9,8,2,128,128]{5,4,3,2,1,0:T(8,128)(2,1)} copy(bf16[2,9,8,2,128,128]{5,4,2,3,1,0:T(8,128)(2,1)} %pad_maximum_fusion) | data formatting | bytes 18874368 | tf_op jit(solution)/shard_map/stack | solution.py:66
  (64 shorter events, 60.3 us)
Async XLA Ops:
  6.5 122.9 %all-reduce.2.cloned.1.call-start = ((), (), s32[]{:S(2)}) async-start(), calls=%async_computation | async-start | bytes 1048576 | tf_op jit(solution)/shard_map/psum | solution.py:40
  9.6 2.3 copy-start.1
  134.7 154.6 %collective-permute-start = (bf16[8,2,512,256]{3,2,0,1:T(8,128)(2,1)}, bf16[8,2,512,256]{3,2,0,1:T(8,128)(2,1)}, u32[]{:S(2)}, u32[]{:S(2)}) collective-permute-start(bf16[8,2,512,256]{3,2,0,1:T(8,128)(2,1)} %multiply_convert_fusion), channel_id=1, source_target_pairs={{16,0},{32,16},{48,32},{64,48},{80,64},{96,80},{112,96},{0,112},{1... | collective-permute-start | bytes 12582920 | tf_op jit(solution)/shard_map/ppermute | solution.py:10
  139.8 88.8 %collective-permute-start.1 = (s32[2,512]{1,0:T(2,128)S(1)}, s32[2,512]{1,0:T(2,128)S(1)}, u32[]{:S(2)}, u32[]{:S(2)}) collective-permute-start(s32[2,512]{1,0:T(2,128)S(1)} %copy-done.1), channel_id=1, source_target_pairs={{16,0},{32,16},{48,32},{64,48},{80,64},{96,80},{112,96},{0,112},{1... | collective-permute-start | bytes 12296 | tf_op jit(solution)/shard_map/ppermute | solution.py:10
  228.6 7.4 %collective-permute-start.3 = (s32[2,512]{1,0:T(2,128)S(1)}, s32[2,512]{1,0:T(2,128)S(1)}, u32[]{:S(2)}, u32[]{:S(2)}) collective-permute-start(s32[2,512]{1,0:T(2,128)S(1)} %collective-permute-done.1), channel_id=1, source_target_pairs={{16,0},{32,16},{48,32},{64,48},{80,64},{96,80},{112,96},{0,112},{1... | collective-permute-start | bytes 12296 | tf_op jit(solution)/shard_map/ppermute | solution.py:10
  236.0 7.2 %collective-permute-start.5 = (s32[2,512]{1,0:T(2,128)S(1)}, s32[2,512]{1,0:T(2,128)S(1)}, u32[]{:S(2)}, u32[]{:S(2)}) collective-permute-start(s32[2,512]{1,0:T(2,128)S(1)} %collective-permute-done.3), channel_id=1, source_target_pairs={{16,0},{32,16},{48,32},{64,48},{80,64},{96,80},{112,96},{0,112},{1... | collective-permute-start | bytes 12296 | tf_op jit(solution)/shard_map/ppermute | solution.py:10
  243.3 7.4 %collective-permute-start.7 = (s32[2,512]{1,0:T(2,128)S(1)}, s32[2,512]{1,0:T(2,128)S(1)}, u32[]{:S(2)}, u32[]{:S(2)}) collective-permute-start(s32[2,512]{1,0:T(2,128)S(1)} %collective-permute-done.5), channel_id=1, source_target_pairs={{16,0},{32,16},{48,32},{64,48},{80,64},{96,80},{112,96},{0,112},{1... | collective-permute-start | bytes 12296 | tf_op jit(solution)/shard_map/ppermute | solution.py:10
  293.3 95.5 %collective-permute-start.2 = (bf16[8,2,512,256]{3,2,0,1:T(8,128)(2,1)}, bf16[8,2,512,256]{3,2,0,1:T(8,128)(2,1)S(1)}, u32[]{:S(2)}, u32[]{:S(2)}) collective-permute-start(bf16[8,2,512,256]{3,2,0,1:T(8,128)(2,1)} %collective-permute-done), channel_id=1, source_target_pairs={{16,0},{32,16},{48,32},{64,48},{80,64},{96,80},{112,96},{0,112},{1... | collective-permute-start | bytes 12582920 | tf_op jit(solution)/shard_map/ppermute | solution.py:10
  392.2 94.6 %collective-permute-start.4 = (bf16[8,2,512,256]{3,2,0,1:T(8,128)(2,1)S(1)}, bf16[8,2,512,256]{3,2,0,1:T(8,128)(2,1)S(1)}, u32[]{:S(2)}, u32[]{:S(2)}) collective-permute-start(bf16[8,2,512,256]{3,2,0,1:T(8,128)(2,1)S(1)} %collective-permute-done.2), channel_id=1, source_target_pairs={{16,0},{32,16},{48,32},{64,48},{80,64},{96,80},{112,96},{0,112},{1... | collective-permute-start | bytes 12582920 | tf_op jit(solution)/shard_map/ppermute | solution.py:10
  490.2 93.4 %collective-permute-start.6 = (bf16[8,2,512,256]{3,2,0,1:T(8,128)(2,1)S(1)}, bf16[8,2,512,256]{3,2,0,1:T(8,128)(2,1)S(1)}, u32[]{:S(2)}, u32[]{:S(2)}) collective-permute-start(bf16[8,2,512,256]{3,2,0,1:T(8,128)(2,1)S(1)} %collective-permute-done.4), channel_id=1, source_target_pairs={{16,0},{32,16},{48,32},{64,48},{80,64},{96,80},{112,96},{0,112},{1... | collective-permute-start | bytes 12582920 | tf_op jit(solution)/shard_map/ppermute | solution.py:10
  597.8 6.0 copy-start
Sparse Core Ops, SparseCore 0:
  12.1 117.2 all-reduce.1
where the time goes:
time: 641 us; the launch traced here: 634 us
  waiting for transfers between devices  390 us (61%)
  matrix products  134 us (21%)
  starting transfers between devices  43 us (7%)
  other arithmetic  29.7 us (5%)
  between operations  25.3 us (4%)
  local copies, waits for them, and re-layouts  12.5 us (2%)
    ppermute x8, waiting for transfers between devices, shifted(): return lax.ppermute(block, axis, route)  273 us
    psum x1, waiting for transfers between devices, shards(): amplitude = lax.psum(partial_value, 'bin')  117 us
    ppermute x8, starting transfers between devices, shifted(): return lax.ppermute(block, axis, route)  43 us
    dot_general x18, matrix products, cross_block(): jnp.einsum('fsa,fsb->fab', left[:, 0], right[:, 1], preferred_element_typ...  33.8 us
    dot_general x18, matrix products, cross_block(): jnp.einsum('fsa,fsb->fab', left[:, 0], right[:, 0], preferred_element_typ...  33.5 us
    dot_general x18, matrix products, cross_block(): jnp.einsum('fsa,fsb->fab', left[:, 1], right[:, 1], preferred_element_typ...  33.2 us
    dot_general x18, matrix products, cross_block(): jnp.einsum('fsa,fsb->fab', left[:, 1], right[:, 0], preferred_element_typ...  33.1 us
  transfers between devices with their start and end apart: 9, of which 8 were waited for; matrix products, arithmetic and copies ran while one was open for 18% of the time, Pallas kernels for 0%

commit v1 on v0

v1 whole, which is shorter than its diff:
```python
import jax
import jax.numpy as jnp
from jax import lax
from jax.experimental import pallas as pl
from jax.experimental.pallas import tpu as pltpu
from jax.sharding import PartitionSpec as P

AXES = ("chan", "bin")
F32 = jnp.float32
BF16 = jnp.bfloat16
PLACES = [
    (p, z, y, x, c)
    for p in range(2)
    for z in range(4)
    for y in range(2)
    for x in range(4)
    for c in range(2)
]
MASK_ROWS = 16


def place(p, z, y, x, c):
    return (p * 4 + z) * 16 + (y * 4 + x) * 2 + c


def route(target):
    pairs = []
    for at in PLACES:
        to = target(*at)
        if to is not None:
            pairs.append((place(*at), place(*to)))
    return pairs


def chan_route(shift):
    def target(p, z, y, x, c):
        to = (p * 4 + z + shift) % 8
        return to // 4, to % 4, y, x, c

    return route(target)


DOWN = route(lambda p, z, y, x, c: (p, (z - 1) % 4, y, x, c))
UP = route(lambda p, z, y, x, c: (p, (z + 1) % 4, y, x, c))
CROSS = chan_route(4)
NEXT = chan_route(1)
CORE = route(lambda p, z, y, x, c: (p, z, y, x, 1 - c))
Y_LO = route(lambda p, z, y, x, c: (p, z, 1 - y, x, c))
X_BY = {d: route(lambda p, z, y, x, c, d=d: (p, z, y, (x + d) % 4, c)) for d in (1, 2, 3)}


def send(value, pairs):
    return lax.ppermute(value, AXES, pairs)


def tie(values):
    return lax.optimization_barrier(values)


def part_of(array, index, rows):
    return lax.dynamic_slice_in_dim(array, index * rows, rows, 0)


def sum_stage_a(partial, x, core):
    half = partial.shape[0] // 2
    mine = part_of(partial, core, half) + send(part_of(partial, 1 - core, half), CORE)
    quarter = half // 4
    own = part_of(mine, x, quarter)
    for d in (1, 2, 3):
        own = own + send(part_of(mine, (x + d) % 4, quarter), X_BY[d])
    return own


def sum_stage_b(own, x, core):
    quarter = own.shape[0]
    own = own + send(own, Y_LO)
    behind = [own] + [send(own, X_BY[d]) for d in (1, 2, 3)]
    line = jnp.concatenate(behind[::-1] * 2, axis=0)
    half = lax.dynamic_slice_in_dim(line, (3 - x) * quarter, 4 * quarter, 0)
    other = send(half, CORE)
    return jnp.where(
        core == 0,
        jnp.concatenate([half, other], axis=0),
        jnp.concatenate([other, half], axis=0),
    )


def pair_kernel(inv, x, y, d, u, sx, sy, sd, su, *rest):
    out, res, wx, wy, wd, wu, lx, ld = rest[-8:]
    width = 128
    depth = x.shape[2]

    def whiten(src, scale, dst):
        factor = scale[...].astype(F32)
        for part in range(2):
            dst[part * depth : (part + 1) * depth, :] = (
                src[0, part].astype(F32) * factor
            ).astype(BF16)

    def turn(src, dst):
        re = src[:depth, :].T
        im = src[depth:, :].T
        cols = re.shape[0]
        dst[:cols, :depth] = re
        dst[:cols, depth:] = im
        dst[cols:, :depth] = im
        dst[cols:, depth:] = -re

    whiten(x, sx, wx)
    whiten(d, sd, wd)
    turn(wx, lx)
    turn(wd, ld)
    whiten(y, sy, wy)
    whiten(u, su, wu)

    def cross(left, right, offset, write):
        both = jnp.dot(left[...], right[...], preferred_element_type=F32)
        for row in range(2):
            for col in range(2):
                factor = inv[offset * 4 + row * 2 + col]
                for part in range(2):
                    top = (part * 2 + row) * width
                    tile = both[top : top + width, col * width : (col + 1) * width]
                    write(row, col, part, (tile * factor).astype(BF16))

    def own_writer(offset):
        def write(row, col, part, tile):
            lag = 2 * offset + col - row
            if 0 <= lag <= 8:
                out[row, lag, 0, part] = tile

        return write

    def res_write(row, col, part, tile):
        res[row, col, 0, part] = tile

    cross(ld, wu, 2, res_write)
    cross(lx, wx, 0, own_writer(0))
    cross(lx, wd, 1, own_writer(1))
    cross(lx, wu, 3, own_writer(3))
    cross(lx, wy, 4, own_writer(4))


def pairs_of(chunk, inv, spectra, y, d, u, sx, sy, sd, su, out):
    bins_here, _, segs, chans = spectra.shape
    count = y.shape[0]
    base = chunk * count
    blk = (1, 2, segs, chans)
    scale = pl.BlockSpec((segs, chans), lambda f: (0, 0))
    local = pl.BlockSpec(blk, lambda f: (f, 0, 0, 0))
    in_specs = [
        pl.BlockSpec(memory_space=pltpu.SMEM),
        pl.BlockSpec(blk, lambda f: (base + f, 0, 0, 0)),
        local,
        local,
        local,
        scale,
        scale,
        scale,
        scale,
    ]
    args = [inv, spectra, y, d, u, sx, sy, sd, su]
    aliases = {}
    if out is not None:
        in_specs.append(pl.BlockSpec(memory_space=pl.ANY))
        aliases = {len(args): 0}
        args.append(out)
    return pl.pallas_call(
        pair_kernel,
        grid=(count,),
        in_specs=in_specs,
        out_specs=[
            pl.BlockSpec((2, 9, 1, 2, 128, 128), lambda f: (0, 0, base + f, 0, 0, 0)),
            pl.BlockSpec((2, 2, 1, 2, 128, 128), lambda f: (0, 0, f, 0, 0, 0)),
        ],
        out_shape=[
            jax.ShapeDtypeStruct((2, 9, bins_here, 2, 128, 128), BF16),
            jax.ShapeDtypeStruct((2, 2, count, 2, 128, 128), BF16),
        ],
        scratch_shapes=[pltpu.VMEM((2 * segs, chans), BF16)] * 4
        + [pltpu.VMEM((2 * chans, 2 * segs), BF16)] * 2,
        input_output_aliases=aliases,
        cost_estimate=pl.CostEstimate(
            flops=count * 5 * 2 * 512 * 1024 * 256,
            bytes_accessed=count * 4 * 1024 * 1024,
            transcendentals=0,
        ),
        compiler_params=pltpu.CompilerParams(vmem_limit_bytes=40 * 1024 * 1024),
    )(*args)


def place_kernel(res, old, out):
    out[...] = res[...]


def placed(chunk, res, out):
    count = res.shape[2]
    blk = (1, 1, count, 2, 128, 128)
    return pl.pallas_call(
        place_kernel,
        grid=(2, 2),
        in_specs=[
            pl.BlockSpec(blk, lambda row, col: (row, col, 0, 0, 0, 0)),
            pl.BlockSpec(memory_space=pl.ANY),
        ],
        out_specs=pl.BlockSpec(
            blk, lambda row, col: (row, 4 + col - row, chunk, 0, 0, 0)
        ),
        out_shape=jax.ShapeDtypeStruct(out.shape, out.dtype),
        input_output_aliases={1: 0},
        cost_estimate=pl.CostEstimate(
            flops=0, bytes_accessed=count * 512 * 1024, transcendentals=0
        ),
    )(res, out)


def shards(spectra, valid):
    bins_here = spectra.shape[0]
    segs, chans = spectra.shape[2:]
    bins = bins_here * lax.axis_size("bin")
    z = lax.axis_index("chan") % 4
    at = lax.axis_index("bin")
    core, x = at % 2, (at // 2) % 4
    chunks = 4
    count = bins_here // chunks
    own = [spectra[i * count : (i + 1) * count] for i in range(chunks)]
    Y, D, U, R = {}, {}, {}, {}
    mask = valid.astype(F32)

    def down_up(i):
        D[i] = send(jnp.where(z == 0, Y[i], own[i]), DOWN)
        U[i] = send(jnp.where(z == 3, own[i], Y[i]), UP)

    Y[0] = send(own[0], CROSS)
    wide = spectra.astype(F32)
    partial = jnp.sum(jnp.sqrt(wide[:, 0] ** 2 + wide[:, 1] ** 2), axis=0)
    piece = sum_stage_a(partial, x, core)
    Y[0], own[1], piece = tie((Y[0], own[1], piece))

    Y[1] = send(own[1], CROSS)
    down_up(0)
    amplitude = sum_stage_b(piece, x, core)
    keep = jnp.repeat(mask.T, chans // valid.shape[0], axis=1)
    sx = keep / (amplitude / bins + 1e-06)
    packed = jnp.concatenate(
        [
            sx.astype(BF16),
            valid.astype(BF16).reshape(-1, chans),
            jnp.zeros((MASK_ROWS - valid.size // chans, chans), BF16),
        ],
        axis=0,
    )
    Y[1], D[0], U[0], own[2], packed = tie((Y[1], D[0], U[0], own[2], packed))

    Y[2] = send(own[2], CROSS)
    down_up(1)
    S = {o: send(packed, chan_route(-o)) for o in (1, 3, 4)}
    Y[2], D[1], U[1], own[3], S = tie((Y[2], D[1], U[1], own[3], S))

    masks = {0: mask}
    for o in S:
        rows = S[o][segs : segs + valid.size // chans]
        masks[o] = rows.reshape(valid.shape).astype(F32)
    sides = [(0, 0), (0, 1), (1, 3), (0, 3), (0, 4)]
    left = jnp.stack([masks[a] for a, _ in sides])
    right = jnp.stack([masks[b] for _, b in sides])
    total = jnp.sum(left[:, :, None] * right[:, None], axis=-1)
    inv = (1.0 / jnp.maximum(total, 1.0)).reshape(-1)

    out = None

    def pairs(i):
        nonlocal out
        out, res = pairs_of(i, inv, spectra, Y[i], D[i], U[i], sx, S[4], S[1], S[3], out)
        R[i] = send(res, NEXT)

    Y[3] = send(own[3], CROSS)
    down_up(2)
    pairs(0)
    pairs(1)
    Y[3], D[2], U[2], R[0], R[1], out = tie((Y[3], D[2], U[2], R[0], R[1], out))

    down_up(3)
    pairs(2)
    for i in (0, 1):
        out = placed(i, R[i], out)
    D[3], U[3], R[2], out = tie((D[3], U[3], R[2], out))

    pairs(3)
    for i in (2, 3):
        out = placed(i, R[i], out)
    return out


def solution(mesh):
    return jax.shard_map(
        shards,
        mesh=mesh,
        in_specs=(P("bin", None, None, "chan"), P("chan", None)),
        out_specs=P("chan", None, "bin", None, None, None),
        check_vma=False,
    )
```

time: 641 us -> 225 us (0.35)
  waiting for transfers between devices: 390 us -> 117 us
  matrix products: 134 us -> 0 us
  Pallas kernels: 0 us -> 34.2 us
  between operations: 25.3 us -> 0.38 us
  other arithmetic: 29.7 us -> 16.1 us
    ppermute x8 -> x28, waiting for transfers between devices: 273 us -> 117 us  [send(): return lax.ppermute(value, AXES, pairs)]
    dot_general x72 -> x0, matrix products: 134 us -> none  [the longest x18 33.8 us: cross_block(): jnp.einsum('fsa,fsb->fab', left[:, 0], right[:, 1], preferred_element_typ...]
    psum x1 -> x0, waiting for transfers between devices: 117 us -> none  [shards(): amplitude = lax.psum(partial_value, 'bin')]
    pallas_call x0 -> x8, Pallas kernels: none -> 34.2 us  [the longest x4 21.6 us: pairs_of(): pl.pallas_call(pair_kernel, grid=(count,), in_specs=in_specs, out_specs=[...]
    another operation x1, local copies, waits for them, and re-layouts: 11.7 us -> 0.01 us  [shards(): right = jnp.stack([masks[b] for _, b in sides])]
    select_n x0 -> x4, other arithmetic: none -> 11 us  [down_up(): U[i] = send(jnp.where(z == 3, own[i], Y[i]), UP)]
    unnamed x5 -> x43, local copies, waits for them, and re-layouts: 0.05 us -> 9.66 us
    another operation x3 -> x1, other arithmetic: 9.35 us -> 0.01 us  [shards(): left = jnp.stack([masks[a] for a, _ in sides])]
  transfers between devices with their start and end apart: 9 -> 28, of which waited for: 8 -> 20; matrix products, arithmetic and copies ran while one was open for 18% -> 5% of each run, Pallas kernels for 0% -> 12%
where the time goes in v1:
time: 225 us; the launch traced here: 221 us
  waiting for transfers between devices  117 us (52%)
  starting transfers between devices  39.5 us (18%)
  Pallas kernels  34.2 us (15%)
  other arithmetic  16.1 us (7%)
  local copies, waits for them, and re-layouts  13.4 us (6%)
    ppermute x28, waiting for transfers between devices, send(): return lax.ppermute(value, AXES, pairs)  117 us
    ppermute x28, starting transfers between devices, send(): return lax.ppermute(value, AXES, pairs)  39.5 us
    pallas_call x4, Pallas kernels, pairs_of(): pl.pallas_call(pair_kernel, grid=(count,), in_specs=in_specs, out_specs=[...  21.6 us
    pallas_call x4, Pallas kernels, placed(): pl.pallas_call(place_kernel, grid=(2, 2), in_specs=[pl.BlockSpec(blk, lam...  12.6 us
    select_n x4, other arithmetic, down_up(): U[i] = send(jnp.where(z == 3, own[i], Y[i]), UP)  11 us
    unnamed x43, local copies, waits for them, and re-layouts  9.66 us
  transfers between devices with their start and end apart: 28, of which 20 were waited for; matrix products, arithmetic and copies ran while one was open for 5% of the time, Pallas kernels for 12%

profile of v1, /device:TPU:6, one launch (start us, length us, event | category | flops | bytes accessed | tf_op | source)
XLA Modules:
  0.0 220.8 jit_solution(10815328406982978907)
XLA Ops:
  0.0 2.6 %fusion.6 = (bf16[2,2,512,256]{3,2,1,0:T(8,128)(2,1)}, bf16[2,2,512,256]{3,2,1,0:T(8,128)(2,1)S(1)}) fusion(bf16[8,2,512,256]{3,2,1,0:T(8,128)(2,1)} %x.7), kind=kLoop, calls=%fused_computation.50 | loop fusion | bytes 4194304 | tf_op jit(solution)/shard_map/slice | solution.py:226
  2.6 3.2 %collective-permute-start = (bf16[2,2,512,256]{3,2,1,0:T(8,128)(2,1)S(1)}, bf16[2,2,512,256]{3,2,1,0:T(8,128)(2,1)S(1)}, u32[]{:S(2)}, u32[]{:S(2)}) collective-permute-start(bf16[2,2,512,256]{3,2,1,0:T(8,128)(2,1)S(1)} %get-tuple-element.78), channel_id=1, source_target_pairs={{0,64},{1,65},{2,66},{3,67},{4,68},{5,69},{6,70},{7,71},{8,72},{9,... | collective-permute-start | bytes 3145736 | tf_op jit(solution)/shard_map/ppermute | solution.py:53
  5.8 3.1 %convert_element_type.52 = f32[8,2,512,256]{3,2,1,0:T(8,128)S(1)} convert(bf16[8,2,512,256]{3,2,1,0:T(8,128)(2,1)} %x.7) | non-fusion elementwise | flops 2097152 | bytes 12582912 | tf_op jit(solution)/shard_map/convert_element_type | solution.py:235
  8.9 1.5 fusion.2
  10.7 1.4 collective-permute-done.1
  12.2 0.5 collective-permute-start.2
  12.7 2.4 %collective-permute-start.3 = (f32[64,256]{1,0:T(8,128)S(1)}, f32[64,256]{1,0:T(8,128)S(1)}, u32[]{:S(2)}, u32[]{:S(2)}) collective-permute-start(f32[64,256]{1,0:T(8,128)S(1)} %get-tuple-element.87), channel_id=1, source_target_pairs={{0,4},{1,5},{2,6},{3,7},{4,0},{5,1},{6,2},{7,3},{8,12},{9,13},{10,... | collective-permute-start | bytes 196616 | tf_op jit(solution)/shard_map/ppermute | solution.py:53
  15.2 1.9 collective-permute-done.2
  17.1 1.4 collective-permute-done.3
  18.5 2.1 collective-permute-done.4
  20.7 8.4 %collective-permute-done.y = bf16[2,2,512,256]{3,2,1,0:T(8,128)(2,1)S(1)} collective-permute-done((bf16[2,2,512,256]{3,2,1,0:T(8,128)(2,1)S(1)}, bf16[2,2,512,256]{3,2,1,0:T(8,128)(2,1)S(1)}, u32[]{:S(2)}, u32[]{:S(2)}) %collective-permute-start) | collective-permute-done | bytes 1048608 | tf_op jit(solution)/shard_map/ppermute | solution.py:53
  29.1 1.6 collective-permute-start.8
  30.6 2.7 %collective-permute-done.8 = f32[64,256]{1,0:T(8,128)S(1)} collective-permute-done((f32[64,256]{1,0:T(8,128)S(1)}, f32[64,256]{1,0:T(8,128)S(1)}, u32[]{:S(2)}, u32[]{:S(2)}) %collective-permute-start.8) | collective-permute-done | bytes 65568 | tf_op jit(solution)/shard_map/ppermute | solution.py:53
  33.3 0.9 collective-permute-start.9
  34.2 4.0 %broadcast_select_fusion.3 = (bf16[2,2,512,256]{3,2,1,0:T(8,128)(2,1)}, bf16[2,2,512,256]{3,2,1,0:T(8,128)(2,1)}, bf16[2,2,512,256]{3,2,1,0:T(8,128)(2,1)}, bf16[2,2,512,256]{3,2,1,0:T(8,128)(2,1)}) fusion(bf16[2,2,512,256]{3,2,1,0:T(8,128)(2,1)S(1)} %collective-permute-done.y, pred[]{:T(512)S(6)} %eq.23, bf16[8,2,512,256]{3,2,1,0:T(8,128)(2,1)} %x.7, pred[]{:T(512)S(6)} %eq.22), kind=kLoop, calls=%fused_computation.8 | loop fusion | flops 1048576 | bytes 8388610 | tf_op jit(solution)/shard_map/jit(_where)/select_n | solution.py:232
  38.2 4.0 %collective-permute-start.6 = (bf16[2,2,512,256]{3,2,1,0:T(8,128)(2,1)}, bf16[2,2,512,256]{3,2,1,0:T(8,128)(2,1)S(1)}, u32[]{:S(2)}, u32[]{:S(2)}) collective-permute-start(bf16[2,2,512,256]{3,2,1,0:T(8,128)(2,1)} %get-tuple-element.74), channel_id=1, source_target_pairs={{0,48},{1,49},{2,50},{3,51},{4,52},{5,53},{6,54},{7,55},{8,56},{9,... | collective-permute-start | bytes 3145736 | tf_op jit(solution)/shard_map/ppermute | solution.py:53
  42.3 3.2 %collective-permute-start.5 = (bf16[2,2,512,256]{3,2,1,0:T(8,128)(2,1)}, bf16[2,2,512,256]{3,2,1,0:T(8,128)(2,1)S(1)}, u32[]{:S(2)}, u32[]{:S(2)}) collective-permute-start(bf16[2,2,512,256]{3,2,1,0:T(8,128)(2,1)} %get-tuple-element.38), channel_id=1, source_target_pairs={{0,64},{1,65},{2,66},{3,67},{4,68},{5,69},{6,70},{7,71},{8,72},{9,... | collective-permute-start | bytes 3145736 | tf_op jit(solution)/shard_map/ppermute | solution.py:53
  45.5 1.1 collective-permute-start.10
  46.6 2.1 collective-permute-start.11
  48.7 2.6 %collective-permute-done.10 = f32[64,256]{1,0:T(8,128)S(1)} collective-permute-done((f32[64,256]{1,0:T(8,128)S(1)}, f32[64,256]{1,0:T(8,128)S(1)}, u32[]{:S(2)}, u32[]{:S(2)}) %collective-permute-start.10) | collective-permute-done | bytes 65568 | tf_op jit(solution)/shard_map/ppermute | solution.py:53
  51.3 0.4 collective-permute-done.11
  51.9 0.1 copy.12
  52.2 1.2 collective-permute-done.12
  53.4 0.6 broadcast_in_dim.8
  54.0 0.1 fusion.5
  54.1 0.1 maximum_maximum_fusion
  54.3 8.4 %collective-permute-done.6.d = bf16[2,2,512,256]{3,2,1,0:T(8,128)(2,1)S(1)} collective-permute-done((bf16[2,2,512,256]{3,2,1,0:T(8,128)(2,1)}, bf16[2,2,512,256]{3,2,1,0:T(8,128)(2,1)S(1)}, u32[]{:S(2)}, u32[]{:S(2)}) %collective-permute-start.6) | collective-permute-done | bytes 1048608 | tf_op jit(solution)/shard_map/ppermute | solution.py:53
  62.7 3.4 %collective-permute-done.7.u = bf16[2,2,512,256]{3,2,1,0:T(8,128)(2,1)} collective-permute-done((bf16[2,2,512,256]{3,2,1,0:T(8,128)(2,1)}, bf16[2,2,512,256]{3,2,1,0:T(8,128)(2,1)}, u32[]{:S(2)}, u32[]{:S(2)}) %collective-permute-start.7) | collective-permute-done | bytes 1048608 | tf_op jit(solution)/shard_map/ppermute | solution.py:53
  66.1 0.2 collective-permute-done.5.y
  66.3 1.4 broadcast_select_fusion.2
  67.7 3.0 %collective-permute-start.14 = (bf16[2,2,512,256]{3,2,1,0:T(8,128)(2,1)S(1)}, bf16[2,2,512,256]{3,2,1,0:T(8,128)(2,1)S(1)}, u32[]{:S(2)}, u32[]{:S(2)}) collective-permute-start(bf16[2,2,512,256]{3,2,1,0:T(8,128)(2,1)S(1)} %get-tuple-element.84), channel_id=1, source_target_pairs={{0,48},{1,49},{2,50},{3,51},{4,52},{5,53},{6,54},{7,55},{8,56},{9,... | collective-permute-start | bytes 3145736 | tf_op jit(solution)/shard_map/ppermute | solution.py:53
  70.7 3.2 %collective-permute-start.13 = (bf16[2,2,512,256]{3,2,1,0:T(8,128)(2,1)}, bf16[2,2,512,256]{3,2,1,0:T(8,128)(2,1)S(1)}, u32[]{:S(2)}, u32[]{:S(2)}) collective-permute-start(bf16[2,2,512,256]{3,2,1,0:T(8,128)(2,1)} %get-tuple-element.41), channel_id=1, source_target_pairs={{0,64},{1,65},{2,66},{3,67},{4,68},{5,69},{6,70},{7,71},{8,72},{9,... | collective-permute-start | bytes 3145736 | tf_op jit(solution)/shard_map/ppermute | solution.py:53
  73.9 3.0 %collective-permute-start.16 = (bf16[528,256]{1,0:T(8,128)(2,1)S(1)}, bf16[528,256]{1,0:T(8,128)(2,1)S(1)}, u32[]{:S(2)}, u32[]{:S(2)}) collective-permute-start(bf16[528,256]{1,0:T(8,128)(2,1)S(1)} %maximum_maximum_fusion), channel_id=1, source_target_pairs={{0,112},{1,113},{2,114},{3,115},{4,116},{5,117},{6,118},{7,119},{8... | collective-permute-start | bytes 811016 | tf_op jit(solution)/shard_map/ppermute | solution.py:53
  76.9 26.6 %collective-permute-done.16.sd = bf16[528,256]{1,0:T(8,128)(2,1)S(1)} collective-permute-done((bf16[528,256]{1,0:T(8,128)(2,1)S(1)}, bf16[528,256]{1,0:T(8,128)(2,1)S(1)}, u32[]{:S(2)}, u32[]{:S(2)}) %collective-permute-start.16) | collective-permute-done | bytes 270368 | tf_op jit(solution)/shard_map/ppermute | solution.py:53
  103.5 0.3 collective-permute-start.18
  103.9 3.1 %collective-permute-done.17.su = bf16[528,256]{1,0:T(8,128)(2,1)S(1)} collective-permute-done((bf16[528,256]{1,0:T(8,128)(2,1)S(1)}, bf16[528,256]{1,0:T(8,128)(2,1)S(1)}, u32[]{:S(2)}, u32[]{:S(2)}) %collective-permute-start.17) | collective-permute-done | bytes 270368 | tf_op jit(solution)/shard_map/ppermute | solution.py:53
  107.0 4.5 %collective-permute-done.18.sy = bf16[528,256]{1,0:T(8,128)(2,1)S(1)} collective-permute-done((bf16[528,256]{1,0:T(8,128)(2,1)S(1)}, bf16[528,256]{1,0:T(8,128)(2,1)S(1)}, u32[]{:S(2)}, u32[]{:S(2)}) %collective-permute-start.18) | collective-permute-done | bytes 270368 | tf_op jit(solution)/shard_map/ppermute | solution.py:53
  111.5 1.0 copy-done.4
  112.5 1.0 copy-done.6
  113.5 2.8 %broadcast_select_fusion.1 = (bf16[2,2,512,256]{3,2,1,0:T(8,128)(2,1)}, bf16[2,2,512,256]{3,2,1,0:T(8,128)(2,1)}) fusion(bf16[2,2,512,256]{3,2,1,0:T(8,128)(2,1)} %get-tuple-element.41, bf16[2,2,512,256]{3,2,1,0:T(8,128)(2,1)S(1)} %collective-permute-done.13.y, pred[]{:T(512)S(6)} %eq.23, pred[]{:T(512)S(6)} %eq.22), kind=kLoop, calls=%fused_computation.6 | loop fusion | flops 1048576 | bytes 4194306 | tf_op jit(solution)/shard_map/jit(_where)/select_n | solution.py:232
  116.3 3.5 %collective-permute-start.20 = (bf16[2,2,512,256]{3,2,1,0:T(8,128)(2,1)}, bf16[2,2,512,256]{3,2,1,0:T(8,128)(2,1)}, u32[]{:S(2)}, u32[]{:S(2)}) collective-permute-start(bf16[2,2,512,256]{3,2,1,0:T(8,128)(2,1)} %get-tuple-element.82), channel_id=1, source_target_pairs={{0,48},{1,49},{2,50},{3,51},{4,52},{5,53},{6,54},{7,55},{8,56},{9,... | collective-permute-start | bytes 3145736 | tf_op jit(solution)/shard_map/ppermute | solution.py:53
  119.8 3.2 %collective-permute-start.19 = (bf16[2,2,512,256]{3,2,1,0:T(8,128)(2,1)}, bf16[2,2,512,256]{3,2,1,0:T(8,128)(2,1)}, u32[]{:S(2)}, u32[]{:S(2)}) collective-permute-start(bf16[2,2,512,256]{3,2,1,0:T(8,128)(2,1)} %get-tuple-element.47), channel_id=1, source_target_pairs={{0,64},{1,65},{2,66},{3,67},{4,68},{5,69},{6,70},{7,71},{8,72},{9,... | collective-permute-start | bytes 3145736 | tf_op jit(solution)/shard_map/ppermute | solution.py:53
  123.2 2.2 copy-done
  125.4 1.2 copy-done.3
  126.6 1.2 copy-done.9
  127.8 5.5 %shard_map.28 = (bf16[2,9,8,2,128,128]{5,4,3,2,1,0:T(8,128)(2,1)}, bf16[2,2,2,2,128,128]{5,4,3,2,1,0:T(8,128)(2,1)S(1)}) custom-call(f32[20]{0:T(128)S(1)} %div.31.inv, bf16[8,2,512,256]{3,2,1,0:T(8,128)(2,1)S(1)} %copy-done, bf16[2,2,512,256]{3,2,1,0:T(8,128)(2,1)S(1)} %copy-done.3, bf16[2,2,512,256]{3,2,1,0:T(8,128)(2,1)S(1)} %copy-done.9, ...), custom_call_target="tpu_custom_call" | custom-call | flops 2684354560 | bytes 8388608 | tf_op jit(solution)/shard_map/pallas_call | solution.py:168
  133.4 4.9 %shard_map.29 = (bf16[2,9,8,2,128,128]{5,4,3,2,1,0:T(8,128)(2,1)}, bf16[2,2,2,2,128,128]{5,4,3,2,1,0:T(8,128)(2,1)S(1)}) custom-call(f32[20]{0:T(128)S(1)} %div.31.inv, bf16[8,2,512,256]{3,2,1,0:T(8,128)(2,1)S(1)} %copy-done, bf16[2,2,512,256]{3,2,1,0:T(8,128)(2,1)S(1)} %collective-permute-done.5.y, ...), custom_call_target="tpu_custom_call", output_to_operand_aliasing={{0}: (9, {})} | custom-call | flops 2684354560 | bytes 8388608 | tf_op jit(solution)/shard_map/pallas_call | solution.py:168
  138.3 1.4 collective-permute-start.22
  139.7 16.4 %collective-permute-done.23.res = bf16[2,2,2,2,128,128]{5,4,3,2,1,0:T(8,128)(2,1)S(1)} collective-permute-done((bf16[2,2,2,2,128,128]{5,4,3,2,1,0:T(8,128)(2,1)S(1)}, bf16[2,2,2,2,128,128]{5,4,3,2,1,0:T(8,128)(2,1)S(1)}, u32[]{:S(2)}, u32[]{:S(2)}) %collective-permute-start.23) | collective-permute-done | bytes 524320 | tf_op jit(solution)/shard_map/ppermute | solution.py:53
  156.1 5.6 %collective-permute-done.22.res = bf16[2,2,2,2,128,128]{5,4,3,2,1,0:T(8,128)(2,1)S(1)} collective-permute-done((bf16[2,2,2,2,128,128]{5,4,3,2,1,0:T(8,128)(2,1)S(1)}, bf16[2,2,2,2,128,128]{5,4,3,2,1,0:T(8,128)(2,1)S(1)}, u32[]{:S(2)}, u32[]{:S(2)}) %collective-permute-start.22) | collective-permute-done | bytes 524320 | tf_op jit(solution)/shard_map/ppermute | solution.py:53
  161.7 2.9 %broadcast_select_fusion = (bf16[2,2,512,256]{3,2,1,0:T(8,128)(2,1)}, bf16[2,2,512,256]{3,2,1,0:T(8,128)(2,1)}) fusion(bf16[2,2,512,256]{3,2,1,0:T(8,128)(2,1)S(1)} %copy-done.10, bf16[2,2,512,256]{3,2,1,0:T(8,128)(2,1)} %collective-permute-done.19.y, pred[]{:T(512)S(6)} %eq.23, pred[]{:T(512)S(6)} %eq.22), kind=kLoop, calls=%fused_computation.5 | loop fusion | flops 1048576 | bytes 4194306 | tf_op jit(solution)/shard_map/jit(_where)/select_n | solution.py:232
  164.6 2.0 collective-permute-start.25
  166.6 5.6 %shard_map.30 = (bf16[2,9,8,2,128,128]{5,4,3,2,1,0:T(8,128)(2,1)}, bf16[2,2,2,2,128,128]{5,4,3,2,1,0:T(8,128)(2,1)}) custom-call(f32[20]{0:T(128)S(1)} %div.31.inv, bf16[8,2,512,256]{3,2,1,0:T(8,128)(2,1)S(1)} %copy-done, bf16[2,2,512,256]{3,2,1,0:T(8,128)(2,1)S(1)} %collective-permute-done.13.y, ...), custom_call_target="tpu_custom_call", output_to_operand_aliasing={{0}: (9, {})} | custom-call | flops 2684354560 | bytes 8388608 | tf_op jit(solution)/shard_map/pallas_call | solution.py:168
  172.3 3.2 %shard_map.31.old = bf16[2,9,8,2,128,128]{5,4,3,2,1,0:T(8,128)(2,1)} custom-call(bf16[2,2,2,2,128,128]{5,4,3,2,1,0:T(8,128)(2,1)} %copy-done.12, bf16[2,9,8,2,128,128]{5,4,3,2,1,0:T(8,128)(2,1)} %get-tuple-element.64.old), custom_call_target="tpu_custom_call", output_to_operand_aliasing={{}: (1, {})} | custom-call | bytes 1048576 | tf_op jit(solution)/shard_map/pallas_call | solution.py:199
  175.4 3.2 %shard_map.32.rest_0_ = bf16[2,9,8,2,128,128]{5,4,3,2,1,0:T(8,128)(2,1)} custom-call(bf16[2,2,2,2,128,128]{5,4,3,2,1,0:T(8,128)(2,1)} %copy-done.11, bf16[2,9,8,2,128,128]{5,4,3,2,1,0:T(8,128)(2,1)} %shard_map.31.old), custom_call_target="tpu_custom_call", output_to_operand_aliasing={{}: (1, {})} | custom-call | bytes 1048576 | tf_op jit(solution)/shard_map/pallas_call | solution.py:199
  178.6 15.7 %collective-permute-done.26.res = bf16[2,2,2,2,128,128]{5,4,3,2,1,0:T(8,128)(2,1)S(1)} collective-permute-done((bf16[2,2,2,2,128,128]{5,4,3,2,1,0:T(8,128)(2,1)}, bf16[2,2,2,2,128,128]{5,4,3,2,1,0:T(8,128)(2,1)S(1)}, u32[]{:S(2)}, u32[]{:S(2)}) %collective-permute-start.26) | collective-permute-done | bytes 524320 | tf_op jit(solution)/shard_map/ppermute | solution.py:53
  194.3 2.0 collective-permute-done.25.u
  196.3 2.2 copy-done.1
  198.5 5.5 %shard_map.33 = (bf16[2,9,8,2,128,128]{5,4,3,2,1,0:T(8,128)(2,1)}, bf16[2,2,2,2,128,128]{5,4,3,2,1,0:T(8,128)(2,1)S(1)}) custom-call(f32[20]{0:T(128)S(1)} %div.31.inv, bf16[8,2,512,256]{3,2,1,0:T(8,128)(2,1)S(1)} %copy-done.1, bf16[2,2,512,256]{3,2,1,0:T(8,128)(2,1)} %collective-permute-done.19.y, ...), custom_call_target="tpu_custom_call", output_to_operand_aliasing={{0}: (9, {})} | custom-call | flops 2684354560 | bytes 8388608 | tf_op jit(solution)/shard_map/pallas_call | solution.py:168
  204.0 0.6 collective-permute-start.27
  204.6 3.2 %shard_map.34.old = bf16[2,9,8,2,128,128]{5,4,3,2,1,0:T(8,128)(2,1)} custom-call(bf16[2,2,2,2,128,128]{5,4,3,2,1,0:T(8,128)(2,1)} %copy-done.13, bf16[2,9,8,2,128,128]{5,4,3,2,1,0:T(8,128)(2,1)} %get-tuple-element.70.old), custom_call_target="tpu_custom_call", output_to_operand_aliasing={{}: (1, {})} | custom-call | bytes 1048576 | tf_op jit(solution)/shard_map/pallas_call | solution.py:199
  207.8 9.1 %collective-permute-done.27.res = bf16[2,2,2,2,128,128]{5,4,3,2,1,0:T(8,128)(2,1)S(1)} collective-permute-done((bf16[2,2,2,2,128,128]{5,4,3,2,1,0:T(8,128)(2,1)S(1)}, bf16[2,2,2,2,128,128]{5,4,3,2,1,0:T(8,128)(2,1)S(1)}, u32[]{:S(2)}, u32[]{:S(2)}) %collective-permute-start.27) | collective-permute-done | bytes 524320 | tf_op jit(solution)/shard_map/ppermute | solution.py:53
  216.8 0.8 copy-done.14
  217.6 3.2 %shard_map.35 = bf16[2,9,8,2,128,128]{5,4,3,2,1,0:T(8,128)(2,1)} custom-call(bf16[2,2,2,2,128,128]{5,4,3,2,1,0:T(8,128)(2,1)} %copy-done.14, bf16[2,9,8,2,128,128]{5,4,3,2,1,0:T(8,128)(2,1)} %shard_map.34.old), custom_call_target="tpu_custom_call", output_to_operand_aliasing={{}: (1, {})} | custom-call | bytes 1048576 | tf_op jit(solution)/shard_map/pallas_call | solution.py:199
  (78 shorter events, 0.9 us)
Async XLA Ops:
  2.6 26.4 %collective-permute-start = (bf16[2,2,512,256]{3,2,1,0:T(8,128)(2,1)S(1)}, bf16[2,2,512,256]{3,2,1,0:T(8,128)(2,1)S(1)}, u32[]{:S(2)}, u32[]{:S(2)}) collective-permute-start(bf16[2,2,512,256]{3,2,1,0:T(8,128)(2,1)S(1)} %get-tuple-element.78), channel_id=1, source_target_pairs={{0,64},{1,65},{2,66},{3,67},{4,68},{5,69},{6,70},{7,71},{8,72},{9,... | collective-permute-start | bytes 3145736 | tf_op jit(solution)/shard_map/ppermute | solution.py:53
  10.5 41.4 %copy-start.15 = (s32[2,512]{1,0:T(2,128)S(1)}, s32[2,512]{1,0:T(2,128)}, u32[]{:S(2)}) copy-start(s32[2,512]{1,0:T(2,128)} %param.3) | copy-start | bytes 12292
  10.5 1.6 collective-permute-start.1
  12.2 4.9 %collective-permute-start.2 = (f32[64,256]{1,0:T(8,128)S(1)}, f32[64,256]{1,0:T(8,128)S(1)}, u32[]{:S(2)}, u32[]{:S(2)}) collective-permute-start(f32[64,256]{1,0:T(8,128)S(1)} %get-tuple-element.85), channel_id=1, source_target_pairs={{0,2},{1,3},{2,4},{3,5},{4,6},{5,7},{6,0},{7,1},{8,10},{9,11},{10,... | collective-permute-start | bytes 196616 | tf_op jit(solution)/shard_map/ppermute | solution.py:53
  12.7 5.8 %collective-permute-start.3 = (f32[64,256]{1,0:T(8,128)S(1)}, f32[64,256]{1,0:T(8,128)S(1)}, u32[]{:S(2)}, u32[]{:S(2)}) collective-permute-start(f32[64,256]{1,0:T(8,128)S(1)} %get-tuple-element.87), channel_id=1, source_target_pairs={{0,4},{1,5},{2,6},{3,7},{4,0},{5,1},{6,2},{7,3},{8,12},{9,13},{10,... | collective-permute-start | bytes 196616 | tf_op jit(solution)/shard_map/ppermute | solution.py:53
  15.2 5.5 %collective-permute-start.4 = (f32[64,256]{1,0:T(8,128)S(1)}, f32[64,256]{1,0:T(8,128)S(1)}, u32[]{:S(2)}, u32[]{:S(2)}) collective-permute-start(f32[64,256]{1,0:T(8,128)S(1)} %get-tuple-element.86), channel_id=1, source_target_pairs={{0,6},{1,7},{2,0},{3,1},{4,2},{5,3},{6,4},{7,5},{8,14},{9,15},{10,... | collective-permute-start | bytes 196616 | tf_op jit(solution)/shard_map/ppermute | solution.py:53
  29.0 13.2 %copy-start.2 = (bf16[2,2,512,256]{3,2,1,0:T(8,128)(2,1)}, bf16[2,2,512,256]{3,2,1,0:T(8,128)(2,1)S(1)}, u32[]{:S(2)}) copy-start(bf16[2,2,512,256]{3,2,1,0:T(8,128)(2,1)S(1)} %collective-permute-done.y) | copy-start | bytes 3145732
  29.1 4.3 %collective-permute-start.8 = (f32[64,256]{1,0:T(8,128)S(1)}, f32[64,256]{1,0:T(8,128)S(1)}, u32[]{:S(2)}, u32[]{:S(2)}) collective-permute-start(f32[64,256]{1,0:T(8,128)S(1)} %add_add_fusion), channel_id=1, source_target_pairs={{0,8},{1,9},{2,10},{3,11},{4,12},{5,13},{6,14},{7,15},{8,0},{9,1},... | collective-permute-start | bytes 196616 | tf_op jit(solution)/shard_map/ppermute | solution.py:53
  33.3 13.3 %collective-permute-start.9 = (f32[64,256]{1,0:T(8,128)S(1)}, f32[64,256]{1,0:T(8,128)S(1)}, u32[]{:S(2)}, u32[]{:S(2)}) collective-permute-start(f32[64,256]{1,0:T(8,128)S(1)} %add.95), channel_id=1, source_target_pairs={{0,6},{1,7},{2,0},{3,1},{4,2},{5,3},{6,4},{7,5},{8,14},{9,15},{10,... | collective-permute-start | bytes 196616 | tf_op jit(solution)/shard_map/ppermute | solution.py:53
  38.2 24.5 %collective-permute-start.6 = (bf16[2,2,512,256]{3,2,1,0:T(8,128)(2,1)}, bf16[2,2,512,256]{3,2,1,0:T(8,128)(2,1)S(1)}, u32[]{:S(2)}, u32[]{:S(2)}) collective-permute-start(bf16[2,2,512,256]{3,2,1,0:T(8,128)(2,1)} %get-tuple-element.74), channel_id=1, source_target_pairs={{0,48},{1,49},{2,50},{3,51},{4,52},{5,53},{6,54},{7,55},{8,56},{9,... | collective-permute-start | bytes 3145736 | tf_op jit(solution)/shard_map/ppermute | solution.py:53
  42.3 23.8 %collective-permute-start.7 = (bf16[2,2,512,256]{3,2,1,0:T(8,128)(2,1)}, bf16[2,2,512,256]{3,2,1,0:T(8,128)(2,1)}, u32[]{:S(2)}, u32[]{:S(2)}) collective-permute-start(bf16[2,2,512,256]{3,2,1,0:T(8,128)(2,1)} %get-tuple-element.73), channel_id=1, source_target_pairs={{0,16},{1,17},{2,18},{3,19},{4,20},{5,21},{6,22},{7,23},{8,24},{9,... | collective-permute-start | bytes 3145736 | tf_op jit(solution)/shard_map/ppermute | solution.py:53
  42.3 24.0 %collective-permute-start.5 = (bf16[2,2,512,256]{3,2,1,0:T(8,128)(2,1)}, bf16[2,2,512,256]{3,2,1,0:T(8,128)(2,1)S(1)}, u32[]{:S(2)}, u32[]{:S(2)}) collective-permute-start(bf16[2,2,512,256]{3,2,1,0:T(8,128)(2,1)} %get-tuple-element.38), channel_id=1, source_target_pairs={{0,64},{1,65},{2,66},{3,67},{4,68},{5,69},{6,70},{7,71},{8,72},{9,... | collective-permute-start | bytes 3145736 | tf_op jit(solution)/shard_map/ppermute | solution.py:53
  45.5 5.8 %collective-permute-start.10 = (f32[64,256]{1,0:T(8,128)S(1)}, f32[64,256]{1,0:T(8,128)S(1)}, u32[]{:S(2)}, u32[]{:S(2)}) collective-permute-start(f32[64,256]{1,0:T(8,128)S(1)} %add.95), channel_id=1, source_target_pairs={{0,4},{1,5},{2,6},{3,7},{4,0},{5,1},{6,2},{7,3},{8,12},{9,13},{10,... | collective-permute-start | bytes 196616 | tf_op jit(solution)/shard_map/ppermute | solution.py:53
  46.6 5.1 %collective-permute-start.11 = (f32[64,256]{1,0:T(8,128)S(1)}, f32[64,256]{1,0:T(8,128)S(1)}, u32[]{:S(2)}, u32[]{:S(2)}) collective-permute-start(f32[64,256]{1,0:T(8,128)S(1)} %add.95), channel_id=1, source_target_pairs={{0,2},{1,3},{2,4},{3,5},{4,6},{5,7},{6,0},{7,1},{8,10},{9,11},{10,... | collective-permute-start | bytes 196616 | tf_op jit(solution)/shard_map/ppermute | solution.py:53
  51.8 1.6 collective-permute-start.12
  62.7 8.0 %copy-start.8 = (bf16[2,2,512,256]{3,2,1,0:T(8,128)(2,1)}, bf16[2,2,512,256]{3,2,1,0:T(8,128)(2,1)S(1)}, u32[]{:S(2)}) copy-start(bf16[2,2,512,256]{3,2,1,0:T(8,128)(2,1)S(1)} %collective-permute-done.6.d) | copy-start | bytes 3145732
  67.7 43.8 %collective-permute-start.14 = (bf16[2,2,512,256]{3,2,1,0:T(8,128)(2,1)S(1)}, bf16[2,2,512,256]{3,2,1,0:T(8,128)(2,1)S(1)}, u32[]{:S(2)}, u32[]{:S(2)}) collective-permute-start(bf16[2,2,512,256]{3,2,1,0:T(8,128)(2,1)S(1)} %get-tuple-element.84), channel_id=1, source_target_pairs={{0,48},{1,49},{2,50},{3,51},{4,52},{5,53},{6,54},{7,55},{8,56},{9,... | collective-permute-start | bytes 3145736 | tf_op jit(solution)/shard_map/ppermute | solution.py:53
  70.7 41.7 %collective-permute-start.15 = (bf16[2,2,512,256]{3,2,1,0:T(8,128)(2,1)S(1)}, bf16[2,2,512,256]{3,2,1,0:T(8,128)(2,1)S(1)}, u32[]{:S(2)}, u32[]{:S(2)}) collective-permute-start(bf16[2,2,512,256]{3,2,1,0:T(8,128)(2,1)S(1)} %get-tuple-element.83), channel_id=1, source_target_pairs={{0,16},{1,17},{2,18},{3,19},{4,20},{5,21},{6,22},{7,23},{8,24},{9,... | collective-permute-start | bytes 3145736 | tf_op jit(solution)/shard_map/ppermute | solution.py:53
  70.7 42.7 %collective-permute-start.13 = (bf16[2,2,512,256]{3,2,1,0:T(8,128)(2,1)}, bf16[2,2,512,256]{3,2,1,0:T(8,128)(2,1)S(1)}, u32[]{:S(2)}, u32[]{:S(2)}) collective-permute-start(bf16[2,2,512,256]{3,2,1,0:T(8,128)(2,1)} %get-tuple-element.41), channel_id=1, source_target_pairs={{0,64},{1,65},{2,66},{3,67},{4,68},{5,69},{6,70},{7,71},{8,72},{9,... | collective-permute-start | bytes 3145736 | tf_op jit(solution)/shard_map/ppermute | solution.py:53
  73.9 29.6 %collective-permute-start.16 = (bf16[528,256]{1,0:T(8,128)(2,1)S(1)}, bf16[528,256]{1,0:T(8,128)(2,1)S(1)}, u32[]{:S(2)}, u32[]{:S(2)}) collective-permute-start(bf16[528,256]{1,0:T(8,128)(2,1)S(1)} %maximum_maximum_fusion), channel_id=1, source_target_pairs={{0,112},{1,113},{2,114},{3,115},{4,116},{5,117},{6,118},{7,119},{8... | collective-permute-start | bytes 811016 | tf_op jit(solution)/shard_map/ppermute | solution.py:53
  76.9 30.0 %collective-permute-start.17 = (bf16[528,256]{1,0:T(8,128)(2,1)S(1)}, bf16[528,256]{1,0:T(8,128)(2,1)S(1)}, u32[]{:S(2)}, u32[]{:S(2)}) collective-permute-start(bf16[528,256]{1,0:T(8,128)(2,1)S(1)} %maximum_maximum_fusion), channel_id=1, source_target_pairs={{0,80},{1,81},{2,82},{3,83},{4,84},{5,85},{6,86},{7,87},{8,88},{9,... | collective-permute-start | bytes 811016 | tf_op jit(solution)/shard_map/ppermute | solution.py:53
  103.5 8.0 %collective-permute-start.18 = (bf16[528,256]{1,0:T(8,128)(2,1)S(1)}, bf16[528,256]{1,0:T(8,128)(2,1)S(1)}, u32[]{:S(2)}, u32[]{:S(2)}) collective-permute-start(bf16[528,256]{1,0:T(8,128)(2,1)S(1)} %maximum_maximum_fusion), channel_id=1, source_target_pairs={{0,64},{1,65},{2,66},{3,67},{4,68},{5,69},{6,70},{7,71},{8,72},{9,... | collective-permute-start | bytes 811016 | tf_op jit(solution)/shard_map/ppermute | solution.py:53
  111.5 1.0 copy-start.4
  112.5 1.0 copy-start.6
  116.3 45.4 %collective-permute-start.20 = (bf16[2,2,512,256]{3,2,1,0:T(8,128)(2,1)}, bf16[2,2,512,256]{3,2,1,0:T(8,128)(2,1)}, u32[]{:S(2)}, u32[]{:S(2)}) collective-permute-start(bf16[2,2,512,256]{3,2,1,0:T(8,128)(2,1)} %get-tuple-element.82), channel_id=1, source_target_pairs={{0,48},{1,49},{2,50},{3,51},{4,52},{5,53},{6,54},{7,55},{8,56},{9,... | collective-permute-start | bytes 3145736 | tf_op jit(solution)/shard_map/ppermute | solution.py:53
  119.8 41.9 %collective-permute-start.21 = (bf16[2,2,512,256]{3,2,1,0:T(8,128)(2,1)}, bf16[2,2,512,256]{3,2,1,0:T(8,128)(2,1)}, u32[]{:S(2)}, u32[]{:S(2)}) collective-permute-start(bf16[2,2,512,256]{3,2,1,0:T(8,128)(2,1)} %get-tuple-element.81), channel_id=1, source_target_pairs={{0,16},{1,17},{2,18},{3,19},{4,20},{5,21},{6,22},{7,23},{8,24},{9,... | collective-permute-start | bytes 3145736 | tf_op jit(solution)/shard_map/ppermute | solution.py:53
  119.8 41.9 %collective-permute-start.19 = (bf16[2,2,512,256]{3,2,1,0:T(8,128)(2,1)}, bf16[2,2,512,256]{3,2,1,0:T(8,128)(2,1)}, u32[]{:S(2)}, u32[]{:S(2)}) collective-permute-start(bf16[2,2,512,256]{3,2,1,0:T(8,128)(2,1)} %get-tuple-element.47), channel_id=1, source_target_pairs={{0,64},{1,65},{2,66},{3,67},{4,68},{5,69},{6,70},{7,71},{8,72},{9,... | collective-permute-start | bytes 3145736 | tf_op jit(solution)/shard_map/ppermute | solution.py:53
  123.2 2.2 copy-start
  125.4 1.2 copy-start.3
  126.6 1.2 copy-start.9
  127.8 5.5 %copy-start.5 = (bf16[2,2,512,256]{3,2,1,0:T(8,128)(2,1)S(1)}, bf16[2,2,512,256]{3,2,1,0:T(8,128)(2,1)}, u32[]{:S(2)}) copy-start(bf16[2,2,512,256]{3,2,1,0:T(8,128)(2,1)} %copy-done.4) | copy-start | bytes 3145732
  127.8 5.5 %copy-start.7 = (bf16[2,2,512,256]{3,2,1,0:T(8,128)(2,1)S(1)}, bf16[2,2,512,256]{3,2,1,0:T(8,128)(2,1)}, u32[]{:S(2)}) copy-start(bf16[2,2,512,256]{3,2,1,0:T(8,128)(2,1)} %copy-done.6) | copy-start | bytes 3145732
  133.4 28.3 %copy-start.10 = (bf16[2,2,512,256]{3,2,1,0:T(8,128)(2,1)S(1)}, bf16[2,2,512,256]{3,2,1,0:T(8,128)(2,1)}, u32[]{:S(2)}) copy-start(bf16[2,2,512,256]{3,2,1,0:T(8,128)(2,1)} %get-tuple-element.47) | copy-start | bytes 3145732
  138.3 17.8 %collective-permute-start.23 = (bf16[2,2,2,2,128,128]{5,4,3,2,1,0:T(8,128)(2,1)S(1)}, bf16[2,2,2,2,128,128]{5,4,3,2,1,0:T(8,128)(2,1)S(1)}, u32[]{:S(2)}, u32[]{:S(2)}) collective-permute-start(bf16[2,2,2,2,128,128]{5,4,3,2,1,0:T(8,128)(2,1)S(1)} %get-tuple-element.55), channel_id=1, source_target_pairs={{0,16},{1,17},{2,18},{3,19},{4,20},{5,21},{6,22},{7,23},{8,24},{9,... | collective-permute-start | bytes 1572872 | tf_op jit(solution)/shard_map/ppermute | solution.py:53
  138.3 23.4 %collective-permute-start.22 = (bf16[2,2,2,2,128,128]{5,4,3,2,1,0:T(8,128)(2,1)S(1)}, bf16[2,2,2,2,128,128]{5,4,3,2,1,0:T(8,128)(2,1)S(1)}, u32[]{:S(2)}, u32[]{:S(2)}) collective-permute-start(bf16[2,2,2,2,128,128]{5,4,3,2,1,0:T(8,128)(2,1)S(1)} %get-tuple-element.51), channel_id=1, source_target_pairs={{0,16},{1,17},{2,18},{3,19},{4,20},{5,21},{6,22},{7,23},{8,24},{9,... | collective-permute-start | bytes 1572872 | tf_op jit(solution)/shard_map/ppermute | solution.py:53
  156.1 8.6 %copy-start.11 = (bf16[2,2,2,2,128,128]{5,4,3,2,1,0:T(8,128)(2,1)}, bf16[2,2,2,2,128,128]{5,4,3,2,1,0:T(8,128)(2,1)S(1)}, u32[]{:S(2)}) copy-start(bf16[2,2,2,2,128,128]{5,4,3,2,1,0:T(8,128)(2,1)S(1)} %collective-permute-done.23.res) | copy-start | bytes 1572868
  161.7 2.9 %copy-start.12 = (bf16[2,2,2,2,128,128]{5,4,3,2,1,0:T(8,128)(2,1)}, bf16[2,2,2,2,128,128]{5,4,3,2,1,0:T(8,128)(2,1)S(1)}, u32[]{:S(2)}) copy-start(bf16[2,2,2,2,128,128]{5,4,3,2,1,0:T(8,128)(2,1)S(1)} %collective-permute-done.22.res) | copy-start | bytes 1572868
  164.6 29.7 %collective-permute-start.24 = (bf16[2,2,512,256]{3,2,1,0:T(8,128)(2,1)}, bf16[2,2,512,256]{3,2,1,0:T(8,128)(2,1)S(1)}, u32[]{:S(2)}, u32[]{:S(2)}) collective-permute-start(bf16[2,2,512,256]{3,2,1,0:T(8,128)(2,1)} %get-tuple-element.80), channel_id=1, source_target_pairs={{0,48},{1,49},{2,50},{3,51},{4,52},{5,53},{6,54},{7,55},{8,56},{9,... | collective-permute-start | bytes 3145736 | tf_op jit(solution)/shard_map/ppermute | solution.py:53
  164.6 31.7 %collective-permute-start.25 = (bf16[2,2,512,256]{3,2,1,0:T(8,128)(2,1)}, bf16[2,2,512,256]{3,2,1,0:T(8,128)(2,1)}, u32[]{:S(2)}, u32[]{:S(2)}) collective-permute-start(bf16[2,2,512,256]{3,2,1,0:T(8,128)(2,1)} %get-tuple-element.79), channel_id=1, source_target_pairs={{0,16},{1,17},{2,18},{3,19},{4,20},{5,21},{6,22},{7,23},{8,24},{9,... | collective-permute-start | bytes 3145736 | tf_op jit(solution)/shard_map/ppermute | solution.py:53
  172.3 22.0 %collective-permute-start.26 = (bf16[2,2,2,2,128,128]{5,4,3,2,1,0:T(8,128)(2,1)}, bf16[2,2,2,2,128,128]{5,4,3,2,1,0:T(8,128)(2,1)S(1)}, u32[]{:S(2)}, u32[]{:S(2)}) collective-permute-start(bf16[2,2,2,2,128,128]{5,4,3,2,1,0:T(8,128)(2,1)} %get-tuple-element.61), channel_id=1, source_target_pairs={{0,16},{1,17},{2,18},{3,19},{4,20},{5,21},{6,22},{7,23},{8,24},{9,... | collective-permute-start | bytes 1572872 | tf_op jit(solution)/shard_map/ppermute | solution.py:53
  194.3 9.8 %copy-start.13 = (bf16[2,2,2,2,128,128]{5,4,3,2,1,0:T(8,128)(2,1)}, bf16[2,2,2,2,128,128]{5,4,3,2,1,0:T(8,128)(2,1)S(1)}, u32[]{:S(2)}) copy-start(bf16[2,2,2,2,128,128]{5,4,3,2,1,0:T(8,128)(2,1)S(1)} %collective-permute-done.26.res) | copy-start | bytes 1572868
  196.3 2.2 copy-start.1
  204.0 12.8 %collective-permute-start.27 = (bf16[2,2,2,2,128,128]{5,4,3,2,1,0:T(8,128)(2,1)S(1)}, bf16[2,2,2,2,128,128]{5,4,3,2,1,0:T(8,128)(2,1)S(1)}, u32[]{:S(2)}, u32[]{:S(2)}) collective-permute-start(bf16[2,2,2,2,128,128]{5,4,3,2,1,0:T(8,128)(2,1)S(1)} %get-tuple-element.68), channel_id=1, source_target_pairs={{0,16},{1,17},{2,18},{3,19},{4,20},{5,21},{6,22},{7,23},{8,24},{9,... | collective-permute-start | bytes 1572872 | tf_op jit(solution)/shard_map/ppermute | solution.py:53
  216.8 0.8 copy-start.14

commit v2 on v1

v2 whole, which is shorter than its diff:
```python
import functools

import jax
import jax.numpy as jnp
from jax import lax
from jax.experimental import pallas as pl
from jax.experimental.pallas import tpu as pltpu
from jax.sharding import PartitionSpec as P

AXES = ("chan", "bin")
F32 = jnp.float32
BF16 = jnp.bfloat16
PLACES = [
    (p, z, y, x, c)
    for p in range(2)
    for z in range(4)
    for y in range(2)
    for x in range(4)
    for c in range(2)
]
VMEM = 40 * 1024 * 1024


def place(p, z, y, x, c):
    return (p * 4 + z) * 16 + (y * 4 + x) * 2 + c


def route(target):
    pairs = []
    for at in PLACES:
        to = target(*at)
        if to is not None:
            pairs.append((place(*at), place(*to)))
    return pairs


def chan_route(shift):
    def target(p, z, y, x, c):
        to = (p * 4 + z + shift) % 8
        return to // 4, to % 4, y, x, c

    return route(target)


DOWN = route(lambda p, z, y, x, c: (p, (z - 1) % 4, y, x, c))
UP = route(lambda p, z, y, x, c: (p, (z + 1) % 4, y, x, c))
CROSS = chan_route(4)
NEXT = chan_route(1)
CORE = route(lambda p, z, y, x, c: (p, z, y, x, 1 - c))
Y_LO = route(lambda p, z, y, x, c: (p, z, 1 - y, x, c))
X_BY = {d: route(lambda p, z, y, x, c, d=d: (p, z, y, (x + d) % 4, c)) for d in (1, 2, 3)}


def send(value, pairs):
    return lax.ppermute(value, AXES, pairs)


def tie(values):
    return lax.optimization_barrier(values)


def part_of(array, index, rows):
    return lax.dynamic_slice_in_dim(array, index * rows, rows, 0)


def sum_pieces(partial, x, core):
    half = partial.shape[0] // 2
    mine = part_of(partial, core, half) + send(part_of(partial, 1 - core, half), CORE)
    quarter = half // 4
    own = part_of(mine, x, quarter)
    for d in (1, 2, 3):
        own = own + send(part_of(mine, (x + d) % 4, quarter), X_BY[d])
    return own


def gather_x(own, x):
    quarter = own.shape[1]
    behind = [own] + [send(own, X_BY[d]) for d in (1, 2, 3)]
    line = jnp.concatenate(behind[::-1] * 2, axis=1)
    return lax.dynamic_slice_in_dim(line, (3 - x) * quarter, 4 * quarter, 1)


def gather_core(half, core):
    other = send(half, CORE)
    return jnp.where(
        core == 0,
        jnp.concatenate([half, other], axis=1),
        jnp.concatenate([other, half], axis=1),
    )


def whiten(src, factor, dst):
    depth = src.shape[1]
    factor = factor.astype(F32)
    for part in range(2):
        dst[part * depth : (part + 1) * depth, :] = (
            src[part].astype(F32) * factor
        ).astype(BF16)


def turn(src, dst):
    depth, cols = src.shape[0] // 2, src.shape[1]
    re = src[:depth, :].T
    im = src[depth:, :].T
    dst[:cols, :depth] = re
    dst[:cols, depth:] = im
    dst[cols:, :depth] = im
    dst[cols:, depth:] = -re


def cross(left, right, inv, side, write):
    both = jnp.dot(left[...], right[...], preferred_element_type=F32)
    width = both.shape[1] // 2
    for row in range(2):
        for col in range(2):
            factor = inv[side * 4 + row * 2 + col]
            for part in range(2):
                top = (part * 2 + row) * width
                tile = both[top : top + width, col * width : (col + 1) * width]
                write(row, col, part, (tile * factor).astype(BF16))


def pair_kernel(offsets, side, inv, scales, *rest):
    n = len(offsets)
    sources = rest[:n]
    out, res = rest[-n - 4 : -n - 2]
    white = rest[-n - 2 : -2]
    lx, ld = rest[-2:]

    for o, src, dst in zip(offsets, sources, white):
        whiten(src.at[0], scales[(0, 1, None, 2, 3)[o]], dst)
    turn(white[0], lx)
    turn(white[1], ld)

    def res_write(row, col, part, tile):
        res[row, col, 0, part] = tile

    cross(ld, white[-1], inv, side, res_write)
    for o, right in zip(offsets, white):

        def out_write(row, col, part, tile, o=o):
            lag = 2 * o + col - row
            if 0 <= lag <= 8:
                out[row, lag, 0, part] = tile

        cross(lx, right, inv, o, out_write)


def pairs_of(base, offsets, side, inv, scales, spectra, others, out):
    bins_here, _, segs, chans = spectra.shape
    count = others[0].shape[0]
    blk = (1, 2, segs, chans)
    in_specs = [
        pl.BlockSpec(memory_space=pltpu.SMEM),
        pl.BlockSpec(scales.shape, lambda f: (0, 0, 0)),
        pl.BlockSpec(blk, lambda f: (base + f, 0, 0, 0)),
    ] + [pl.BlockSpec(blk, lambda f: (f, 0, 0, 0))] * len(others)
    args = [inv, scales, spectra, *others]
    aliases = {}
    if out is not None:
        in_specs.append(pl.BlockSpec(memory_space=pl.ANY))
        aliases = {len(args): 0}
        args.append(out)
    return pl.pallas_call(
        functools.partial(pair_kernel, offsets, side),
        grid=(count,),
        in_specs=in_specs,
        out_specs=[
            pl.BlockSpec((2, 9, 1, 2, 128, 128), lambda f: (0, 0, base + f, 0, 0, 0)),
            pl.BlockSpec((2, 2, 1, 2, 128, 128), lambda f: (0, 0, f, 0, 0, 0)),
        ],
        out_shape=[
            jax.ShapeDtypeStruct((2, 9, bins_here, 2, 128, 128), BF16),
            jax.ShapeDtypeStruct((2, 2, count, 2, 128, 128), BF16),
        ],
        scratch_shapes=[pltpu.VMEM((2 * segs, chans), BF16)] * (len(others) + 1)
        + [pltpu.VMEM((2 * chans, 2 * segs), BF16)] * 2,
        input_output_aliases=aliases,
        cost_estimate=pl.CostEstimate(
            flops=count * 5 * 2 * 512 * 1024 * 256,
            bytes_accessed=count * 4 * 1024 * 1024,
            transcendentals=0,
        ),
        compiler_params=pltpu.CompilerParams(vmem_limit_bytes=VMEM),
    )(*args)


def place_kernel(res, old, out):
    out[...] = res[...]


def placed(base, offset, res, out):
    count = res.shape[2]
    blk = (1, 1, count, 2, 128, 128)
    return pl.pallas_call(
        place_kernel,
        grid=(2, 2),
        in_specs=[
            pl.BlockSpec(blk, lambda row, col: (row, col, 0, 0, 0, 0)),
            pl.BlockSpec(memory_space=pl.ANY),
        ],
        out_specs=pl.BlockSpec(
            blk, lambda row, col: (row, 2 * offset + col - row, base // count, 0, 0, 0)
        ),
        out_shape=jax.ShapeDtypeStruct(out.shape, out.dtype),
        input_output_aliases={1: 0},
        cost_estimate=pl.CostEstimate(
            flops=0, bytes_accessed=count * 512 * 1024, transcendentals=0
        ),
        compiler_params=pltpu.CompilerParams(vmem_limit_bytes=VMEM),
    )(res, out)


def last_kernel(base, spots, count, inv, scales, x, far, *rest):
    n = len(spots)
    incoming = rest[:n]
    out = rest[n + 1]
    wx, wf, lx, own = rest[n + 2 : n + 6]
    held = rest[n + 6 : 2 * n + 6]
    load_sems, store_sems = rest[2 * n + 6 :]
    step = pl.program_id(0)
    loads = [
        pltpu.make_async_copy(src, dst, load_sems.at[i])
        for i, (src, dst) in enumerate(zip(incoming, held))
    ]

    @pl.when(step == 0)
    def _():
        for copy in loads:
            copy.start()

    whiten(x.at[0], scales[0], wx)
    whiten(far.at[0], scales[1], wf)
    turn(wx, lx)

    def write(row, col, part, tile):
        own[row, col, step, part] = tile

    cross(lx, wf, inv, 2, write)

    @pl.when(step == count - 1)
    def _():
        stores = []
        for copy in loads:
            copy.wait()
        for i, (start, offset, src) in enumerate(
            [(base, 2, own)] + [(*spot, src) for spot, src in zip(spots, held)]
        ):
            for row in range(2):
                for col in range(2):
                    stores.append(
                        pltpu.make_async_copy(
                            src.at[row, col],
                            out.at[row, 2 * offset + col - row, pl.ds(start, count)],
                            store_sems.at[i * 4 + row * 2 + col],
                        )
                    )
        for copy in stores:
            copy.start()
        for copy in stores:
            copy.wait()


def last_of(base, inv, scales, spectra, far, spots, incoming, out):
    segs, chans = spectra.shape[2:]
    count = far.shape[0]
    n = len(spots)
    blk = (1, 2, segs, chans)
    anywhere = pl.BlockSpec(memory_space=pl.ANY)
    res_shape = incoming[0].shape
    return pl.pallas_call(
        functools.partial(last_kernel, base, spots, count),
        grid=(count,),
        in_specs=[
            pl.BlockSpec(memory_space=pltpu.SMEM),
            pl.BlockSpec(scales.shape, lambda f: (0, 0, 0)),
            pl.BlockSpec(blk, lambda f: (base + f, 0, 0, 0)),
            pl.BlockSpec(blk, lambda f: (f, 0, 0, 0)),
        ]
        + [anywhere] * (n + 1),
        out_specs=anywhere,
        out_shape=jax.ShapeDtypeStruct(out.shape, out.dtype),
        scratch_shapes=[pltpu.VMEM((2 * segs, chans), BF16)] * 2
        + [pltpu.VMEM((2 * chans, 2 * segs), BF16)]
        + [pltpu.VMEM(res_shape, BF16)] * (n + 1)
        + [pltpu.SemaphoreType.DMA((n,)), pltpu.SemaphoreType.DMA((4 * (n + 1),))],
        input_output_aliases={4 + n: 0},
        cost_estimate=pl.CostEstimate(
            flops=count * 2 * 512 * 1024 * 256,
            bytes_accessed=count * 4 * 1024 * 1024,
            transcendentals=0,
        ),
        compiler_params=pltpu.CompilerParams(vmem_limit_bytes=VMEM),
    )(inv, scales, spectra, far, *incoming, out)


def shards(spectra, valid):
    bins_here = spectra.shape[0]
    segs, chans = spectra.shape[2:]
    bins = bins_here * lax.axis_size("bin")
    z = lax.axis_index("chan") % 4
    at = lax.axis_index("bin")
    core, x = at % 2, (at // 2) % 4
    chunks = 4
    count = bins_here // chunks
    own = [spectra[i * count : (i + 1) * count] for i in range(chunks)]
    Y, D, U, R = {}, {}, {}, {}

    def for_down(i):
        return jnp.where(z == 0, Y[i], own[i])

    def for_up(i):
        return jnp.where(z == 3, own[i], Y[i])

    own[0], spectra0, valid0 = tie((own[0], spectra, valid))
    Y[0] = send(own[0], CROSS)
    wide = spectra0.astype(F32)
    partial = jnp.sum(jnp.sqrt(wide[:, 0] ** 2 + wide[:, 1] ** 2), axis=0)
    piece = sum_pieces(partial, x, core)
    masks = {o: send(valid0, chan_route(-o)) for o in (1, 2, 3, 4)}
    masks[0] = valid0
    Y[0], own[1], piece, masks = tie((Y[0], own[1], piece, masks))

    below, above = for_down(0), for_up(0)
    below, above, piece, masks = tie((below, above, piece, masks))
    D[0], U[0] = send(below, DOWN), send(above, UP)
    Y[1] = send(own[1], CROSS)
    amplitude = piece + send(piece, Y_LO)
    rows = amplitude.shape[0]
    here = part_of(valid.astype(F32).T, core * 4 + x, rows)
    keep = jnp.repeat(here, chans // valid.shape[0], axis=1)
    scale = (keep / (amplitude / bins + 1e-06)).astype(BF16)
    sides = [(0, 0), (0, 1), (0, 2), (0, 3), (0, 4), (1, 3), (1, 4)]
    left = jnp.stack([masks[a] for a, _ in sides]).astype(F32)
    right = jnp.stack([masks[b] for _, b in sides]).astype(F32)
    total = jnp.sum(left[:, :, None] * right[:, None], axis=-1)
    inv = (1.0 / jnp.maximum(total, 1.0)).reshape(-1)
    Y[1], D[0], U[0], own[2], scale, inv = tie((Y[1], D[0], U[0], own[2], scale, inv))

    below, above = for_down(1), for_up(1)
    below, above, scale = tie((below, above, scale))
    D[1], U[1] = send(below, DOWN), send(above, UP)
    Y[2] = send(own[2], CROSS)
    far = [scale] + [send(scale, chan_route(-o)) for o in (1, 3, 4)]
    Y[2], D[1], U[1], own[3], far = tie((Y[2], D[1], U[1], own[3], far))

    below, above = for_down(2), for_up(2)
    below, above, far = tie((below, above, far))
    D[2], U[2] = send(below, DOWN), send(above, UP)
    Y[3] = send(own[3], CROSS)
    scales = gather_core(gather_x(jnp.stack(far), x), core)
    out = None
    res = {}

    def pairs(i, offsets, side, others):
        nonlocal out
        out, res[i] = pairs_of(
            i * count, offsets, side, inv, scales, spectra, others, out
        )

    Y[3], D[2], U[2], scales, inv = tie((Y[3], D[2], U[2], scales, inv))

    pairs(0, (0, 1, 4, 3), 5, (D[0], Y[0], U[0]))
    R[0] = send(res[0], NEXT)
    D[3] = send(for_down(3), DOWN)
    scale2 = send(scales[1], chan_route(-1))
    pairs(1, (0, 1, 4, 3), 5, (D[1], Y[1], U[1]))
    R[1] = send(res[1], NEXT)
    pairs(2, (0, 1, 4, 3), 5, (D[2], Y[2], U[2]))
    D[3], R[0], R[1], out, res[2], scale2 = tie(
        (D[3], R[0], R[1], out, res[2], scale2)
    )

    far2 = send(D[3], chan_route(-1))
    R[2] = send(res[2], NEXT)
    pairs(3, (0, 1, 4), 6, (D[3], Y[3]))
    R[3] = send(res[3], NEXT)
    for i in (0, 1):
        out = placed(i * count, 2, R[i], out)
    return last_of(
        3 * count,
        inv,
        jnp.stack([scales[0], scale2]),
        spectra,
        far2,
        ((2 * count, 2), (3 * count, 3)),
        (R[2], R[3]),
        out,
    )


def solution(mesh):
    return jax.shard_map(
        shards,
        mesh=mesh,
        in_specs=(P("bin", None, None, "chan"), P("chan", None)),
        out_specs=P("chan", None, "bin", None, None, None),
        check_vma=False,
    )
```

time: 225 us -> 185 us (0.82); the launches traced: 221 us -> 184 us
  waiting for transfers between devices: 117 us -> 84.3 us
  starting transfers between devices: 39.5 us -> 53 us
  Pallas kernels: 34.2 us -> 26 us
  local copies, waits for them, and re-layouts: 13.4 us -> 8.55 us
  other arithmetic: 16.1 us -> 12 us
    ppermute x28 -> x33, waiting for transfers between devices: 117 us -> 84.3 us  [send(): return lax.ppermute(value, AXES, pairs)]
    ppermute x28 -> x33, starting transfers between devices: 39.5 us -> 53 us  [send(): return lax.ppermute(value, AXES, pairs)]
    pallas_call x4 -> x2, Pallas kernels: 12.6 us -> 2.74 us  [placed(): pl.pallas_call(place_kernel, grid=(2, 2), in_specs=[pl.BlockSpec(blk, lam...]
    unnamed x43 -> x39, local copies, waits for them, and re-layouts: 9.66 us -> 3.37 us
    select_n x4 -> x5, other arithmetic: 11 us -> 6.39 us  [the longest x3 4.52 us: for_up(): return jnp.where(z == 3, own[i], Y[i])]
    pallas_call x4 -> x5, Pallas kernels: 21.6 us -> 23.3 us  [the longest x4 20.3 us: pairs_of(): pl.pallas_call(functools.partial(pair_kernel, offsets, side), grid=(count...]
  transfers between devices with their start and end apart: 28 -> 33, of which waited for: 20 -> 17; matrix products, arithmetic and copies ran while one was open for 5% -> 6% of each run, Pallas kernels for 12% -> 12%
where the time goes in v2:
time: 185 us; the launch traced here: 184 us
  waiting for transfers between devices  84.3 us (46%)
  starting transfers between devices  53 us (29%)
  Pallas kernels  26 us (14%)
  other arithmetic  12 us (6%)
  local copies, waits for them, and re-layouts  8.55 us (5%)
    ppermute x33, waiting for transfers between devices, send(): return lax.ppermute(value, AXES, pairs)  84.3 us
    ppermute x33, starting transfers between devices, send(): return lax.ppermute(value, AXES, pairs)  53 us
    pallas_call x4, Pallas kernels, pairs_of(): pl.pallas_call(functools.partial(pair_kernel, offsets, side), grid=(count...  20.3 us
    select_n x3, other arithmetic, for_up(): return jnp.where(z == 3, own[i], Y[i])  4.52 us
    slice x1, local copies, waits for them, and re-layouts, shards(): own = [spectra[i * count:(i + 1) * count] for i in range(chunks)]  3.9 us
  transfers between devices with their start and end apart: 33, of which 17 were waited for; matrix products, arithmetic and copies ran while one was open for 6% of the time, Pallas kernels for 12%

profile of v2, /device:TPU:6, one launch (start us, length us, event | category | flops | bytes accessed | tf_op | source)
XLA Modules:
  0.0 184.3 jit_solution(9811649352875553926)
XLA Ops:
  0.0 3.9 %fusion.6 = (bf16[2,2,512,256]{3,2,1,0:T(8,128)(2,1)}, bf16[2,2,512,256]{3,2,1,0:T(8,128)(2,1)}, bf16[2,2,512,256]{3,2,1,0:T(8,128)(2,1)}, bf16[2,2,512,256]{3,2,1,0:T(8,128)(2,1)S(1)}) fusion(bf16[8,2,512,256]{3,2,1,0:T(8,128)(2,1)} %x.1), kind=kLoop, calls=%fused_computation.52 | loop fusion | bytes 8388608 | tf_op jit(solution)/shard_map/slice | solution.py:306
  3.9 3.2 %collective-permute-start = (bf16[2,2,512,256]{3,2,1,0:T(8,128)(2,1)S(1)}, bf16[2,2,512,256]{3,2,1,0:T(8,128)(2,1)S(1)}, u32[]{:S(2)}, u32[]{:S(2)}) collective-permute-start(bf16[2,2,512,256]{3,2,1,0:T(8,128)(2,1)S(1)} %get-tuple-element.66), channel_id=1, source_target_pairs={{0,64},{1,65},{2,66},{3,67},{4,68},{5,69},{6,70},{7,71},{8,72},{9,... | collective-permute-start | bytes 3145736 | tf_op jit(solution)/shard_map/ppermute | solution.py:55
  7.1 3.1 %convert_element_type.23 = f32[8,2,512,256]{3,2,1,0:T(8,128)S(1)} convert(bf16[8,2,512,256]{3,2,1,0:T(8,128)(2,1)} %x.1) | non-fusion elementwise | flops 2097152 | bytes 12582912 | tf_op jit(solution)/shard_map/convert_element_type | solution.py:317
  10.2 1.5 fusion.2
  11.9 3.9 %collective-permute-start.5 = (s32[2,512]{1,0:T(2,128)S(1)}, s32[2,512]{1,0:T(2,128)S(1)}, u32[]{:S(2)}, u32[]{:S(2)}) collective-permute-start(s32[2,512]{1,0:T(2,128)S(1)} %copy-done.10), channel_id=1, source_target_pairs={{0,112},{1,113},{2,114},{3,115},{4,116},{5,117},{6,118},{7,119},{8... | collective-permute-start | bytes 12296 | tf_op jit(solution)/shard_map/ppermute | solution.py:55
  15.8 0.9 collective-permute-start.4
  16.7 1.1 collective-permute-start.3
  17.8 2.1 %collective-permute-start.2 = (f32[64,256]{1,0:T(8,128)S(1)}, f32[64,256]{1,0:T(8,128)S(1)}, u32[]{:S(2)}, u32[]{:S(2)}) collective-permute-start(f32[64,256]{1,0:T(8,128)S(1)} %get-tuple-element.139), channel_id=1, source_target_pairs={{0,2},{1,3},{2,4},{3,5},{4,6},{5,7},{6,0},{7,1},{8,10},{9,11},{10,... | collective-permute-start | bytes 196616 | tf_op jit(solution)/shard_map/ppermute | solution.py:55
  20.1 2.7 %collective-permute-done.4 = f32[64,256]{1,0:T(8,128)S(1)} collective-permute-done((f32[64,256]{1,0:T(8,128)S(1)}, f32[64,256]{1,0:T(8,128)S(1)}, u32[]{:S(2)}, u32[]{:S(2)}) %collective-permute-start.4) | collective-permute-done | bytes 65568 | tf_op jit(solution)/shard_map/ppermute | solution.py:55
  22.8 1.3 collective-permute-start.6
  24.1 3.6 %collective-permute-start.7 = (s32[2,512]{1,0:T(2,128)S(1)}, s32[2,512]{1,0:T(2,128)S(1)}, u32[]{:S(2)}, u32[]{:S(2)}) collective-permute-start(s32[2,512]{1,0:T(2,128)S(1)} %copy-done.10), channel_id=1, source_target_pairs={{0,80},{1,81},{2,82},{3,83},{4,84},{5,85},{6,86},{7,87},{8,88},{9,... | collective-permute-start | bytes 12296 | tf_op jit(solution)/shard_map/ppermute | solution.py:55
  27.7 0.3 collective-permute-start.8
  28.1 1.7 collective-permute-done.5
  29.8 3.0 %collective-permute-done.8 = s32[2,512]{1,0:T(2,128)S(1)} collective-permute-done((s32[2,512]{1,0:T(2,128)S(1)}, s32[2,512]{1,0:T(2,128)S(1)}, u32[]{:S(2)}, u32[]{:S(2)}) %collective-permute-start.8) | collective-permute-done | bytes 4128 | tf_op jit(solution)/shard_map/ppermute | solution.py:55
  32.8 1.0 collective-permute-start.9
  33.9 1.5 broadcast_select_fusion.2
  35.3 3.9 %collective-permute-start.10 = (bf16[2,2,512,256]{3,2,1,0:T(8,128)(2,1)}, bf16[2,2,512,256]{3,2,1,0:T(8,128)(2,1)S(1)}, u32[]{:S(2)}, u32[]{:S(2)}) collective-permute-start(bf16[2,2,512,256]{3,2,1,0:T(8,128)(2,1)} %get-tuple-element.77), channel_id=1, source_target_pairs={{0,48},{1,49},{2,50},{3,51},{4,52},{5,53},{6,54},{7,55},{8,56},{9,... | collective-permute-start | bytes 3145736 | tf_op jit(solution)/shard_map/ppermute | solution.py:55
  39.3 0.7 collective-permute-start.12
  40.4 17.8 %collective-permute-done.12 = f32[64,256]{1,0:T(8,128)S(1)} collective-permute-done((f32[64,256]{1,0:T(8,128)S(1)}, f32[64,256]{1,0:T(8,128)S(1)}, u32[]{:S(2)}, u32[]{:S(2)}) %collective-permute-start.12) | collective-permute-done | bytes 65568 | tf_op jit(solution)/shard_map/ppermute | solution.py:55
  58.1 0.1 broadcast_in_dim.2
  58.3 2.4 %collective-permute-done.10.rest_1_ = bf16[2,2,512,256]{3,2,1,0:T(8,128)(2,1)S(1)} collective-permute-done((bf16[2,2,512,256]{3,2,1,0:T(8,128)(2,1)}, bf16[2,2,512,256]{3,2,1,0:T(8,128)(2,1)S(1)}, u32[]{:S(2)}, u32[]{:S(2)}) %collective-permute-start.10) | collective-permute-done | bytes 1048608 | tf_op jit(solution)/shard_map/ppermute | solution.py:55
  60.7 3.4 %collective-permute-done.11.rest_3_ = bf16[2,2,512,256]{3,2,1,0:T(8,128)(2,1)} collective-permute-done((bf16[2,2,512,256]{3,2,1,0:T(8,128)(2,1)}, bf16[2,2,512,256]{3,2,1,0:T(8,128)(2,1)}, u32[]{:S(2)}, u32[]{:S(2)}) %collective-permute-start.11) | collective-permute-done | bytes 1048608 | tf_op jit(solution)/shard_map/ppermute | solution.py:55
  64.1 0.5 collective-permute-start.13
  64.6 1.5 broadcast_select_fusion.1
  66.1 0.3 collective-permute-start.14
  66.4 1.8 collective-permute-start.15
  68.2 4.0 %collective-permute-start.16 = (bf16[64,256]{1,0:T(8,128)(2,1)S(1)}, bf16[64,256]{1,0:T(8,128)(2,1)S(1)}, u32[]{:S(2)}, u32[]{:S(2)}) collective-permute-start(bf16[64,256]{1,0:T(8,128)(2,1)S(1)} %fusion.3), channel_id=1, source_target_pairs={{0,112},{1,113},{2,114},{3,115},{4,116},{5,117},{6,118},{7,119},{8... | collective-permute-start | bytes 98312 | tf_op jit(solution)/shard_map/ppermute | solution.py:55
  72.1 0.6 collective-permute-start.17
  72.7 16.4 %collective-permute-done.16 = bf16[64,256]{1,0:T(8,128)(2,1)S(1)} collective-permute-done((bf16[64,256]{1,0:T(8,128)(2,1)S(1)}, bf16[64,256]{1,0:T(8,128)(2,1)S(1)}, u32[]{:S(2)}, u32[]{:S(2)}) %collective-permute-start.16) | collective-permute-done | bytes 32800 | tf_op jit(solution)/shard_map/ppermute | solution.py:55
  89.0 3.0 %collective-permute-start.18 = (bf16[64,256]{1,0:T(8,128)(2,1)S(1)}, bf16[64,256]{1,0:T(8,128)(2,1)S(1)}, u32[]{:S(2)}, u32[]{:S(2)}) collective-permute-start(bf16[64,256]{1,0:T(8,128)(2,1)S(1)} %fusion.3), channel_id=1, source_target_pairs={{0,64},{1,65},{2,66},{3,67},{4,68},{5,69},{6,70},{7,71},{8,72},{9,... | collective-permute-start | bytes 98312 | tf_op jit(solution)/shard_map/ppermute | solution.py:55
  92.0 2.5 %collective-permute-done.18 = bf16[64,256]{1,0:T(8,128)(2,1)S(1)} collective-permute-done((bf16[64,256]{1,0:T(8,128)(2,1)S(1)}, bf16[64,256]{1,0:T(8,128)(2,1)S(1)}, u32[]{:S(2)}, u32[]{:S(2)}) %collective-permute-start.18) | collective-permute-done | bytes 32800 | tf_op jit(solution)/shard_map/ppermute | solution.py:55
  94.5 1.0 copy-done.3
  95.5 1.0 copy-done.5
  96.4 1.5 broadcast_select_fusion
  98.0 0.7 pad_maximum_fusion.1
  98.7 0.8 collective-permute-start.22
  99.5 1.1 collective-permute-start.23
  100.6 2.1 %collective-permute-start.24 = (bf16[4,64,256]{2,1,0:T(8,128)(2,1)}, bf16[4,64,256]{2,1,0:T(8,128)(2,1)S(1)}, u32[]{:S(2)}, u32[]{:S(2)}) collective-permute-start(bf16[4,64,256]{2,1,0:T(8,128)(2,1)} %pad_maximum_fusion.1), channel_id=1, source_target_pairs={{0,2},{1,3},{2,4},{3,5},{4,6},{5,7},{6,0},{7,1},{8,10},{9,11},{10,... | collective-permute-start | bytes 393224 | tf_op jit(solution)/shard_map/ppermute | solution.py:55
  102.7 3.0 %collective-permute-start.19 = (bf16[2,2,512,256]{3,2,1,0:T(8,128)(2,1)}, bf16[2,2,512,256]{3,2,1,0:T(8,128)(2,1)S(1)}, u32[]{:S(2)}, u32[]{:S(2)}) collective-permute-start(bf16[2,2,512,256]{3,2,1,0:T(8,128)(2,1)} %get-tuple-element.91), channel_id=1, source_target_pairs={{0,64},{1,65},{2,66},{3,67},{4,68},{5,69},{6,70},{7,71},{8,72},{9,... | collective-permute-start | bytes 3145736 | tf_op jit(solution)/shard_map/ppermute | solution.py:55
  105.7 0.6 collective-permute-start.20
  106.3 0.2 collective-permute-done.22
  106.5 1.2 collective-permute-start.21
  107.9 0.9 constant_dynamic-slice_fusion
  108.7 2.2 %collective-permute-done.25 = bf16[4,256,256]{2,1,0:T(8,128)(2,1)} collective-permute-done((bf16[4,256,256]{2,1,0:T(8,128)(2,1)}, bf16[4,256,256]{2,1,0:T(8,128)(2,1)}, u32[]{:S(2)}, u32[]{:S(2)}) %collective-permute-start.25) | collective-permute-done | bytes 524320 | tf_op jit(solution)/shard_map/ppermute | solution.py:55
  111.0 1.8 maximum_select_fusion.scales
  112.7 11.2 %collective-permute-done.19.rest_2_ = bf16[2,2,512,256]{3,2,1,0:T(8,128)(2,1)S(1)} collective-permute-done((bf16[2,2,512,256]{3,2,1,0:T(8,128)(2,1)}, bf16[2,2,512,256]{3,2,1,0:T(8,128)(2,1)S(1)}, u32[]{:S(2)}, u32[]{:S(2)}) %collective-permute-start.19) | collective-permute-done | bytes 1048608 | tf_op jit(solution)/shard_map/ppermute | solution.py:55
  124.0 3.0 %collective-permute-done.20.rest_1_ = bf16[2,2,512,256]{3,2,1,0:T(8,128)(2,1)} collective-permute-done((bf16[2,2,512,256]{3,2,1,0:T(8,128)(2,1)}, bf16[2,2,512,256]{3,2,1,0:T(8,128)(2,1)}, u32[]{:S(2)}, u32[]{:S(2)}) %collective-permute-start.20) | collective-permute-done | bytes 1048608 | tf_op jit(solution)/shard_map/ppermute | solution.py:55
  126.9 0.3 collective-permute-done.21.rest_3_
  127.3 2.3 %collective-permute-start.26 = (bf16[2,2,512,256]{3,2,1,0:T(8,128)(2,1)S(1)}, bf16[2,2,512,256]{3,2,1,0:T(8,128)(2,1)S(1)}, u32[]{:S(2)}, u32[]{:S(2)}) collective-permute-start(bf16[2,2,512,256]{3,2,1,0:T(8,128)(2,1)S(1)} %broadcast_select_fusion.3), channel_id=1, source_target_pairs={{0,48},{1,49},{2,50},{3,51},{4,52},{5,53},{6,54},{7,55},{8,56},{9,... | collective-permute-start | bytes 3145736 | tf_op jit(solution)/shard_map/ppermute | solution.py:55
  129.7 1.2 copy-done.8
  130.9 5.4 %shard_map.28 = (bf16[2,9,8,2,128,128]{5,4,3,2,1,0:T(8,128)(2,1)}, bf16[2,2,2,2,128,128]{5,4,3,2,1,0:T(8,128)(2,1)S(1)}) custom-call(f32[28]{0:T(128)S(1)} %div.31.inv, bf16[4,512,256]{2,1,0:T(8,128)(2,1)S(1)} %maximum_select_fusion.scales, bf16[8,2,512,256]{3,2,1,0:T(8,128)(2,1)S(1)} %copy-done, bf16[2,2,512,256]{3,2,1,0:T(8,128)(2,1)S(1)} %copy-done.8, ...), custom_call_target="tpu_custom_call" | custom-call | flops 2684354560 | bytes 8388608 | tf_op jit(solution)/shard_map/pallas_call | solution.py:164
  136.3 4.9 %shard_map.29 = (bf16[2,9,8,2,128,128]{5,4,3,2,1,0:T(8,128)(2,1)}, bf16[2,2,2,2,128,128]{5,4,3,2,1,0:T(8,128)(2,1)S(1)}) custom-call(f32[28]{0:T(128)S(1)} %div.31.inv, bf16[4,512,256]{2,1,0:T(8,128)(2,1)S(1)} %maximum_select_fusion.scales, bf16[8,2,512,256]{3,2,1,0:T(8,128)(2,1)S(1)} %copy-done, ...), custom_call_target="tpu_custom_call", output_to_operand_aliasing={{0}: (6, {})} | custom-call | flops 2684354560 | bytes 8388608 | tf_op jit(solution)/shard_map/pallas_call | solution.py:164
  141.2 0.6 collective-permute-start.28
  141.9 5.1 %collective-permute-start.29 = (bf16[512,256]{1,0:T(8,128)(2,1)S(1)}, bf16[512,256]{1,0:T(8,128)(2,1)S(1)}, u32[]{:S(2)}, u32[]{:S(2)}) collective-permute-start(bf16[512,256]{1,0:T(8,128)(2,1)S(1)} %get-tuple-element.138), channel_id=1, source_target_pairs={{0,112},{1,113},{2,114},{3,115},{4,116},{5,117},{6,118},{7,119},{8... | collective-permute-start | bytes 786440 | tf_op jit(solution)/shard_map/ppermute | solution.py:55
  146.9 5.5 %shard_map.30 = (bf16[2,9,8,2,128,128]{5,4,3,2,1,0:T(8,128)(2,1)}, bf16[2,2,2,2,128,128]{5,4,3,2,1,0:T(8,128)(2,1)S(1)}) custom-call(f32[28]{0:T(128)S(1)} %div.31.inv, bf16[4,512,256]{2,1,0:T(8,128)(2,1)S(1)} %maximum_select_fusion.scales, bf16[8,2,512,256]{3,2,1,0:T(8,128)(2,1)S(1)} %copy-done, ...), custom_call_target="tpu_custom_call", output_to_operand_aliasing={{0}: (6, {})} | custom-call | flops 2684354560 | bytes 8388608 | tf_op jit(solution)/shard_map/pallas_call | solution.py:164
  152.5 2.4 %collective-permute-done.29 = bf16[512,256]{1,0:T(8,128)(2,1)S(1)} collective-permute-done((bf16[512,256]{1,0:T(8,128)(2,1)S(1)}, bf16[512,256]{1,0:T(8,128)(2,1)S(1)}, u32[]{:S(2)}, u32[]{:S(2)}) %collective-permute-start.29) | collective-permute-done | bytes 262176 | tf_op jit(solution)/shard_map/ppermute | solution.py:55
  154.9 2.4 %collective-permute-done.28.res = bf16[2,2,2,2,128,128]{5,4,3,2,1,0:T(8,128)(2,1)S(1)} collective-permute-done((bf16[2,2,2,2,128,128]{5,4,3,2,1,0:T(8,128)(2,1)S(1)}, bf16[2,2,2,2,128,128]{5,4,3,2,1,0:T(8,128)(2,1)S(1)}, u32[]{:S(2)}, u32[]{:S(2)}) %collective-permute-start.28) | collective-permute-done | bytes 524320 | tf_op jit(solution)/shard_map/ppermute | solution.py:55
  157.3 3.9 %collective-permute-start.30 = (bf16[2,2,512,256]{3,2,1,0:T(8,128)(2,1)S(1)}, bf16[2,2,512,256]{3,2,1,0:T(8,128)(2,1)S(1)}, u32[]{:S(2)}, u32[]{:S(2)}) collective-permute-start(bf16[2,2,512,256]{3,2,1,0:T(8,128)(2,1)S(1)} %collective-permute-done.26.rest_1_), channel_id=1, source_target_pairs={{0,112},{1,113},{2,114},{3,115},{4,116},{5,117},{6,118},{7,119},{8... | collective-permute-start | bytes 3145736 | tf_op jit(solution)/shard_map/ppermute | solution.py:55
  161.2 4.5 %shard_map.31 = (bf16[2,9,8,2,128,128]{5,4,3,2,1,0:T(8,128)(2,1)}, bf16[2,2,2,2,128,128]{5,4,3,2,1,0:T(8,128)(2,1)S(1)}) custom-call(f32[28]{0:T(128)S(1)} %div.31.inv, bf16[4,512,256]{2,1,0:T(8,128)(2,1)S(1)} %maximum_select_fusion.scales, bf16[8,2,512,256]{3,2,1,0:T(8,128)(2,1)S(1)} %copy-done, ...), custom_call_target="tpu_custom_call", output_to_operand_aliasing={{0}: (5, {})} | custom-call | flops 2684354560 | bytes 8388608 | tf_op jit(solution)/shard_map/pallas_call | solution.py:164
  165.7 1.4 shard_map.32.old
  167.0 1.4 shard_map.33.rest_2_
  168.5 7.1 %collective-permute-done.31.rest_0_ = bf16[2,2,2,2,128,128]{5,4,3,2,1,0:T(8,128)(2,1)S(1)} collective-permute-done((bf16[2,2,2,2,128,128]{5,4,3,2,1,0:T(8,128)(2,1)S(1)}, bf16[2,2,2,2,128,128]{5,4,3,2,1,0:T(8,128)(2,1)S(1)}, u32[]{:S(2)}, u32[]{:S(2)}) %collective-permute-start.31) | collective-permute-done | bytes 524320 | tf_op jit(solution)/shard_map/ppermute | solution.py:55
  175.5 5.6 %collective-permute-done.32.rest_1_ = bf16[2,2,2,2,128,128]{5,4,3,2,1,0:T(8,128)(2,1)S(1)} collective-permute-done((bf16[2,2,2,2,128,128]{5,4,3,2,1,0:T(8,128)(2,1)S(1)}, bf16[2,2,2,2,128,128]{5,4,3,2,1,0:T(8,128)(2,1)S(1)}, u32[]{:S(2)}, u32[]{:S(2)}) %collective-permute-start.32) | collective-permute-done | bytes 524320 | tf_op jit(solution)/shard_map/ppermute | solution.py:55
  181.2 3.0 %shard_map.34 = bf16[2,9,8,2,128,128]{5,4,3,2,1,0:T(8,128)(2,1)} custom-call(f32[28]{0:T(128)S(1)} %div.31.inv, bf16[2,512,256]{2,1,0:T(8,128)(2,1)S(1)} %pad_maximum_fusion.scales, bf16[8,2,512,256]{3,2,1,0:T(8,128)(2,1)S(1)} %copy-done, bf16[2,2,512,256]{3,2,1,0:T(8,128)(2,1)S(1)} %collective-permute-done.30.far, ...), custom_call_target="tpu_custom_call", output_to_operand_aliasing={{}: (6, {})} | custom-call | flops 536870912 | bytes 8388608 | tf_op jit(solution)/shard_map/pallas_call | solution.py:271
  (77 shorter events, 1.2 us)
Async XLA Ops:
  3.9 28.9 %collective-permute-start = (bf16[2,2,512,256]{3,2,1,0:T(8,128)(2,1)S(1)}, bf16[2,2,512,256]{3,2,1,0:T(8,128)(2,1)S(1)}, u32[]{:S(2)}, u32[]{:S(2)}) collective-permute-start(bf16[2,2,512,256]{3,2,1,0:T(8,128)(2,1)S(1)} %get-tuple-element.66), channel_id=1, source_target_pairs={{0,64},{1,65},{2,66},{3,67},{4,68},{5,69},{6,70},{7,71},{8,72},{9,... | collective-permute-start | bytes 3145736 | tf_op jit(solution)/shard_map/ppermute | solution.py:55
  10.2 1.7 copy-start.10
  11.8 4.0 %collective-permute-start.1 = (f32[256,256]{1,0:T(8,128)S(1)}, f32[256,256]{1,0:T(8,128)S(1)}, u32[]{:S(2)}, u32[]{:S(2)}) collective-permute-start(f32[256,256]{1,0:T(8,128)S(1)} %constant_dynamic-slice_fusion.5), channel_id=1, source_target_pairs={{0,1},{1,0},{2,3},{3,2},{4,5},{5,4},{6,7},{7,6},{8,9},{9,8},{10,11... | collective-permute-start | bytes 786440 | tf_op jit(solution)/shard_map/ppermute | solution.py:55
  11.9 17.9 %collective-permute-start.5 = (s32[2,512]{1,0:T(2,128)S(1)}, s32[2,512]{1,0:T(2,128)S(1)}, u32[]{:S(2)}, u32[]{:S(2)}) collective-permute-start(s32[2,512]{1,0:T(2,128)S(1)} %copy-done.10), channel_id=1, source_target_pairs={{0,112},{1,113},{2,114},{3,115},{4,116},{5,117},{6,118},{7,119},{8... | collective-permute-start | bytes 12296 | tf_op jit(solution)/shard_map/ppermute | solution.py:55
  15.8 6.9 %collective-permute-start.4 = (f32[64,256]{1,0:T(8,128)S(1)}, f32[64,256]{1,0:T(8,128)S(1)}, u32[]{:S(2)}, u32[]{:S(2)}) collective-permute-start(f32[64,256]{1,0:T(8,128)S(1)} %get-tuple-element.140), channel_id=1, source_target_pairs={{0,6},{1,7},{2,0},{3,1},{4,2},{5,3},{6,4},{7,5},{8,14},{9,15},{10,... | collective-permute-start | bytes 196616 | tf_op jit(solution)/shard_map/ppermute | solution.py:55
  16.7 7.3 %collective-permute-start.3 = (f32[64,256]{1,0:T(8,128)S(1)}, f32[64,256]{1,0:T(8,128)S(1)}, u32[]{:S(2)}, u32[]{:S(2)}) collective-permute-start(f32[64,256]{1,0:T(8,128)S(1)} %get-tuple-element.141), channel_id=1, source_target_pairs={{0,4},{1,5},{2,6},{3,7},{4,0},{5,1},{6,2},{7,3},{8,12},{9,13},{10,... | collective-permute-start | bytes 196616 | tf_op jit(solution)/shard_map/ppermute | solution.py:55
  17.8 9.9 %collective-permute-start.2 = (f32[64,256]{1,0:T(8,128)S(1)}, f32[64,256]{1,0:T(8,128)S(1)}, u32[]{:S(2)}, u32[]{:S(2)}) collective-permute-start(f32[64,256]{1,0:T(8,128)S(1)} %get-tuple-element.139), channel_id=1, source_target_pairs={{0,2},{1,3},{2,4},{3,5},{4,6},{5,7},{6,0},{7,1},{8,10},{9,11},{10,... | collective-permute-start | bytes 196616 | tf_op jit(solution)/shard_map/ppermute | solution.py:55
  22.8 7.0 %collective-permute-start.6 = (s32[2,512]{1,0:T(2,128)S(1)}, s32[2,512]{1,0:T(2,128)S(1)}, u32[]{:S(2)}, u32[]{:S(2)}) collective-permute-start(s32[2,512]{1,0:T(2,128)S(1)} %copy-done.10), channel_id=1, source_target_pairs={{0,96},{1,97},{2,98},{3,99},{4,100},{5,101},{6,102},{7,103},{8,104... | collective-permute-start | bytes 12296 | tf_op jit(solution)/shard_map/ppermute | solution.py:55
  24.1 5.8 %collective-permute-start.7 = (s32[2,512]{1,0:T(2,128)S(1)}, s32[2,512]{1,0:T(2,128)S(1)}, u32[]{:S(2)}, u32[]{:S(2)}) collective-permute-start(s32[2,512]{1,0:T(2,128)S(1)} %copy-done.10), channel_id=1, source_target_pairs={{0,80},{1,81},{2,82},{3,83},{4,84},{5,85},{6,86},{7,87},{8,88},{9,... | collective-permute-start | bytes 12296 | tf_op jit(solution)/shard_map/ppermute | solution.py:55
  27.7 5.1 %collective-permute-start.8 = (s32[2,512]{1,0:T(2,128)S(1)}, s32[2,512]{1,0:T(2,128)S(1)}, u32[]{:S(2)}, u32[]{:S(2)}) collective-permute-start(s32[2,512]{1,0:T(2,128)S(1)} %copy-done.10), channel_id=1, source_target_pairs={{0,64},{1,65},{2,66},{3,67},{4,68},{5,69},{6,70},{7,71},{8,72},{9,... | collective-permute-start | bytes 12296 | tf_op jit(solution)/shard_map/ppermute | solution.py:55
  32.8 31.3 %copy-start.1 = (bf16[2,2,512,256]{3,2,1,0:T(8,128)(2,1)}, bf16[2,2,512,256]{3,2,1,0:T(8,128)(2,1)S(1)}, u32[]{:S(2)}) copy-start(bf16[2,2,512,256]{3,2,1,0:T(8,128)(2,1)S(1)} %collective-permute-done.rest_2_) | copy-start | bytes 3145732
  32.8 25.5 %collective-permute-start.9 = (bf16[2,2,512,256]{3,2,1,0:T(8,128)(2,1)}, bf16[2,2,512,256]{3,2,1,0:T(8,128)(2,1)S(1)}, u32[]{:S(2)}, u32[]{:S(2)}) collective-permute-start(bf16[2,2,512,256]{3,2,1,0:T(8,128)(2,1)} %get-tuple-element.69), channel_id=1, source_target_pairs={{0,64},{1,65},{2,66},{3,67},{4,68},{5,69},{6,70},{7,71},{8,72},{9,... | collective-permute-start | bytes 3145736 | tf_op jit(solution)/shard_map/ppermute | solution.py:55
  35.3 25.4 %collective-permute-start.10 = (bf16[2,2,512,256]{3,2,1,0:T(8,128)(2,1)}, bf16[2,2,512,256]{3,2,1,0:T(8,128)(2,1)S(1)}, u32[]{:S(2)}, u32[]{:S(2)}) collective-permute-start(bf16[2,2,512,256]{3,2,1,0:T(8,128)(2,1)} %get-tuple-element.77), channel_id=1, source_target_pairs={{0,48},{1,49},{2,50},{3,51},{4,52},{5,53},{6,54},{7,55},{8,56},{9,... | collective-permute-start | bytes 3145736 | tf_op jit(solution)/shard_map/ppermute | solution.py:55
  39.3 24.8 %collective-permute-start.11 = (bf16[2,2,512,256]{3,2,1,0:T(8,128)(2,1)}, bf16[2,2,512,256]{3,2,1,0:T(8,128)(2,1)}, u32[]{:S(2)}, u32[]{:S(2)}) collective-permute-start(bf16[2,2,512,256]{3,2,1,0:T(8,128)(2,1)} %get-tuple-element.78), channel_id=1, source_target_pairs={{0,16},{1,17},{2,18},{3,19},{4,20},{5,21},{6,22},{7,23},{8,24},{9,... | collective-permute-start | bytes 3145736 | tf_op jit(solution)/shard_map/ppermute | solution.py:55
  39.3 18.9 %collective-permute-start.12 = (f32[64,256]{1,0:T(8,128)S(1)}, f32[64,256]{1,0:T(8,128)S(1)}, u32[]{:S(2)}, u32[]{:S(2)}) collective-permute-start(f32[64,256]{1,0:T(8,128)S(1)} %add_add_fusion), channel_id=1, source_target_pairs={{0,8},{1,9},{2,10},{3,11},{4,12},{5,13},{6,14},{7,15},{8,0},{9,1},... | collective-permute-start | bytes 196616 | tf_op jit(solution)/shard_map/ppermute | solution.py:55
  40.4 56.1 %copy-start.9 = (bf16[2,2,512,256]{3,2,1,0:T(8,128)(2,1)S(1)}, bf16[2,2,512,256]{3,2,1,0:T(8,128)(2,1)}, u32[]{:S(2)}) copy-start(bf16[2,2,512,256]{3,2,1,0:T(8,128)(2,1)} %get-tuple-element.85) | copy-start | bytes 3145732
  60.7 37.3 %copy-start.7 = (bf16[2,2,512,256]{3,2,1,0:T(8,128)(2,1)}, bf16[2,2,512,256]{3,2,1,0:T(8,128)(2,1)S(1)}, u32[]{:S(2)}) copy-start(bf16[2,2,512,256]{3,2,1,0:T(8,128)(2,1)S(1)} %collective-permute-done.10.rest_1_) | copy-start | bytes 3145732
  64.1 30.4 %collective-permute-start.13 = (bf16[2,2,512,256]{3,2,1,0:T(8,128)(2,1)}, bf16[2,2,512,256]{3,2,1,0:T(8,128)(2,1)S(1)}, u32[]{:S(2)}, u32[]{:S(2)}) collective-permute-start(bf16[2,2,512,256]{3,2,1,0:T(8,128)(2,1)} %get-tuple-element.85), channel_id=1, source_target_pairs={{0,64},{1,65},{2,66},{3,67},{4,68},{5,69},{6,70},{7,71},{8,72},{9,... | collective-permute-start | bytes 3145736 | tf_op jit(solution)/shard_map/ppermute | solution.py:55
  66.1 28.4 %collective-permute-start.14 = (bf16[2,2,512,256]{3,2,1,0:T(8,128)(2,1)S(1)}, bf16[2,2,512,256]{3,2,1,0:T(8,128)(2,1)S(1)}, u32[]{:S(2)}, u32[]{:S(2)}) collective-permute-start(bf16[2,2,512,256]{3,2,1,0:T(8,128)(2,1)S(1)} %get-tuple-element.88), channel_id=1, source_target_pairs={{0,48},{1,49},{2,50},{3,51},{4,52},{5,53},{6,54},{7,55},{8,56},{9,... | collective-permute-start | bytes 3145736 | tf_op jit(solution)/shard_map/ppermute | solution.py:55
  66.4 29.1 %collective-permute-start.15 = (bf16[2,2,512,256]{3,2,1,0:T(8,128)(2,1)S(1)}, bf16[2,2,512,256]{3,2,1,0:T(8,128)(2,1)S(1)}, u32[]{:S(2)}, u32[]{:S(2)}) collective-permute-start(bf16[2,2,512,256]{3,2,1,0:T(8,128)(2,1)S(1)} %get-tuple-element.89), channel_id=1, source_target_pairs={{0,16},{1,17},{2,18},{3,19},{4,20},{5,21},{6,22},{7,23},{8,24},{9,... | collective-permute-start | bytes 3145736 | tf_op jit(solution)/shard_map/ppermute | solution.py:55
  68.2 20.9 %collective-permute-start.16 = (bf16[64,256]{1,0:T(8,128)(2,1)S(1)}, bf16[64,256]{1,0:T(8,128)(2,1)S(1)}, u32[]{:S(2)}, u32[]{:S(2)}) collective-permute-start(bf16[64,256]{1,0:T(8,128)(2,1)S(1)} %fusion.3), channel_id=1, source_target_pairs={{0,112},{1,113},{2,114},{3,115},{4,116},{5,117},{6,118},{7,119},{8... | collective-permute-start | bytes 98312 | tf_op jit(solution)/shard_map/ppermute | solution.py:55
  72.1 19.9 %collective-permute-start.17 = (bf16[64,256]{1,0:T(8,128)(2,1)S(1)}, bf16[64,256]{1,0:T(8,128)(2,1)S(1)}, u32[]{:S(2)}, u32[]{:S(2)}) collective-permute-start(bf16[64,256]{1,0:T(8,128)(2,1)S(1)} %fusion.3), channel_id=1, source_target_pairs={{0,80},{1,81},{2,82},{3,83},{4,84},{5,85},{6,86},{7,87},{8,88},{9,... | collective-permute-start | bytes 98312 | tf_op jit(solution)/shard_map/ppermute | solution.py:55
  89.0 5.4 %collective-permute-start.18 = (bf16[64,256]{1,0:T(8,128)(2,1)S(1)}, bf16[64,256]{1,0:T(8,128)(2,1)S(1)}, u32[]{:S(2)}, u32[]{:S(2)}) collective-permute-start(bf16[64,256]{1,0:T(8,128)(2,1)S(1)} %fusion.3), channel_id=1, source_target_pairs={{0,64},{1,65},{2,66},{3,67},{4,68},{5,69},{6,70},{7,71},{8,72},{9,... | collective-permute-start | bytes 98312 | tf_op jit(solution)/shard_map/ppermute | solution.py:55
  94.5 1.0 copy-start.3
  95.4 1.0 copy-start.5
  98.7 7.8 %collective-permute-start.22 = (bf16[4,64,256]{2,1,0:T(8,128)(2,1)}, bf16[4,64,256]{2,1,0:T(8,128)(2,1)S(1)}, u32[]{:S(2)}, u32[]{:S(2)}) collective-permute-start(bf16[4,64,256]{2,1,0:T(8,128)(2,1)} %pad_maximum_fusion.1), channel_id=1, source_target_pairs={{0,6},{1,7},{2,0},{3,1},{4,2},{5,3},{6,4},{7,5},{8,14},{9,15},{10,... | collective-permute-start | bytes 393224 | tf_op jit(solution)/shard_map/ppermute | solution.py:55
  99.5 8.2 %collective-permute-start.23 = (bf16[4,64,256]{2,1,0:T(8,128)(2,1)}, bf16[4,64,256]{2,1,0:T(8,128)(2,1)S(1)}, u32[]{:S(2)}, u32[]{:S(2)}) collective-permute-start(bf16[4,64,256]{2,1,0:T(8,128)(2,1)} %pad_maximum_fusion.1), channel_id=1, source_target_pairs={{0,4},{1,5},{2,6},{3,7},{4,0},{5,1},{6,2},{7,3},{8,12},{9,13},{10,... | collective-permute-start | bytes 393224 | tf_op jit(solution)/shard_map/ppermute | solution.py:55
  100.6 7.1 %collective-permute-start.24 = (bf16[4,64,256]{2,1,0:T(8,128)(2,1)}, bf16[4,64,256]{2,1,0:T(8,128)(2,1)S(1)}, u32[]{:S(2)}, u32[]{:S(2)}) collective-permute-start(bf16[4,64,256]{2,1,0:T(8,128)(2,1)} %pad_maximum_fusion.1), channel_id=1, source_target_pairs={{0,2},{1,3},{2,4},{3,5},{4,6},{5,7},{6,0},{7,1},{8,10},{9,11},{10,... | collective-permute-start | bytes 393224 | tf_op jit(solution)/shard_map/ppermute | solution.py:55
  102.7 21.2 %collective-permute-start.19 = (bf16[2,2,512,256]{3,2,1,0:T(8,128)(2,1)}, bf16[2,2,512,256]{3,2,1,0:T(8,128)(2,1)S(1)}, u32[]{:S(2)}, u32[]{:S(2)}) collective-permute-start(bf16[2,2,512,256]{3,2,1,0:T(8,128)(2,1)} %get-tuple-element.91), channel_id=1, source_target_pairs={{0,64},{1,65},{2,66},{3,67},{4,68},{5,69},{6,70},{7,71},{8,72},{9,... | collective-permute-start | bytes 3145736 | tf_op jit(solution)/shard_map/ppermute | solution.py:55
  105.7 21.3 %collective-permute-start.20 = (bf16[2,2,512,256]{3,2,1,0:T(8,128)(2,1)}, bf16[2,2,512,256]{3,2,1,0:T(8,128)(2,1)}, u32[]{:S(2)}, u32[]{:S(2)}) collective-permute-start(bf16[2,2,512,256]{3,2,1,0:T(8,128)(2,1)} %get-tuple-element.97), channel_id=1, source_target_pairs={{0,48},{1,49},{2,50},{3,51},{4,52},{5,53},{6,54},{7,55},{8,56},{9,... | collective-permute-start | bytes 3145736 | tf_op jit(solution)/shard_map/ppermute | solution.py:55
  106.5 20.7 %collective-permute-start.21 = (bf16[2,2,512,256]{3,2,1,0:T(8,128)(2,1)}, bf16[2,2,512,256]{3,2,1,0:T(8,128)(2,1)}, u32[]{:S(2)}, u32[]{:S(2)}) collective-permute-start(bf16[2,2,512,256]{3,2,1,0:T(8,128)(2,1)} %get-tuple-element.98), channel_id=1, source_target_pairs={{0,16},{1,17},{2,18},{3,19},{4,20},{5,21},{6,22},{7,23},{8,24},{9,... | collective-permute-start | bytes 3145736 | tf_op jit(solution)/shard_map/ppermute | solution.py:55
  108.7 2.3 %collective-permute-start.25 = (bf16[4,256,256]{2,1,0:T(8,128)(2,1)}, bf16[4,256,256]{2,1,0:T(8,128)(2,1)}, u32[]{:S(2)}, u32[]{:S(2)}) collective-permute-start(bf16[4,256,256]{2,1,0:T(8,128)(2,1)} %constant_dynamic-slice_fusion), channel_id=1, source_target_pairs={{0,1},{1,0},{2,3},{3,2},{4,5},{5,4},{6,7},{7,6},{8,9},{9,8},{10,11... | collective-permute-start | bytes 1572872 | tf_op jit(solution)/shard_map/ppermute | solution.py:55
  108.7 21.0 %copy-start = (bf16[8,2,512,256]{3,2,1,0:T(8,128)(2,1)S(1)}, bf16[8,2,512,256]{3,2,1,0:T(8,128)(2,1)}, u32[]{:S(2)}) copy-start(bf16[8,2,512,256]{3,2,1,0:T(8,128)(2,1)} %x.1) | copy-start | bytes 12582916
  108.7 21.0 %copy-start.2 = (bf16[2,2,512,256]{3,2,1,0:T(8,128)(2,1)S(1)}, bf16[2,2,512,256]{3,2,1,0:T(8,128)(2,1)}, u32[]{:S(2)}) copy-start(bf16[2,2,512,256]{3,2,1,0:T(8,128)(2,1)} %copy-done.1) | copy-start | bytes 3145732
  127.3 9.0 %copy-start.4 = (bf16[2,2,512,256]{3,2,1,0:T(8,128)(2,1)S(1)}, bf16[2,2,512,256]{3,2,1,0:T(8,128)(2,1)}, u32[]{:S(2)}) copy-start(bf16[2,2,512,256]{3,2,1,0:T(8,128)(2,1)} %copy-done.3) | copy-start | bytes 3145732
  127.3 9.0 %copy-start.6 = (bf16[2,2,512,256]{3,2,1,0:T(8,128)(2,1)S(1)}, bf16[2,2,512,256]{3,2,1,0:T(8,128)(2,1)}, u32[]{:S(2)}) copy-start(bf16[2,2,512,256]{3,2,1,0:T(8,128)(2,1)} %copy-done.5) | copy-start | bytes 3145732
  127.3 30.0 %collective-permute-start.26 = (bf16[2,2,512,256]{3,2,1,0:T(8,128)(2,1)S(1)}, bf16[2,2,512,256]{3,2,1,0:T(8,128)(2,1)S(1)}, u32[]{:S(2)}, u32[]{:S(2)}) collective-permute-start(bf16[2,2,512,256]{3,2,1,0:T(8,128)(2,1)S(1)} %broadcast_select_fusion.3), channel_id=1, source_target_pairs={{0,48},{1,49},{2,50},{3,51},{4,52},{5,53},{6,54},{7,55},{8,56},{9,... | collective-permute-start | bytes 3145736 | tf_op jit(solution)/shard_map/ppermute | solution.py:55
  129.7 1.2 copy-start.8
  136.3 18.6 %collective-permute-start.27 = (bf16[2,2,2,2,128,128]{5,4,3,2,1,0:T(8,128)(2,1)S(1)}, bf16[2,2,2,2,128,128]{5,4,3,2,1,0:T(8,128)(2,1)S(1)}, u32[]{:S(2)}, u32[]{:S(2)}) collective-permute-start(bf16[2,2,2,2,128,128]{5,4,3,2,1,0:T(8,128)(2,1)S(1)} %get-tuple-element.109), channel_id=1, source_target_pairs={{0,16},{1,17},{2,18},{3,19},{4,20},{5,21},{6,22},{7,23},{8,24},{9,... | collective-permute-start | bytes 1572872 | tf_op jit(solution)/shard_map/ppermute | solution.py:55
  141.2 16.1 %collective-permute-start.28 = (bf16[2,2,2,2,128,128]{5,4,3,2,1,0:T(8,128)(2,1)S(1)}, bf16[2,2,2,2,128,128]{5,4,3,2,1,0:T(8,128)(2,1)S(1)}, u32[]{:S(2)}, u32[]{:S(2)}) collective-permute-start(bf16[2,2,2,2,128,128]{5,4,3,2,1,0:T(8,128)(2,1)S(1)} %get-tuple-element.113), channel_id=1, source_target_pairs={{0,16},{1,17},{2,18},{3,19},{4,20},{5,21},{6,22},{7,23},{8,24},{9,... | collective-permute-start | bytes 1572872 | tf_op jit(solution)/shard_map/ppermute | solution.py:55
  141.9 13.0 %collective-permute-start.29 = (bf16[512,256]{1,0:T(8,128)(2,1)S(1)}, bf16[512,256]{1,0:T(8,128)(2,1)S(1)}, u32[]{:S(2)}, u32[]{:S(2)}) collective-permute-start(bf16[512,256]{1,0:T(8,128)(2,1)S(1)} %get-tuple-element.138), channel_id=1, source_target_pairs={{0,112},{1,113},{2,114},{3,115},{4,116},{5,117},{6,118},{7,119},{8... | collective-permute-start | bytes 786440 | tf_op jit(solution)/shard_map/ppermute | solution.py:55
  157.3 23.8 %collective-permute-start.30 = (bf16[2,2,512,256]{3,2,1,0:T(8,128)(2,1)S(1)}, bf16[2,2,512,256]{3,2,1,0:T(8,128)(2,1)S(1)}, u32[]{:S(2)}, u32[]{:S(2)}) collective-permute-start(bf16[2,2,512,256]{3,2,1,0:T(8,128)(2,1)S(1)} %collective-permute-done.26.rest_1_), channel_id=1, source_target_pairs={{0,112},{1,113},{2,114},{3,115},{4,116},{5,117},{6,118},{7,119},{8... | collective-permute-start | bytes 3145736 | tf_op jit(solution)/shard_map/ppermute | solution.py:55
  161.2 14.3 %collective-permute-start.31 = (bf16[2,2,2,2,128,128]{5,4,3,2,1,0:T(8,128)(2,1)S(1)}, bf16[2,2,2,2,128,128]{5,4,3,2,1,0:T(8,128)(2,1)S(1)}, u32[]{:S(2)}, u32[]{:S(2)}) collective-permute-start(bf16[2,2,2,2,128,128]{5,4,3,2,1,0:T(8,128)(2,1)S(1)} %get-tuple-element.121), channel_id=1, source_target_pairs={{0,16},{1,17},{2,18},{3,19},{4,20},{5,21},{6,22},{7,23},{8,24},{9,... | collective-permute-start | bytes 1572872 | tf_op jit(solution)/shard_map/ppermute | solution.py:55
  165.7 15.5 %collective-permute-start.32 = (bf16[2,2,2,2,128,128]{5,4,3,2,1,0:T(8,128)(2,1)S(1)}, bf16[2,2,2,2,128,128]{5,4,3,2,1,0:T(8,128)(2,1)S(1)}, u32[]{:S(2)}, u32[]{:S(2)}) collective-permute-start(bf16[2,2,2,2,128,128]{5,4,3,2,1,0:T(8,128)(2,1)S(1)} %get-tuple-element.123), channel_id=1, source_target_pairs={{0,16},{1,17},{2,18},{3,19},{4,20},{5,21},{6,22},{7,23},{8,24},{9,... | collective-permute-start | bytes 1572872 | tf_op jit(solution)/shard_map/ppermute | solution.py:55

commit v3 on v2

--- a/solution.py
+++ b/solution.py
@@ -146,16 +146,15 @@
         cross(lx, right, inv, o, out_write)
 
 
-def pairs_of(base, offsets, side, inv, scales, spectra, others, out):
+def pairs_of(base, count, offsets, side, inv, scales, spectra, others, out):
     bins_here, _, segs, chans = spectra.shape
-    count = others[0].shape[0]
     blk = (1, 2, segs, chans)
     in_specs = [
         pl.BlockSpec(memory_space=pltpu.SMEM),
         pl.BlockSpec(scales.shape, lambda f: (0, 0, 0)),
         pl.BlockSpec(blk, lambda f: (base + f, 0, 0, 0)),
-    ] + [pl.BlockSpec(blk, lambda f: (f, 0, 0, 0))] * len(others)
-    args = [inv, scales, spectra, *others]
+    ] + [pl.BlockSpec(blk, lambda f, at=at: (at + f, 0, 0, 0)) for _, at in others]
+    args = [inv, scales, spectra] + [array for array, _ in others]
     aliases = {}
     if out is not None:
         in_specs.append(pl.BlockSpec(memory_space=pl.ANY))
@@ -230,7 +229,9 @@
             copy.start()
 
     whiten(x.at[0], scales[0], wx)
-    whiten(far.at[0], scales[1], wf)
+    depth = far.shape[2]
+    wf[:depth, :] = far[0, 0]
+    wf[depth:, :] = far[0, 1]
     turn(wx, lx)
 
     def write(row, col, part, tile):
@@ -251,7 +252,9 @@
                     stores.append(
                         pltpu.make_async_copy(
                             src.at[row, col],
-                            out.at[row, 2 * offset + col - row, pl.ds(start, count)],
+                            out.at[
+                                row, 2 * offset + col - row, pl.ds(start, src.shape[2])
+                            ],
                             store_sems.at[i * 4 + row * 2 + col],
                         )
                     )
@@ -267,7 +270,6 @@
     n = len(spots)
     blk = (1, 2, segs, chans)
     anywhere = pl.BlockSpec(memory_space=pl.ANY)
-    res_shape = incoming[0].shape
     return pl.pallas_call(
         functools.partial(last_kernel, base, spots, count),
         grid=(count,),
@@ -282,7 +284,8 @@
         out_shape=jax.ShapeDtypeStruct(out.shape, out.dtype),
         scratch_shapes=[pltpu.VMEM((2 * segs, chans), BF16)] * 2
         + [pltpu.VMEM((2 * chans, 2 * segs), BF16)]
-        + [pltpu.VMEM(res_shape, BF16)] * (n + 1)
+        + [pltpu.VMEM((2, 2, count, 2, 128, 128), BF16)]
+        + [pltpu.VMEM(res.shape, BF16) for res in incoming]
         + [pltpu.SemaphoreType.DMA((n,)), pltpu.SemaphoreType.DMA((4 * (n + 1),))],
         input_output_aliases={4 + n: 0},
         cost_estimate=pl.CostEstimate(
@@ -304,7 +307,7 @@
     chunks = 4
     count = bins_here // chunks
     own = [spectra[i * count : (i + 1) * count] for i in range(chunks)]
-    Y, D, U, R = {}, {}, {}, {}
+    Y, D, U, R, res = {}, {}, {}, {}, {}
 
     def for_down(i):
         return jnp.where(z == 0, Y[i], own[i])
@@ -319,10 +322,10 @@
     piece = sum_pieces(partial, x, core)
     masks = {o: send(valid0, chan_route(-o)) for o in (1, 2, 3, 4)}
     masks[0] = valid0
-    Y[0], own[1], piece, masks = tie((Y[0], own[1], piece, masks))
+    Y[0], piece, masks = tie((Y[0], piece, masks))
 
     below, above = for_down(0), for_up(0)
-    below, above, piece, masks = tie((below, above, piece, masks))
+    below, above, masks, piece = tie((below, above, masks, piece))
     D[0], U[0] = send(below, DOWN), send(above, UP)
     Y[1] = send(own[1], CROSS)
     amplitude = piece + send(piece, Y_LO)
@@ -335,56 +338,71 @@
     right = jnp.stack([masks[b] for _, b in sides]).astype(F32)
     total = jnp.sum(left[:, :, None] * right[:, None], axis=-1)
     inv = (1.0 / jnp.maximum(total, 1.0)).reshape(-1)
-    Y[1], D[0], U[0], own[2], scale, inv = tie((Y[1], D[0], U[0], own[2], scale, inv))
+    Y[1], D[0], U[0] = tie((Y[1], D[0], U[0]))
+    Y[1], own[2], inv, scale = tie((Y[1], own[2], inv, scale))
 
     below, above = for_down(1), for_up(1)
-    below, above, scale = tie((below, above, scale))
+    below, above, scale, D[0], U[0] = tie((below, above, scale, D[0], U[0]))
     D[1], U[1] = send(below, DOWN), send(above, UP)
     Y[2] = send(own[2], CROSS)
     far = [scale] + [send(scale, chan_route(-o)) for o in (1, 3, 4)]
-    Y[2], D[1], U[1], own[3], far = tie((Y[2], D[1], U[1], own[3], far))
+    Y[2], D[1], U[1] = tie((Y[2], D[1], U[1]))
+    Y[2], own[3], far = tie((Y[2], own[3], far))
 
     below, above = for_down(2), for_up(2)
-    below, above, far = tie((below, above, far))
+    below, above, far, D[1], U[1] = tie((below, above, far, D[1], U[1]))
     D[2], U[2] = send(below, DOWN), send(above, UP)
     Y[3] = send(own[3], CROSS)
     scales = gather_core(gather_x(jnp.stack(far), x), core)
     out = None
-    res = {}
-
-    def pairs(i, offsets, side, others):
+
+    def pairs(i, base, n, offsets, side, others):
         nonlocal out
         out, res[i] = pairs_of(
-            i * count, offsets, side, inv, scales, spectra, others, out
+            base, n, offsets, side, inv, scales, spectra, others, out
         )
 
-    Y[3], D[2], U[2], scales, inv = tie((Y[3], D[2], U[2], scales, inv))
-
-    pairs(0, (0, 1, 4, 3), 5, (D[0], Y[0], U[0]))
+    def whole(i):
+        three = ((D[i], 0), (Y[i], 0), (U[i], 0))
+        pairs(i, i * count, count, (0, 1, 4, 3), 5, three)
+
+    whole(0)
     R[0] = send(res[0], NEXT)
-    D[3] = send(for_down(3), DOWN)
-    scale2 = send(scales[1], chan_route(-1))
-    pairs(1, (0, 1, 4, 3), 5, (D[1], Y[1], U[1]))
+    Y[3], D[2], U[2] = tie((Y[3], D[2], U[2]))
+    Y[3], scales, out = tie((Y[3], scales, out))
+
+    def whitened(block):
+        return (block.astype(F32) * scales[1].astype(F32)).astype(BF16)
+
+    below = for_down(3)
+    below, D[2], U[2], scales = tie((below, D[2], U[2], scales))
+    half = count // 2
+    last = 3 * count
+    first, second = send(below[:half], DOWN), send(below[half:], DOWN)
+    whole(1)
     R[1] = send(res[1], NEXT)
-    pairs(2, (0, 1, 4, 3), 5, (D[2], Y[2], U[2]))
-    D[3], R[0], R[1], out, res[2], scale2 = tie(
-        (D[3], R[0], R[1], out, res[2], scale2)
-    )
-
-    far2 = send(D[3], chan_route(-1))
+    whole(2)
     R[2] = send(res[2], NEXT)
-    pairs(3, (0, 1, 4), 6, (D[3], Y[3]))
+    first, R[0], out = tie((first, R[0], out))
+
+    beyond = send(whitened(first), chan_route(-1))
+    pairs(3, last, half, (0, 1, 4), 6, ((first, 0), (Y[3], 0)))
     R[3] = send(res[3], NEXT)
+    second, R[1], out = tie((second, R[1], out))
+    beyond2 = send(whitened(second), chan_route(-1))
+    pairs(4, last + half, half, (0, 1, 4), 6, ((second, 0), (Y[3], half)))
+    R[4] = send(res[4], NEXT)
     for i in (0, 1):
         out = placed(i * count, 2, R[i], out)
+    out = last_of(last, inv, scales, spectra, beyond, ((2 * count, 2),), (R[2],), out)
     return last_of(
-        3 * count,
+        last + half,
         inv,
-        jnp.stack([scales[0], scale2]),
+        scales,
         spectra,
-        far2,
-        ((2 * count, 2), (3 * count, 3)),
-        (R[2], R[3]),
+        beyond2,
+        ((last, 3), (last + half, 3)),
+        (R[3], R[4]),
         out,
     )
 

time: 185 us -> 179 us (0.968); the launches traced: 184 us -> 176 us
  waiting for transfers between devices: 84.3 us -> 69.1 us
  local copies, waits for them, and re-layouts: 8.55 us -> 12.5 us
  Pallas kernels: 26 us -> 28.7 us
    ppermute x33 -> x35, waiting for transfers between devices: 84.3 us -> 69.1 us  [send(): return lax.ppermute(value, AXES, pairs)]
    unnamed x39 -> x43, local copies, waits for them, and re-layouts: 3.37 us -> 7.82 us
    pallas_call x4 -> x5, Pallas kernels: 20.3 us -> 21.8 us  [pairs_of(): pl.pallas_call(functools.partial(pair_kernel, offsets, side), grid=(count...]
    ppermute x33 -> x35, starting transfers between devices: 53 us -> 51.8 us  [send(): return lax.ppermute(value, AXES, pairs)]
    pallas_call x1 -> x2, Pallas kernels: 3 us -> 4.1 us  [last_of(): pl.pallas_call(functools.partial(last_kernel, base, spots, count), grid=(...]
  transfers between devices with their start and end apart: 33 -> 35, of which waited for: 17 -> 18; matrix products, arithmetic and copies ran while one was open for 6% -> 7% of each run, Pallas kernels for 12% -> 15%
where the time goes in v3:
time: 179 us; the launch traced here: 176 us
  waiting for transfers between devices  69.1 us (39%)
  starting transfers between devices  51.8 us (29%)
  Pallas kernels  28.7 us (16%)
  other arithmetic  13.5 us (8%)
  local copies, waits for them, and re-layouts  12.5 us (7%)
    ppermute x35, waiting for transfers between devices, send(): return lax.ppermute(value, AXES, pairs)  69.1 us
    ppermute x35, starting transfers between devices, send(): return lax.ppermute(value, AXES, pairs)  51.8 us
    pallas_call x5, Pallas kernels, pairs_of(): pl.pallas_call(functools.partial(pair_kernel, offsets, side), grid=(count...  21.8 us
    unnamed x43, local copies, waits for them, and re-layouts  7.82 us
    select_n x3, other arithmetic, for_up(): return jnp.where(z == 3, own[i], Y[i])  5.76 us
    pallas_call x2, Pallas kernels, last_of(): pl.pallas_call(functools.partial(last_kernel, base, spots, count), grid=(...  4.1 us
  transfers between devices with their start and end apart: 35, of which 18 were waited for; matrix products, arithmetic and copies ran while one was open for 7% of the time, Pallas kernels for 15%

profile of v3, /device:TPU:6, one launch (start us, length us, event | category | flops | bytes accessed | tf_op | source)
XLA Modules:
  0.0 176.0 jit_solution(13583713712113894125)
XLA Ops:
  0.0 3.4 %fusion.6 = (bf16[2,2,512,256]{3,2,1,0:T(8,128)(2,1)}, bf16[2,2,512,256]{3,2,1,0:T(8,128)(2,1)S(1)}, bf16[2,2,512,256]{3,2,1,0:T(8,128)(2,1)}) fusion(bf16[8,2,512,256]{3,2,1,0:T(8,128)(2,1)} %x.3), kind=kLoop, calls=%fused_computation.53 | loop fusion | bytes 6291456 | tf_op jit(solution)/shard_map/slice | solution.py:309
  3.4 3.2 %collective-permute-start.1 = (bf16[2,2,512,256]{3,2,1,0:T(8,128)(2,1)S(1)}, bf16[2,2,512,256]{3,2,1,0:T(8,128)(2,1)S(1)}, u32[]{:S(2)}, u32[]{:S(2)}) collective-permute-start(bf16[2,2,512,256]{3,2,1,0:T(8,128)(2,1)S(1)} %get-tuple-element.78), channel_id=1, source_target_pairs={{0,64},{1,65},{2,66},{3,67},{4,68},{5,69},{6,70},{7,71},{8,72},{9,... | collective-permute-start | bytes 3145736 | tf_op jit(solution)/shard_map/ppermute | solution.py:55
  6.6 3.1 %convert_element_type.46 = f32[8,2,512,256]{3,2,1,0:T(8,128)S(1)} convert(bf16[8,2,512,256]{3,2,1,0:T(8,128)(2,1)} %x.3) | non-fusion elementwise | flops 2097152 | bytes 12582912 | tf_op jit(solution)/shard_map/convert_element_type | solution.py:320
  9.7 1.5 fusion.2
  11.8 1.1 collective-permute-done.2
  12.9 0.5 collective-permute-start.3
  13.5 1.5 collective-permute-start.5
  15.0 1.4 collective-permute-start.4
  16.6 0.7 collective-permute-done.3
  17.3 3.5 %collective-permute-start.8 = (s32[2,512]{1,0:T(2,128)S(1)}, s32[2,512]{1,0:T(2,128)S(1)}, u32[]{:S(2)}, u32[]{:S(2)}) collective-permute-start(s32[2,512]{1,0:T(2,128)S(1)} %copy-done.12), channel_id=1, source_target_pairs={{0,80},{1,81},{2,82},{3,83},{4,84},{5,85},{6,86},{7,87},{8,88},{9,... | collective-permute-start | bytes 12296 | tf_op jit(solution)/shard_map/ppermute | solution.py:55
  20.7 4.4 %collective-permute-start.7 = (s32[2,512]{1,0:T(2,128)S(1)}, s32[2,512]{1,0:T(2,128)S(1)}, u32[]{:S(2)}, u32[]{:S(2)}) collective-permute-start(s32[2,512]{1,0:T(2,128)S(1)} %copy-done.12), channel_id=1, source_target_pairs={{0,96},{1,97},{2,98},{3,99},{4,100},{5,101},{6,102},{7,103},{8,104... | collective-permute-start | bytes 12296 | tf_op jit(solution)/shard_map/ppermute | solution.py:55
  25.2 1.2 collective-permute-start.6
  26.4 3.6 %collective-permute-done.9 = s32[2,512]{1,0:T(2,128)S(1)} collective-permute-done((s32[2,512]{1,0:T(2,128)S(1)}, s32[2,512]{1,0:T(2,128)S(1)}, u32[]{:S(2)}, u32[]{:S(2)}) %collective-permute-start.9) | collective-permute-done | bytes 4128 | tf_op jit(solution)/shard_map/ppermute | solution.py:55
  30.0 3.2 %collective-permute-start = (bf16[2,2,512,256]{3,2,1,0:T(8,128)(2,1)}, bf16[2,2,512,256]{3,2,1,0:T(8,128)(2,1)S(1)}, u32[]{:S(2)}, u32[]{:S(2)}) collective-permute-start(bf16[2,2,512,256]{3,2,1,0:T(8,128)(2,1)} %get-tuple-element.156), channel_id=1, source_target_pairs={{0,64},{1,65},{2,66},{3,67},{4,68},{5,69},{6,70},{7,71},{8,72},{9,... | collective-permute-start | bytes 3145736 | tf_op jit(solution)/shard_map/ppermute | solution.py:55
  33.2 1.6 broadcast_select_fusion.2
  34.9 4.0 %collective-permute-start.10 = (bf16[2,2,512,256]{3,2,1,0:T(8,128)(2,1)}, bf16[2,2,512,256]{3,2,1,0:T(8,128)(2,1)S(1)}, u32[]{:S(2)}, u32[]{:S(2)}) collective-permute-start(bf16[2,2,512,256]{3,2,1,0:T(8,128)(2,1)} %get-tuple-element.88), channel_id=1, source_target_pairs={{0,48},{1,49},{2,50},{3,51},{4,52},{5,53},{6,54},{7,55},{8,56},{9,... | collective-permute-start | bytes 3145736 | tf_op jit(solution)/shard_map/ppermute | solution.py:55
  39.0 0.8 collective-permute-start.12
  39.9 17.4 %collective-permute-done.12 = f32[64,256]{1,0:T(8,128)S(1)} collective-permute-done((f32[64,256]{1,0:T(8,128)S(1)}, f32[64,256]{1,0:T(8,128)S(1)}, u32[]{:S(2)}, u32[]{:S(2)}) %collective-permute-start.12) | collective-permute-done | bytes 65568 | tf_op jit(solution)/shard_map/ppermute | solution.py:55
  57.5 2.9 %collective-permute-done.10.rest_1_ = bf16[2,2,512,256]{3,2,1,0:T(8,128)(2,1)S(1)} collective-permute-done((bf16[2,2,512,256]{3,2,1,0:T(8,128)(2,1)}, bf16[2,2,512,256]{3,2,1,0:T(8,128)(2,1)S(1)}, u32[]{:S(2)}, u32[]{:S(2)}) %collective-permute-start.10) | collective-permute-done | bytes 1048608 | tf_op jit(solution)/shard_map/ppermute | solution.py:55
  60.4 1.0 copy-done.8
  61.5 2.4 %collective-permute-done.11.rest_3_ = bf16[2,2,512,256]{3,2,1,0:T(8,128)(2,1)} collective-permute-done((bf16[2,2,512,256]{3,2,1,0:T(8,128)(2,1)}, bf16[2,2,512,256]{3,2,1,0:T(8,128)(2,1)}, u32[]{:S(2)}, u32[]{:S(2)}) %collective-permute-start.11) | collective-permute-done | bytes 1048608 | tf_op jit(solution)/shard_map/ppermute | solution.py:55
  64.2 2.7 %broadcast_select_fusion.1 = (bf16[2,2,512,256]{3,2,1,0:T(8,128)(2,1)S(1)}, bf16[2,2,512,256]{3,2,1,0:T(8,128)(2,1)S(1)}, bf16[2,2,512,256]{3,2,1,0:T(8,128)(2,1)}) fusion(bf16[2,2,512,256]{3,2,1,0:T(8,128)(2,1)S(1)} %collective-permute-done.rest_2_, pred[]{:T(512)S(6)} %eq.22, bf16[8,2,512,256]{3,2,1,0:T(8,128)(2,1)} %x.3, pred[]{:T(512)S(6)} %eq.21), kind=kLoop, calls=%fused_computation.9 | loop fusion | flops 1048576 | bytes 6291458 | tf_op jit(solution)/shard_map/jit(_where)/select_n | solution.py:316
  66.9 1.2 collective-permute-start.14
  68.1 0.8 collective-permute-start.15
  68.9 3.2 %collective-permute-start.18 = (bf16[64,256]{1,0:T(8,128)(2,1)S(1)}, bf16[64,256]{1,0:T(8,128)(2,1)S(1)}, u32[]{:S(2)}, u32[]{:S(2)}) collective-permute-start(bf16[64,256]{1,0:T(8,128)(2,1)S(1)} %fusion.3), channel_id=1, source_target_pairs={{0,64},{1,65},{2,66},{3,67},{4,68},{5,69},{6,70},{7,71},{8,72},{9,... | collective-permute-start | bytes 98312 | tf_op jit(solution)/shard_map/ppermute | solution.py:55
  72.1 16.7 %collective-permute-done.13.rest_2_ = bf16[2,2,512,256]{3,2,1,0:T(8,128)(2,1)S(1)} collective-permute-done((bf16[2,2,512,256]{3,2,1,0:T(8,128)(2,1)}, bf16[2,2,512,256]{3,2,1,0:T(8,128)(2,1)S(1)}, u32[]{:S(2)}, u32[]{:S(2)}) %collective-permute-start.13) | collective-permute-done | bytes 1048608 | tf_op jit(solution)/shard_map/ppermute | solution.py:55
  88.8 0.9 collective-permute-start.16
  89.7 1.0 copy-done.4
  90.7 1.2 collective-permute-done.15.rest_3_
  92.0 1.0 copy-done.6
  93.0 1.5 broadcast_select_fusion
  94.4 0.7 pad_maximum_fusion
  95.1 0.8 collective-permute-start.22
  95.9 1.1 collective-permute-start.23
  97.0 2.1 %collective-permute-start.24 = (bf16[4,64,256]{2,1,0:T(8,128)(2,1)}, bf16[4,64,256]{2,1,0:T(8,128)(2,1)S(1)}, u32[]{:S(2)}, u32[]{:S(2)}) collective-permute-start(bf16[4,64,256]{2,1,0:T(8,128)(2,1)} %pad_maximum_fusion), channel_id=1, source_target_pairs={{0,2},{1,3},{2,4},{3,5},{4,6},{5,7},{6,0},{7,1},{8,10},{9,11},{10,... | collective-permute-start | bytes 393224 | tf_op jit(solution)/shard_map/ppermute | solution.py:55
  99.1 4.5 %collective-permute-start.20 = (bf16[2,2,512,256]{3,2,1,0:T(8,128)(2,1)}, bf16[2,2,512,256]{3,2,1,0:T(8,128)(2,1)}, u32[]{:S(2)}, u32[]{:S(2)}) collective-permute-start(bf16[2,2,512,256]{3,2,1,0:T(8,128)(2,1)} %get-tuple-element.115), channel_id=1, source_target_pairs={{0,48},{1,49},{2,50},{3,51},{4,52},{5,53},{6,54},{7,55},{8,56},{9,... | collective-permute-start | bytes 3145736 | tf_op jit(solution)/shard_map/ppermute | solution.py:55
  103.7 2.4 %collective-permute-start.19 = (bf16[2,2,512,256]{3,2,1,0:T(8,128)(2,1)}, bf16[2,2,512,256]{3,2,1,0:T(8,128)(2,1)S(1)}, u32[]{:S(2)}, u32[]{:S(2)}) collective-permute-start(bf16[2,2,512,256]{3,2,1,0:T(8,128)(2,1)} %get-tuple-element.107), channel_id=1, source_target_pairs={{0,64},{1,65},{2,66},{3,67},{4,68},{5,69},{6,70},{7,71},{8,72},{9,... | collective-permute-start | bytes 3145736 | tf_op jit(solution)/shard_map/ppermute | solution.py:55
  106.3 0.8 constant_dynamic-slice_fusion
  107.1 2.2 %collective-permute-done.25 = bf16[4,256,256]{2,1,0:T(8,128)(2,1)} collective-permute-done((bf16[4,256,256]{2,1,0:T(8,128)(2,1)}, bf16[4,256,256]{2,1,0:T(8,128)(2,1)}, u32[]{:S(2)}, u32[]{:S(2)}) %collective-permute-start.25) | collective-permute-done | bytes 524320 | tf_op jit(solution)/shard_map/ppermute | solution.py:55
  109.4 1.8 %maximum_select_fusion.scales = bf16[4,512,256]{2,1,0:T(8,128)(2,1)S(1)} fusion(bf16[4,256,256]{2,1,0:T(8,128)(2,1)} %collective-permute-done.25, bf16[4,256,256]{2,1,0:T(8,128)(2,1)} %constant_dynamic-slice_fusion, pred[]{:T(512)S(6)} %eq.23), kind=kLoop, calls=%fused_computation.5 | loop fusion | flops 4718592 | bytes 2097153 | tf_op jit(solution)/shard_map/jit(_where)/select_n | solution.py:85
  111.2 2.2 %copy-done = bf16[8,2,512,256]{3,2,1,0:T(8,128)(2,1)S(1)} copy-done((bf16[8,2,512,256]{3,2,1,0:T(8,128)(2,1)S(1)}, bf16[8,2,512,256]{3,2,1,0:T(8,128)(2,1)}, u32[]{:S(2)}) %copy-start) | copy-done | bytes 4194328
  113.4 1.2 copy-done.3
  114.6 1.2 copy-done.9
  115.8 5.4 %shard_map.28 = (bf16[2,9,8,2,128,128]{5,4,3,2,1,0:T(8,128)(2,1)}, bf16[2,2,2,2,128,128]{5,4,3,2,1,0:T(8,128)(2,1)S(1)}) custom-call(f32[28]{0:T(128)S(1)} %div.28.inv, bf16[4,512,256]{2,1,0:T(8,128)(2,1)S(1)} %maximum_select_fusion.scales, bf16[8,2,512,256]{3,2,1,0:T(8,128)(2,1)S(1)} %copy-done, bf16[2,2,512,256]{3,2,1,0:T(8,128)(2,1)S(1)} %copy-done.9, ...), custom_call_target="tpu_custom_call" | custom-call | flops 2684354560 | bytes 8388608 | tf_op jit(solution)/shard_map/pallas_call | solution.py:163
  121.3 3.2 %collective-permute-done.21.rest_3_ = bf16[2,2,512,256]{3,2,1,0:T(8,128)(2,1)} collective-permute-done((bf16[2,2,512,256]{3,2,1,0:T(8,128)(2,1)}, bf16[2,2,512,256]{3,2,1,0:T(8,128)(2,1)}, u32[]{:S(2)}, u32[]{:S(2)}) %collective-permute-start.21) | collective-permute-done | bytes 1048608 | tf_op jit(solution)/shard_map/ppermute | solution.py:55
  124.9 3.9 %collective-permute-start.28 = (bf16[1,2,512,256]{3,2,1,0:T(8,128)(2,1)S(1)}, bf16[1,2,512,256]{3,2,1,0:T(8,128)(2,1)S(1)}, u32[]{:S(2)}, u32[]{:S(2)}) collective-permute-start(bf16[1,2,512,256]{3,2,1,0:T(8,128)(2,1)S(1)} %get-tuple-element.161), channel_id=1, source_target_pairs={{0,48},{1,49},{2,50},{3,51},{4,52},{5,53},{6,54},{7,55},{8,56},{9,... | collective-permute-start | bytes 1572872 | tf_op jit(solution)/shard_map/ppermute | solution.py:55
  128.9 4.9 %shard_map.29 = (bf16[2,9,8,2,128,128]{5,4,3,2,1,0:T(8,128)(2,1)}, bf16[2,2,2,2,128,128]{5,4,3,2,1,0:T(8,128)(2,1)S(1)}) custom-call(f32[28]{0:T(128)S(1)} %div.28.inv, bf16[4,512,256]{2,1,0:T(8,128)(2,1)S(1)} %maximum_select_fusion.scales, bf16[8,2,512,256]{3,2,1,0:T(8,128)(2,1)S(1)} %copy-done, ...), custom_call_target="tpu_custom_call", output_to_operand_aliasing={{0}: (6, {})} | custom-call | flops 2684354560 | bytes 8388608 | tf_op jit(solution)/shard_map/pallas_call | solution.py:163
  133.8 1.9 %collective-permute-start.27 = (bf16[2,2,2,2,128,128]{5,4,3,2,1,0:T(8,128)(2,1)S(1)}, bf16[2,2,2,2,128,128]{5,4,3,2,1,0:T(8,128)(2,1)S(1)}, u32[]{:S(2)}, u32[]{:S(2)}) collective-permute-start(bf16[2,2,2,2,128,128]{5,4,3,2,1,0:T(8,128)(2,1)S(1)} %get-tuple-element.134), channel_id=1, source_target_pairs={{0,16},{1,17},{2,18},{3,19},{4,20},{5,21},{6,22},{7,23},{8,24},{9,... | collective-permute-start | bytes 1572872 | tf_op jit(solution)/shard_map/ppermute | solution.py:55
  135.7 5.6 %shard_map.30 = (bf16[2,9,8,2,128,128]{5,4,3,2,1,0:T(8,128)(2,1)}, bf16[2,2,2,2,128,128]{5,4,3,2,1,0:T(8,128)(2,1)S(1)}) custom-call(f32[28]{0:T(128)S(1)} %div.28.inv, bf16[4,512,256]{2,1,0:T(8,128)(2,1)S(1)} %maximum_select_fusion.scales, bf16[8,2,512,256]{3,2,1,0:T(8,128)(2,1)S(1)} %copy-done, ...), custom_call_target="tpu_custom_call", output_to_operand_aliasing={{0}: (6, {})} | custom-call | flops 2684354560 | bytes 8388608 | tf_op jit(solution)/shard_map/pallas_call | solution.py:163
  141.3 3.0 %shard_map.31 = (bf16[2,9,8,2,128,128]{5,4,3,2,1,0:T(8,128)(2,1)}, bf16[2,2,1,2,128,128]{5,4,3,2,1,0:T(8,128)(2,1)S(1)}) custom-call(f32[28]{0:T(128)S(1)} %div.28.inv, bf16[4,512,256]{2,1,0:T(8,128)(2,1)S(1)} %maximum_select_fusion.scales, bf16[8,2,512,256]{3,2,1,0:T(8,128)(2,1)S(1)} %copy-done, ...), custom_call_target="tpu_custom_call", output_to_operand_aliasing={{0}: (5, {})} | custom-call | flops 1342177280 | bytes 4194304 | tf_op jit(solution)/shard_map/pallas_call | solution.py:163
  144.3 3.4 %collective-permute-done.26.rest_1_ = bf16[1,2,512,256]{3,2,1,0:T(8,128)(2,1)S(1)} collective-permute-done((bf16[1,2,512,256]{3,2,1,0:T(8,128)(2,1)S(1)}, bf16[1,2,512,256]{3,2,1,0:T(8,128)(2,1)S(1)}, u32[]{:S(2)}, u32[]{:S(2)}) %collective-permute-start.26) | collective-permute-done | bytes 524320 | tf_op jit(solution)/shard_map/ppermute | solution.py:55
  147.8 4.5 %collective-permute-done.27.res = bf16[2,2,2,2,128,128]{5,4,3,2,1,0:T(8,128)(2,1)S(1)} collective-permute-done((bf16[2,2,2,2,128,128]{5,4,3,2,1,0:T(8,128)(2,1)S(1)}, bf16[2,2,2,2,128,128]{5,4,3,2,1,0:T(8,128)(2,1)S(1)}, u32[]{:S(2)}, u32[]{:S(2)}) %collective-permute-start.27) | collective-permute-done | bytes 524320 | tf_op jit(solution)/shard_map/ppermute | solution.py:55
  152.4 1.2 collective-permute-start.33
  153.7 3.0 %shard_map.32 = (bf16[2,9,8,2,128,128]{5,4,3,2,1,0:T(8,128)(2,1)}, bf16[2,2,1,2,128,128]{5,4,3,2,1,0:T(8,128)(2,1)S(1)}) custom-call(f32[28]{0:T(128)S(1)} %div.28.inv, bf16[4,512,256]{2,1,0:T(8,128)(2,1)S(1)} %maximum_select_fusion.scales, bf16[8,2,512,256]{3,2,1,0:T(8,128)(2,1)S(1)} %copy-done, ...), custom_call_target="tpu_custom_call", output_to_operand_aliasing={{0}: (5, {})} | custom-call | flops 1342177280 | bytes 4194304 | tf_op jit(solution)/shard_map/pallas_call | solution.py:163
  156.7 1.9 %collective-permute-start.32 = (bf16[2,2,1,2,128,128]{5,4,3,2,1,0:T(8,128)(2,1)S(1)}, bf16[2,2,1,2,128,128]{5,4,3,2,1,0:T(8,128)(2,1)S(1)}, u32[]{:S(2)}, u32[]{:S(2)}) collective-permute-start(bf16[2,2,1,2,128,128]{5,4,3,2,1,0:T(8,128)(2,1)S(1)} %get-tuple-element.146), channel_id=1, source_target_pairs={{0,16},{1,17},{2,18},{3,19},{4,20},{5,21},{6,22},{7,23},{8,24},{9,... | collective-permute-start | bytes 786440 | tf_op jit(solution)/shard_map/ppermute | solution.py:55
  158.6 0.9 collective-permute-start.31
  159.6 1.4 shard_map.33.old
  160.9 1.4 shard_map.34.rest_1_
  162.3 0.9 collective-permute-done.34.rest_0_
  163.2 4.2 %collective-permute-done.33.far = bf16[1,2,512,256]{3,2,1,0:T(8,128)(2,1)S(1)} collective-permute-done((bf16[1,2,512,256]{3,2,1,0:T(8,128)(2,1)S(1)}, bf16[1,2,512,256]{3,2,1,0:T(8,128)(2,1)S(1)}, u32[]{:S(2)}, u32[]{:S(2)}) %collective-permute-start.33) | collective-permute-done | bytes 524320 | tf_op jit(solution)/shard_map/ppermute | solution.py:55
  167.4 2.0 %shard_map.35.rest_2_ = bf16[2,9,8,2,128,128]{5,4,3,2,1,0:T(8,128)(2,1)} custom-call(f32[28]{0:T(128)S(1)} %div.28.inv, bf16[4,512,256]{2,1,0:T(8,128)(2,1)S(1)} %maximum_select_fusion.scales, bf16[8,2,512,256]{3,2,1,0:T(8,128)(2,1)S(1)} %copy-done.1, bf16[1,2,512,256]{3,2,1,0:T(8,128)(2,1)S(1)} %collective-permute-done.33.far, ...), custom_call_target="tpu_custom_call", output_to_operand_aliasing={{}: (5, {})} | custom-call | flops 268435456 | bytes 4194304 | tf_op jit(solution)/shard_map/pallas_call | solution.py:273
  169.5 3.2 %collective-permute-done.31.rest_0_ = bf16[2,2,1,2,128,128]{5,4,3,2,1,0:T(8,128)(2,1)S(1)} collective-permute-done((bf16[2,2,1,2,128,128]{5,4,3,2,1,0:T(8,128)(2,1)S(1)}, bf16[2,2,1,2,128,128]{5,4,3,2,1,0:T(8,128)(2,1)S(1)}, u32[]{:S(2)}, u32[]{:S(2)}) %collective-permute-start.31) | collective-permute-done | bytes 262176 | tf_op jit(solution)/shard_map/ppermute | solution.py:55
  172.8 1.0 collective-permute-done.30.far
  173.8 2.1 %shard_map.36 = bf16[2,9,8,2,128,128]{5,4,3,2,1,0:T(8,128)(2,1)} custom-call(f32[28]{0:T(128)S(1)} %div.28.inv, bf16[4,512,256]{2,1,0:T(8,128)(2,1)S(1)} %maximum_select_fusion.scales, bf16[8,2,512,256]{3,2,1,0:T(8,128)(2,1)S(1)} %copy-done.1, bf16[1,2,512,256]{3,2,1,0:T(8,128)(2,1)S(1)} %collective-permute-done.30.far, ...), custom_call_target="tpu_custom_call", output_to_operand_aliasing={{}: (6, {})} | custom-call | flops 268435456 | bytes 4194304 | tf_op jit(solution)/shard_map/pallas_call | solution.py:273
  (88 shorter events, 2.7 us)
Async XLA Ops:
  3.4 29.8 %collective-permute-start.1 = (bf16[2,2,512,256]{3,2,1,0:T(8,128)(2,1)S(1)}, bf16[2,2,512,256]{3,2,1,0:T(8,128)(2,1)S(1)}, u32[]{:S(2)}, u32[]{:S(2)}) collective-permute-start(bf16[2,2,512,256]{3,2,1,0:T(8,128)(2,1)S(1)} %get-tuple-element.78), channel_id=1, source_target_pairs={{0,64},{1,65},{2,66},{3,67},{4,68},{5,69},{6,70},{7,71},{8,72},{9,... | collective-permute-start | bytes 3145736 | tf_op jit(solution)/shard_map/ppermute | solution.py:55
  9.7 1.7 copy-start.12
  11.2 1.6 collective-permute-start.2
  11.3 18.7 %collective-permute-start.9 = (s32[2,512]{1,0:T(2,128)S(1)}, s32[2,512]{1,0:T(2,128)S(1)}, u32[]{:S(2)}, u32[]{:S(2)}) collective-permute-start(s32[2,512]{1,0:T(2,128)S(1)} %copy-done.12), channel_id=1, source_target_pairs={{0,64},{1,65},{2,66},{3,67},{4,68},{5,69},{6,70},{7,71},{8,72},{9,... | collective-permute-start | bytes 12296 | tf_op jit(solution)/shard_map/ppermute | solution.py:55
  12.9 4.3 %collective-permute-start.3 = (f32[64,256]{1,0:T(8,128)S(1)}, f32[64,256]{1,0:T(8,128)S(1)}, u32[]{:S(2)}, u32[]{:S(2)}) collective-permute-start(f32[64,256]{1,0:T(8,128)S(1)} %get-tuple-element.165), channel_id=1, source_target_pairs={{0,2},{1,3},{2,4},{3,5},{4,6},{5,7},{6,0},{7,1},{8,10},{9,11},{10,... | collective-permute-start | bytes 196616 | tf_op jit(solution)/shard_map/ppermute | solution.py:55
  13.5 7.2 %collective-permute-start.5 = (f32[64,256]{1,0:T(8,128)S(1)}, f32[64,256]{1,0:T(8,128)S(1)}, u32[]{:S(2)}, u32[]{:S(2)}) collective-permute-start(f32[64,256]{1,0:T(8,128)S(1)} %get-tuple-element.166), channel_id=1, source_target_pairs={{0,6},{1,7},{2,0},{3,1},{4,2},{5,3},{6,4},{7,5},{8,14},{9,15},{10,... | collective-permute-start | bytes 196616 | tf_op jit(solution)/shard_map/ppermute | solution.py:55
  15.0 10.2 %collective-permute-start.4 = (f32[64,256]{1,0:T(8,128)S(1)}, f32[64,256]{1,0:T(8,128)S(1)}, u32[]{:S(2)}, u32[]{:S(2)}) collective-permute-start(f32[64,256]{1,0:T(8,128)S(1)} %get-tuple-element.167), channel_id=1, source_target_pairs={{0,4},{1,5},{2,6},{3,7},{4,0},{5,1},{6,2},{7,3},{8,12},{9,13},{10,... | collective-permute-start | bytes 196616 | tf_op jit(solution)/shard_map/ppermute | solution.py:55
  17.3 15.9 %collective-permute-start.8 = (s32[2,512]{1,0:T(2,128)S(1)}, s32[2,512]{1,0:T(2,128)S(1)}, u32[]{:S(2)}, u32[]{:S(2)}) collective-permute-start(s32[2,512]{1,0:T(2,128)S(1)} %copy-done.12), channel_id=1, source_target_pairs={{0,80},{1,81},{2,82},{3,83},{4,84},{5,85},{6,86},{7,87},{8,88},{9,... | collective-permute-start | bytes 12296 | tf_op jit(solution)/shard_map/ppermute | solution.py:55
  20.7 12.5 %collective-permute-start.7 = (s32[2,512]{1,0:T(2,128)S(1)}, s32[2,512]{1,0:T(2,128)S(1)}, u32[]{:S(2)}, u32[]{:S(2)}) collective-permute-start(s32[2,512]{1,0:T(2,128)S(1)} %copy-done.12), channel_id=1, source_target_pairs={{0,96},{1,97},{2,98},{3,99},{4,100},{5,101},{6,102},{7,103},{8,104... | collective-permute-start | bytes 12296 | tf_op jit(solution)/shard_map/ppermute | solution.py:55
  25.2 8.0 %collective-permute-start.6 = (s32[2,512]{1,0:T(2,128)S(1)}, s32[2,512]{1,0:T(2,128)S(1)}, u32[]{:S(2)}, u32[]{:S(2)}) collective-permute-start(s32[2,512]{1,0:T(2,128)S(1)} %copy-done.12), channel_id=1, source_target_pairs={{0,112},{1,113},{2,114},{3,115},{4,116},{5,117},{6,118},{7,119},{8... | collective-permute-start | bytes 12296 | tf_op jit(solution)/shard_map/ppermute | solution.py:55
  30.0 27.5 %collective-permute-start = (bf16[2,2,512,256]{3,2,1,0:T(8,128)(2,1)}, bf16[2,2,512,256]{3,2,1,0:T(8,128)(2,1)S(1)}, u32[]{:S(2)}, u32[]{:S(2)}) collective-permute-start(bf16[2,2,512,256]{3,2,1,0:T(8,128)(2,1)} %get-tuple-element.156), channel_id=1, source_target_pairs={{0,64},{1,65},{2,66},{3,67},{4,68},{5,69},{6,70},{7,71},{8,72},{9,... | collective-permute-start | bytes 3145736 | tf_op jit(solution)/shard_map/ppermute | solution.py:55
  33.2 33.7 %copy-start.2 = (bf16[2,2,512,256]{3,2,1,0:T(8,128)(2,1)}, bf16[2,2,512,256]{3,2,1,0:T(8,128)(2,1)S(1)}, u32[]{:S(2)}) copy-start(bf16[2,2,512,256]{3,2,1,0:T(8,128)(2,1)S(1)} %collective-permute-done.1.rest_2_) | copy-start | bytes 3145732
  34.9 25.6 %collective-permute-start.10 = (bf16[2,2,512,256]{3,2,1,0:T(8,128)(2,1)}, bf16[2,2,512,256]{3,2,1,0:T(8,128)(2,1)S(1)}, u32[]{:S(2)}, u32[]{:S(2)}) collective-permute-start(bf16[2,2,512,256]{3,2,1,0:T(8,128)(2,1)} %get-tuple-element.88), channel_id=1, source_target_pairs={{0,48},{1,49},{2,50},{3,51},{4,52},{5,53},{6,54},{7,55},{8,56},{9,... | collective-permute-start | bytes 3145736 | tf_op jit(solution)/shard_map/ppermute | solution.py:55
  38.9 25.0 %collective-permute-start.11 = (bf16[2,2,512,256]{3,2,1,0:T(8,128)(2,1)}, bf16[2,2,512,256]{3,2,1,0:T(8,128)(2,1)}, u32[]{:S(2)}, u32[]{:S(2)}) collective-permute-start(bf16[2,2,512,256]{3,2,1,0:T(8,128)(2,1)} %get-tuple-element.89), channel_id=1, source_target_pairs={{0,16},{1,17},{2,18},{3,19},{4,20},{5,21},{6,22},{7,23},{8,24},{9,... | collective-permute-start | bytes 3145736 | tf_op jit(solution)/shard_map/ppermute | solution.py:55
  39.0 18.4 %collective-permute-start.12 = (f32[64,256]{1,0:T(8,128)S(1)}, f32[64,256]{1,0:T(8,128)S(1)}, u32[]{:S(2)}, u32[]{:S(2)}) collective-permute-start(f32[64,256]{1,0:T(8,128)S(1)} %add_add_fusion), channel_id=1, source_target_pairs={{0,8},{1,9},{2,10},{3,11},{4,12},{5,13},{6,14},{7,15},{8,0},{9,1},... | collective-permute-start | bytes 196616 | tf_op jit(solution)/shard_map/ppermute | solution.py:55
  39.9 53.0 %copy-start.10 = (bf16[2,2,512,256]{3,2,1,0:T(8,128)(2,1)S(1)}, bf16[2,2,512,256]{3,2,1,0:T(8,128)(2,1)}, u32[]{:S(2)}) copy-start(bf16[2,2,512,256]{3,2,1,0:T(8,128)(2,1)} %get-tuple-element.98) | copy-start | bytes 3145732
  60.4 1.0 copy-start.8
  63.9 25.0 %collective-permute-start.13 = (bf16[2,2,512,256]{3,2,1,0:T(8,128)(2,1)}, bf16[2,2,512,256]{3,2,1,0:T(8,128)(2,1)S(1)}, u32[]{:S(2)}, u32[]{:S(2)}) collective-permute-start(bf16[2,2,512,256]{3,2,1,0:T(8,128)(2,1)} %get-tuple-element.98), channel_id=1, source_target_pairs={{0,64},{1,65},{2,66},{3,67},{4,68},{5,69},{6,70},{7,71},{8,72},{9,... | collective-permute-start | bytes 3145736 | tf_op jit(solution)/shard_map/ppermute | solution.py:55
  66.9 22.8 %collective-permute-start.14 = (bf16[2,2,512,256]{3,2,1,0:T(8,128)(2,1)S(1)}, bf16[2,2,512,256]{3,2,1,0:T(8,128)(2,1)S(1)}, u32[]{:S(2)}, u32[]{:S(2)}) collective-permute-start(bf16[2,2,512,256]{3,2,1,0:T(8,128)(2,1)S(1)} %get-tuple-element.103), channel_id=1, source_target_pairs={{0,48},{1,49},{2,50},{3,51},{4,52},{5,53},{6,54},{7,55},{8,56},{9,... | collective-permute-start | bytes 3145736 | tf_op jit(solution)/shard_map/ppermute | solution.py:55
  68.1 23.8 %collective-permute-start.15 = (bf16[2,2,512,256]{3,2,1,0:T(8,128)(2,1)S(1)}, bf16[2,2,512,256]{3,2,1,0:T(8,128)(2,1)S(1)}, u32[]{:S(2)}, u32[]{:S(2)}) collective-permute-start(bf16[2,2,512,256]{3,2,1,0:T(8,128)(2,1)S(1)} %get-tuple-element.104), channel_id=1, source_target_pairs={{0,16},{1,17},{2,18},{3,19},{4,20},{5,21},{6,22},{7,23},{8,24},{9,... | collective-permute-start | bytes 3145736 | tf_op jit(solution)/shard_map/ppermute | solution.py:55
  68.9 24.0 %collective-permute-start.18 = (bf16[64,256]{1,0:T(8,128)(2,1)S(1)}, bf16[64,256]{1,0:T(8,128)(2,1)S(1)}, u32[]{:S(2)}, u32[]{:S(2)}) collective-permute-start(bf16[64,256]{1,0:T(8,128)(2,1)S(1)} %fusion.3), channel_id=1, source_target_pairs={{0,64},{1,65},{2,66},{3,67},{4,68},{5,69},{6,70},{7,71},{8,72},{9,... | collective-permute-start | bytes 98312 | tf_op jit(solution)/shard_map/ppermute | solution.py:55
  72.1 20.8 %collective-permute-start.17 = (bf16[64,256]{1,0:T(8,128)(2,1)S(1)}, bf16[64,256]{1,0:T(8,128)(2,1)S(1)}, u32[]{:S(2)}, u32[]{:S(2)}) collective-permute-start(bf16[64,256]{1,0:T(8,128)(2,1)S(1)} %fusion.3), channel_id=1, source_target_pairs={{0,80},{1,81},{2,82},{3,83},{4,84},{5,85},{6,86},{7,87},{8,88},{9,... | collective-permute-start | bytes 98312 | tf_op jit(solution)/shard_map/ppermute | solution.py:55
  88.8 4.1 %collective-permute-start.16 = (bf16[64,256]{1,0:T(8,128)(2,1)S(1)}, bf16[64,256]{1,0:T(8,128)(2,1)S(1)}, u32[]{:S(2)}, u32[]{:S(2)}) collective-permute-start(bf16[64,256]{1,0:T(8,128)(2,1)S(1)} %fusion.3), channel_id=1, source_target_pairs={{0,112},{1,113},{2,114},{3,115},{4,116},{5,117},{6,118},{7,119},{8... | collective-permute-start | bytes 98312 | tf_op jit(solution)/shard_map/ppermute | solution.py:55
  89.7 1.0 copy-start.4
  92.0 1.0 copy-start.6
  95.1 8.6 %collective-permute-start.22 = (bf16[4,64,256]{2,1,0:T(8,128)(2,1)}, bf16[4,64,256]{2,1,0:T(8,128)(2,1)S(1)}, u32[]{:S(2)}, u32[]{:S(2)}) collective-permute-start(bf16[4,64,256]{2,1,0:T(8,128)(2,1)} %pad_maximum_fusion), channel_id=1, source_target_pairs={{0,6},{1,7},{2,0},{3,1},{4,2},{5,3},{6,4},{7,5},{8,14},{9,15},{10,... | collective-permute-start | bytes 393224 | tf_op jit(solution)/shard_map/ppermute | solution.py:55
  95.9 10.2 %collective-permute-start.23 = (bf16[4,64,256]{2,1,0:T(8,128)(2,1)}, bf16[4,64,256]{2,1,0:T(8,128)(2,1)S(1)}, u32[]{:S(2)}, u32[]{:S(2)}) collective-permute-start(bf16[4,64,256]{2,1,0:T(8,128)(2,1)} %pad_maximum_fusion), channel_id=1, source_target_pairs={{0,4},{1,5},{2,6},{3,7},{4,0},{5,1},{6,2},{7,3},{8,12},{9,13},{10,... | collective-permute-start | bytes 393224 | tf_op jit(solution)/shard_map/ppermute | solution.py:55
  97.0 9.1 %collective-permute-start.24 = (bf16[4,64,256]{2,1,0:T(8,128)(2,1)}, bf16[4,64,256]{2,1,0:T(8,128)(2,1)S(1)}, u32[]{:S(2)}, u32[]{:S(2)}) collective-permute-start(bf16[4,64,256]{2,1,0:T(8,128)(2,1)} %pad_maximum_fusion), channel_id=1, source_target_pairs={{0,2},{1,3},{2,4},{3,5},{4,6},{5,7},{6,0},{7,1},{8,10},{9,11},{10,... | collective-permute-start | bytes 393224 | tf_op jit(solution)/shard_map/ppermute | solution.py:55
  99.1 22.1 %collective-permute-start.20 = (bf16[2,2,512,256]{3,2,1,0:T(8,128)(2,1)}, bf16[2,2,512,256]{3,2,1,0:T(8,128)(2,1)}, u32[]{:S(2)}, u32[]{:S(2)}) collective-permute-start(bf16[2,2,512,256]{3,2,1,0:T(8,128)(2,1)} %get-tuple-element.115), channel_id=1, source_target_pairs={{0,48},{1,49},{2,50},{3,51},{4,52},{5,53},{6,54},{7,55},{8,56},{9,... | collective-permute-start | bytes 3145736 | tf_op jit(solution)/shard_map/ppermute | solution.py:55
  103.7 20.8 %collective-permute-start.21 = (bf16[2,2,512,256]{3,2,1,0:T(8,128)(2,1)}, bf16[2,2,512,256]{3,2,1,0:T(8,128)(2,1)}, u32[]{:S(2)}, u32[]{:S(2)}) collective-permute-start(bf16[2,2,512,256]{3,2,1,0:T(8,128)(2,1)} %get-tuple-element.116), channel_id=1, source_target_pairs={{0,16},{1,17},{2,18},{3,19},{4,20},{5,21},{6,22},{7,23},{8,24},{9,... | collective-permute-start | bytes 3145736 | tf_op jit(solution)/shard_map/ppermute | solution.py:55
  103.7 21.0 %collective-permute-start.19 = (bf16[2,2,512,256]{3,2,1,0:T(8,128)(2,1)}, bf16[2,2,512,256]{3,2,1,0:T(8,128)(2,1)S(1)}, u32[]{:S(2)}, u32[]{:S(2)}) collective-permute-start(bf16[2,2,512,256]{3,2,1,0:T(8,128)(2,1)} %get-tuple-element.107), channel_id=1, source_target_pairs={{0,64},{1,65},{2,66},{3,67},{4,68},{5,69},{6,70},{7,71},{8,72},{9,... | collective-permute-start | bytes 3145736 | tf_op jit(solution)/shard_map/ppermute | solution.py:55
  107.1 2.3 %collective-permute-start.25 = (bf16[4,256,256]{2,1,0:T(8,128)(2,1)}, bf16[4,256,256]{2,1,0:T(8,128)(2,1)}, u32[]{:S(2)}, u32[]{:S(2)}) collective-permute-start(bf16[4,256,256]{2,1,0:T(8,128)(2,1)} %constant_dynamic-slice_fusion), channel_id=1, source_target_pairs={{0,1},{1,0},{2,3},{3,2},{4,5},{5,4},{6,7},{7,6},{8,9},{9,8},{10,11... | collective-permute-start | bytes 1572872 | tf_op jit(solution)/shard_map/ppermute | solution.py:55
  111.2 2.2 %copy-start = (bf16[8,2,512,256]{3,2,1,0:T(8,128)(2,1)S(1)}, bf16[8,2,512,256]{3,2,1,0:T(8,128)(2,1)}, u32[]{:S(2)}) copy-start(bf16[8,2,512,256]{3,2,1,0:T(8,128)(2,1)} %x.3) | copy-start | bytes 12582916
  113.4 1.2 copy-start.3
  114.6 1.2 copy-start.9
  115.8 8.9 %copy-start.11 = (bf16[2,2,512,256]{3,2,1,0:T(8,128)(2,1)S(1)}, bf16[2,2,512,256]{3,2,1,0:T(8,128)(2,1)}, u32[]{:S(2)}) copy-start(bf16[2,2,512,256]{3,2,1,0:T(8,128)(2,1)} %get-tuple-element.107) | copy-start | bytes 3145732
  121.3 7.6 %copy-start.5 = (bf16[2,2,512,256]{3,2,1,0:T(8,128)(2,1)S(1)}, bf16[2,2,512,256]{3,2,1,0:T(8,128)(2,1)}, u32[]{:S(2)}) copy-start(bf16[2,2,512,256]{3,2,1,0:T(8,128)(2,1)} %copy-done.4) | copy-start | bytes 3145732
  121.3 7.6 %copy-start.7 = (bf16[2,2,512,256]{3,2,1,0:T(8,128)(2,1)S(1)}, bf16[2,2,512,256]{3,2,1,0:T(8,128)(2,1)}, u32[]{:S(2)}) copy-start(bf16[2,2,512,256]{3,2,1,0:T(8,128)(2,1)} %copy-done.6) | copy-start | bytes 3145732
  121.3 20.0 %collective-permute-start.29 = (bf16[2,2,2,2,128,128]{5,4,3,2,1,0:T(8,128)(2,1)S(1)}, bf16[2,2,2,2,128,128]{5,4,3,2,1,0:T(8,128)(2,1)S(1)}, u32[]{:S(2)}, u32[]{:S(2)}) collective-permute-start(bf16[2,2,2,2,128,128]{5,4,3,2,1,0:T(8,128)(2,1)S(1)} %get-tuple-element.135), channel_id=1, source_target_pairs={{0,16},{1,17},{2,18},{3,19},{4,20},{5,21},{6,22},{7,23},{8,24},{9,... | collective-permute-start | bytes 1572872 | tf_op jit(solution)/shard_map/ppermute | solution.py:55
  124.9 16.5 %collective-permute-start.28 = (bf16[1,2,512,256]{3,2,1,0:T(8,128)(2,1)S(1)}, bf16[1,2,512,256]{3,2,1,0:T(8,128)(2,1)S(1)}, u32[]{:S(2)}, u32[]{:S(2)}) collective-permute-start(bf16[1,2,512,256]{3,2,1,0:T(8,128)(2,1)S(1)} %get-tuple-element.161), channel_id=1, source_target_pairs={{0,48},{1,49},{2,50},{3,51},{4,52},{5,53},{6,54},{7,55},{8,56},{9,... | collective-permute-start | bytes 1572872 | tf_op jit(solution)/shard_map/ppermute | solution.py:55
  128.8 19.0 %collective-permute-start.26 = (bf16[1,2,512,256]{3,2,1,0:T(8,128)(2,1)S(1)}, bf16[1,2,512,256]{3,2,1,0:T(8,128)(2,1)S(1)}, u32[]{:S(2)}, u32[]{:S(2)}) collective-permute-start(bf16[1,2,512,256]{3,2,1,0:T(8,128)(2,1)S(1)} %get-tuple-element.162), channel_id=1, source_target_pairs={{0,48},{1,49},{2,50},{3,51},{4,52},{5,53},{6,54},{7,55},{8,56},{9,... | collective-permute-start | bytes 1572872 | tf_op jit(solution)/shard_map/ppermute | solution.py:55
  133.8 18.5 %collective-permute-start.27 = (bf16[2,2,2,2,128,128]{5,4,3,2,1,0:T(8,128)(2,1)S(1)}, bf16[2,2,2,2,128,128]{5,4,3,2,1,0:T(8,128)(2,1)S(1)}, u32[]{:S(2)}, u32[]{:S(2)}) collective-permute-start(bf16[2,2,2,2,128,128]{5,4,3,2,1,0:T(8,128)(2,1)S(1)} %get-tuple-element.134), channel_id=1, source_target_pairs={{0,16},{1,17},{2,18},{3,19},{4,20},{5,21},{6,22},{7,23},{8,24},{9,... | collective-permute-start | bytes 1572872 | tf_op jit(solution)/shard_map/ppermute | solution.py:55
  141.3 21.9 %collective-permute-start.34 = (bf16[2,2,2,2,128,128]{5,4,3,2,1,0:T(8,128)(2,1)S(1)}, bf16[2,2,2,2,128,128]{5,4,3,2,1,0:T(8,128)(2,1)S(1)}, u32[]{:S(2)}, u32[]{:S(2)}) collective-permute-start(bf16[2,2,2,2,128,128]{5,4,3,2,1,0:T(8,128)(2,1)S(1)} %get-tuple-element.147), channel_id=1, source_target_pairs={{0,16},{1,17},{2,18},{3,19},{4,20},{5,21},{6,22},{7,23},{8,24},{9,... | collective-permute-start | bytes 1572872 | tf_op jit(solution)/shard_map/ppermute | solution.py:55
  152.4 14.9 %collective-permute-start.33 = (bf16[1,2,512,256]{3,2,1,0:T(8,128)(2,1)S(1)}, bf16[1,2,512,256]{3,2,1,0:T(8,128)(2,1)S(1)}, u32[]{:S(2)}, u32[]{:S(2)}) collective-permute-start(bf16[1,2,512,256]{3,2,1,0:T(8,128)(2,1)S(1)} %get-tuple-element.163), channel_id=1, source_target_pairs={{0,112},{1,113},{2,114},{3,115},{4,116},{5,117},{6,118},{7,119},{8... | collective-permute-start | bytes 1572872 | tf_op jit(solution)/shard_map/ppermute | solution.py:55
  153.6 20.2 %collective-permute-start.30 = (bf16[1,2,512,256]{3,2,1,0:T(8,128)(2,1)S(1)}, bf16[1,2,512,256]{3,2,1,0:T(8,128)(2,1)S(1)}, u32[]{:S(2)}, u32[]{:S(2)}) collective-permute-start(bf16[1,2,512,256]{3,2,1,0:T(8,128)(2,1)S(1)} %get-tuple-element.164), channel_id=1, source_target_pairs={{0,112},{1,113},{2,114},{3,115},{4,116},{5,117},{6,118},{7,119},{8... | collective-permute-start | bytes 1572872 | tf_op jit(solution)/shard_map/ppermute | solution.py:55
  156.7 12.9 %collective-permute-start.32 = (bf16[2,2,1,2,128,128]{5,4,3,2,1,0:T(8,128)(2,1)S(1)}, bf16[2,2,1,2,128,128]{5,4,3,2,1,0:T(8,128)(2,1)S(1)}, u32[]{:S(2)}, u32[]{:S(2)}) collective-permute-start(bf16[2,2,1,2,128,128]{5,4,3,2,1,0:T(8,128)(2,1)S(1)} %get-tuple-element.146), channel_id=1, source_target_pairs={{0,16},{1,17},{2,18},{3,19},{4,20},{5,21},{6,22},{7,23},{8,24},{9,... | collective-permute-start | bytes 786440 | tf_op jit(solution)/shard_map/ppermute | solution.py:55
  158.6 14.1 %collective-permute-start.31 = (bf16[2,2,1,2,128,128]{5,4,3,2,1,0:T(8,128)(2,1)S(1)}, bf16[2,2,1,2,128,128]{5,4,3,2,1,0:T(8,128)(2,1)S(1)}, u32[]{:S(2)}, u32[]{:S(2)}) collective-permute-start(bf16[2,2,1,2,128,128]{5,4,3,2,1,0:T(8,128)(2,1)S(1)} %get-tuple-element.144), channel_id=1, source_target_pairs={{0,16},{1,17},{2,18},{3,19},{4,20},{5,21},{6,22},{7,23},{8,24},{9,... | collective-permute-start | bytes 786440 | tf_op jit(solution)/shard_map/ppermute | solution.py:55
  160.9 6.5 %copy-start.1 = (bf16[8,2,512,256]{3,2,1,0:T(8,128)(2,1)S(1)}, bf16[8,2,512,256]{3,2,1,0:T(8,128)(2,1)}, u32[]{:S(2)}) copy-start(bf16[8,2,512,256]{3,2,1,0:T(8,128)(2,1)} %x.3) | copy-start | bytes 12582916

commit v4 on v3

--- a/solution.py
+++ b/solution.py
@@ -388,7 +388,7 @@
     beyond = send(whitened(first), chan_route(-1))
     pairs(3, last, half, (0, 1, 4), 6, ((first, 0), (Y[3], 0)))
     R[3] = send(res[3], NEXT)
-    second, R[1], out = tie((second, R[1], out))
+    second, out = tie((second, out))
     beyond2 = send(whitened(second), chan_route(-1))
     pairs(4, last + half, half, (0, 1, 4), 6, ((second, 0), (Y[3], half)))
     R[4] = send(res[4], NEXT)

time: 179 us -> 182 us (1.017)
  starting transfers between devices: 51.8 us -> 55.3 us
    ppermute x35, starting transfers between devices: 51.8 us -> 55.3 us  [send(): return lax.ppermute(value, AXES, pairs)]
  transfers between devices with their start and end apart: 35 -> 35, of which waited for: 18 -> 14; matrix products, arithmetic and copies ran while one was open for 7% -> 7% of each run, Pallas kernels for 15% -> 15%
where the time goes in v4:
time: 182 us; the launch traced here: 180 us
  waiting for transfers between devices  68.9 us (38%)
  starting transfers between devices  55.3 us (30%)
  Pallas kernels  28.7 us (16%)
  other arithmetic  13.6 us (7%)
  local copies, waits for them, and re-layouts  13.5 us (7%)
    ppermute x35, waiting for transfers between devices, send(): return lax.ppermute(value, AXES, pairs)  68.9 us
    ppermute x35, starting transfers between devices, send(): return lax.ppermute(value, AXES, pairs)  55.3 us
    pallas_call x5, Pallas kernels, pairs_of(): pl.pallas_call(functools.partial(pair_kernel, offsets, side), grid=(count...  21.9 us
    unnamed x43, local copies, waits for them, and re-layouts  8.81 us
    select_n x3, other arithmetic, for_up(): return jnp.where(z == 3, own[i], Y[i])  5.76 us
    pallas_call x2, Pallas kernels, last_of(): pl.pallas_call(functools.partial(last_kernel, base, spots, count), grid=(...  4.1 us
  transfers between devices with their start and end apart: 35, of which 14 were waited for; matrix products, arithmetic and copies ran while one was open for 7% of the time, Pallas kernels for 15%

profile of v4, /device:TPU:6, one launch (start us, length us, event | category | flops | bytes accessed | tf_op | source)
XLA Modules:
  0.0 180.5 jit_solution(14118448845475599149)
XLA Ops:
  0.0 3.4 %fusion.6 = (bf16[2,2,512,256]{3,2,1,0:T(8,128)(2,1)}, bf16[2,2,512,256]{3,2,1,0:T(8,128)(2,1)S(1)}, bf16[2,2,512,256]{3,2,1,0:T(8,128)(2,1)}) fusion(bf16[8,2,512,256]{3,2,1,0:T(8,128)(2,1)} %x.3), kind=kLoop, calls=%fused_computation.53 | loop fusion | bytes 6291456 | tf_op jit(solution)/shard_map/slice | solution.py:309
  3.4 3.2 %collective-permute-start.1 = (bf16[2,2,512,256]{3,2,1,0:T(8,128)(2,1)S(1)}, bf16[2,2,512,256]{3,2,1,0:T(8,128)(2,1)S(1)}, u32[]{:S(2)}, u32[]{:S(2)}) collective-permute-start(bf16[2,2,512,256]{3,2,1,0:T(8,128)(2,1)S(1)} %get-tuple-element.77), channel_id=1, source_target_pairs={{0,64},{1,65},{2,66},{3,67},{4,68},{5,69},{6,70},{7,71},{8,72},{9,... | collective-permute-start | bytes 3145736 | tf_op jit(solution)/shard_map/ppermute | solution.py:55
  6.6 3.1 %convert_element_type.46 = f32[8,2,512,256]{3,2,1,0:T(8,128)S(1)} convert(bf16[8,2,512,256]{3,2,1,0:T(8,128)(2,1)} %x.3) | non-fusion elementwise | flops 2097152 | bytes 12582912 | tf_op jit(solution)/shard_map/convert_element_type | solution.py:320
  9.7 1.5 fusion.2
  11.3 0.4 collective-permute-start.9
  11.8 1.1 collective-permute-done.2
  12.9 0.5 collective-permute-start.3
  13.5 1.5 collective-permute-start.5
  15.0 1.4 collective-permute-start.4
  16.6 0.7 collective-permute-done.3
  17.3 3.5 %collective-permute-start.8 = (s32[2,512]{1,0:T(2,128)S(1)}, s32[2,512]{1,0:T(2,128)S(1)}, u32[]{:S(2)}, u32[]{:S(2)}) collective-permute-start(s32[2,512]{1,0:T(2,128)S(1)} %copy-done.12), channel_id=1, source_target_pairs={{0,80},{1,81},{2,82},{3,83},{4,84},{5,85},{6,86},{7,87},{8,88},{9,... | collective-permute-start | bytes 12296 | tf_op jit(solution)/shard_map/ppermute | solution.py:55
  20.7 4.4 %collective-permute-start.7 = (s32[2,512]{1,0:T(2,128)S(1)}, s32[2,512]{1,0:T(2,128)S(1)}, u32[]{:S(2)}, u32[]{:S(2)}) collective-permute-start(s32[2,512]{1,0:T(2,128)S(1)} %copy-done.12), channel_id=1, source_target_pairs={{0,96},{1,97},{2,98},{3,99},{4,100},{5,101},{6,102},{7,103},{8,104... | collective-permute-start | bytes 12296 | tf_op jit(solution)/shard_map/ppermute | solution.py:55
  25.2 1.2 collective-permute-start.6
  26.4 3.6 %collective-permute-done.9 = s32[2,512]{1,0:T(2,128)S(1)} collective-permute-done((s32[2,512]{1,0:T(2,128)S(1)}, s32[2,512]{1,0:T(2,128)S(1)}, u32[]{:S(2)}, u32[]{:S(2)}) %collective-permute-start.9) | collective-permute-done | bytes 4128 | tf_op jit(solution)/shard_map/ppermute | solution.py:55
  30.0 3.2 %collective-permute-start = (bf16[2,2,512,256]{3,2,1,0:T(8,128)(2,1)}, bf16[2,2,512,256]{3,2,1,0:T(8,128)(2,1)S(1)}, u32[]{:S(2)}, u32[]{:S(2)}) collective-permute-start(bf16[2,2,512,256]{3,2,1,0:T(8,128)(2,1)} %get-tuple-element.154), channel_id=1, source_target_pairs={{0,64},{1,65},{2,66},{3,67},{4,68},{5,69},{6,70},{7,71},{8,72},{9,... | collective-permute-start | bytes 3145736 | tf_op jit(solution)/shard_map/ppermute | solution.py:55
  33.2 1.6 broadcast_select_fusion.2
  34.9 4.0 %collective-permute-start.10 = (bf16[2,2,512,256]{3,2,1,0:T(8,128)(2,1)}, bf16[2,2,512,256]{3,2,1,0:T(8,128)(2,1)S(1)}, u32[]{:S(2)}, u32[]{:S(2)}) collective-permute-start(bf16[2,2,512,256]{3,2,1,0:T(8,128)(2,1)} %get-tuple-element.87), channel_id=1, source_target_pairs={{0,48},{1,49},{2,50},{3,51},{4,52},{5,53},{6,54},{7,55},{8,56},{9,... | collective-permute-start | bytes 3145736 | tf_op jit(solution)/shard_map/ppermute | solution.py:55
  39.0 0.8 collective-permute-start.12
  39.9 17.4 %collective-permute-done.12 = f32[64,256]{1,0:T(8,128)S(1)} collective-permute-done((f32[64,256]{1,0:T(8,128)S(1)}, f32[64,256]{1,0:T(8,128)S(1)}, u32[]{:S(2)}, u32[]{:S(2)}) %collective-permute-start.12) | collective-permute-done | bytes 65568 | tf_op jit(solution)/shard_map/ppermute | solution.py:55
  57.5 2.9 %collective-permute-done.10.rest_1_ = bf16[2,2,512,256]{3,2,1,0:T(8,128)(2,1)S(1)} collective-permute-done((bf16[2,2,512,256]{3,2,1,0:T(8,128)(2,1)}, bf16[2,2,512,256]{3,2,1,0:T(8,128)(2,1)S(1)}, u32[]{:S(2)}, u32[]{:S(2)}) %collective-permute-start.10) | collective-permute-done | bytes 1048608 | tf_op jit(solution)/shard_map/ppermute | solution.py:55
  60.4 1.0 copy-done.8
  61.5 2.4 %collective-permute-done.11.rest_3_ = bf16[2,2,512,256]{3,2,1,0:T(8,128)(2,1)} collective-permute-done((bf16[2,2,512,256]{3,2,1,0:T(8,128)(2,1)}, bf16[2,2,512,256]{3,2,1,0:T(8,128)(2,1)}, u32[]{:S(2)}, u32[]{:S(2)}) %collective-permute-start.11) | collective-permute-done | bytes 1048608 | tf_op jit(solution)/shard_map/ppermute | solution.py:55
  63.9 0.3 collective-permute-start.13
  64.2 2.7 %broadcast_select_fusion.1 = (bf16[2,2,512,256]{3,2,1,0:T(8,128)(2,1)S(1)}, bf16[2,2,512,256]{3,2,1,0:T(8,128)(2,1)S(1)}, bf16[2,2,512,256]{3,2,1,0:T(8,128)(2,1)}) fusion(bf16[2,2,512,256]{3,2,1,0:T(8,128)(2,1)S(1)} %collective-permute-done.rest_2_, pred[]{:T(512)S(6)} %eq.22, bf16[8,2,512,256]{3,2,1,0:T(8,128)(2,1)} %x.3, pred[]{:T(512)S(6)} %eq.21), kind=kLoop, calls=%fused_computation.9 | loop fusion | flops 1048576 | bytes 6291458 | tf_op jit(solution)/shard_map/jit(_where)/select_n | solution.py:316
  66.9 1.2 collective-permute-start.14
  68.1 0.8 collective-permute-start.15
  68.9 3.2 %collective-permute-start.18 = (bf16[64,256]{1,0:T(8,128)(2,1)S(1)}, bf16[64,256]{1,0:T(8,128)(2,1)S(1)}, u32[]{:S(2)}, u32[]{:S(2)}) collective-permute-start(bf16[64,256]{1,0:T(8,128)(2,1)S(1)} %fusion.3), channel_id=1, source_target_pairs={{0,64},{1,65},{2,66},{3,67},{4,68},{5,69},{6,70},{7,71},{8,72},{9,... | collective-permute-start | bytes 98312 | tf_op jit(solution)/shard_map/ppermute | solution.py:55
  72.1 16.7 %collective-permute-done.13.rest_2_ = bf16[2,2,512,256]{3,2,1,0:T(8,128)(2,1)S(1)} collective-permute-done((bf16[2,2,512,256]{3,2,1,0:T(8,128)(2,1)}, bf16[2,2,512,256]{3,2,1,0:T(8,128)(2,1)S(1)}, u32[]{:S(2)}, u32[]{:S(2)}) %collective-permute-start.13) | collective-permute-done | bytes 1048608 | tf_op jit(solution)/shard_map/ppermute | solution.py:55
  88.8 0.9 collective-permute-start.16
  89.7 1.0 copy-done.4
  90.7 1.2 collective-permute-done.15.rest_3_
  92.0 1.0 copy-done.6
  93.0 1.5 broadcast_select_fusion
  94.4 0.7 pad_maximum_fusion
  95.1 0.8 collective-permute-start.22
  95.9 1.1 collective-permute-start.23
  97.0 2.1 %collective-permute-start.24 = (bf16[4,64,256]{2,1,0:T(8,128)(2,1)}, bf16[4,64,256]{2,1,0:T(8,128)(2,1)S(1)}, u32[]{:S(2)}, u32[]{:S(2)}) collective-permute-start(bf16[4,64,256]{2,1,0:T(8,128)(2,1)} %pad_maximum_fusion), channel_id=1, source_target_pairs={{0,2},{1,3},{2,4},{3,5},{4,6},{5,7},{6,0},{7,1},{8,10},{9,11},{10,... | collective-permute-start | bytes 393224 | tf_op jit(solution)/shard_map/ppermute | solution.py:55
  99.1 4.5 %collective-permute-start.20 = (bf16[2,2,512,256]{3,2,1,0:T(8,128)(2,1)}, bf16[2,2,512,256]{3,2,1,0:T(8,128)(2,1)}, u32[]{:S(2)}, u32[]{:S(2)}) collective-permute-start(bf16[2,2,512,256]{3,2,1,0:T(8,128)(2,1)} %get-tuple-element.114), channel_id=1, source_target_pairs={{0,48},{1,49},{2,50},{3,51},{4,52},{5,53},{6,54},{7,55},{8,56},{9,... | collective-permute-start | bytes 3145736 | tf_op jit(solution)/shard_map/ppermute | solution.py:55
  103.7 2.4 %collective-permute-start.19 = (bf16[2,2,512,256]{3,2,1,0:T(8,128)(2,1)}, bf16[2,2,512,256]{3,2,1,0:T(8,128)(2,1)S(1)}, u32[]{:S(2)}, u32[]{:S(2)}) collective-permute-start(bf16[2,2,512,256]{3,2,1,0:T(8,128)(2,1)} %get-tuple-element.106), channel_id=1, source_target_pairs={{0,64},{1,65},{2,66},{3,67},{4,68},{5,69},{6,70},{7,71},{8,72},{9,... | collective-permute-start | bytes 3145736 | tf_op jit(solution)/shard_map/ppermute | solution.py:55
  106.3 0.8 constant_dynamic-slice_fusion
  107.1 2.2 %collective-permute-done.25 = bf16[4,256,256]{2,1,0:T(8,128)(2,1)} collective-permute-done((bf16[4,256,256]{2,1,0:T(8,128)(2,1)}, bf16[4,256,256]{2,1,0:T(8,128)(2,1)}, u32[]{:S(2)}, u32[]{:S(2)}) %collective-permute-start.25) | collective-permute-done | bytes 524320 | tf_op jit(solution)/shard_map/ppermute | solution.py:55
  109.3 1.8 %maximum_select_fusion.scales = bf16[4,512,256]{2,1,0:T(8,128)(2,1)S(1)} fusion(bf16[4,256,256]{2,1,0:T(8,128)(2,1)} %collective-permute-done.25, bf16[4,256,256]{2,1,0:T(8,128)(2,1)} %constant_dynamic-slice_fusion, pred[]{:T(512)S(6)} %eq.23), kind=kLoop, calls=%fused_computation.5 | loop fusion | flops 4718592 | bytes 2097153 | tf_op jit(solution)/shard_map/jit(_where)/select_n | solution.py:85
  111.2 2.2 %copy-done = bf16[8,2,512,256]{3,2,1,0:T(8,128)(2,1)S(1)} copy-done((bf16[8,2,512,256]{3,2,1,0:T(8,128)(2,1)S(1)}, bf16[8,2,512,256]{3,2,1,0:T(8,128)(2,1)}, u32[]{:S(2)}) %copy-start) | copy-done | bytes 4194328
  113.4 1.2 copy-done.3
  114.6 1.2 copy-done.9
  115.8 5.5 %shard_map.28 = (bf16[2,9,8,2,128,128]{5,4,3,2,1,0:T(8,128)(2,1)}, bf16[2,2,2,2,128,128]{5,4,3,2,1,0:T(8,128)(2,1)S(1)}) custom-call(f32[28]{0:T(128)S(1)} %div.28.inv, bf16[4,512,256]{2,1,0:T(8,128)(2,1)S(1)} %maximum_select_fusion.scales, bf16[8,2,512,256]{3,2,1,0:T(8,128)(2,1)S(1)} %copy-done, bf16[2,2,512,256]{3,2,1,0:T(8,128)(2,1)S(1)} %copy-done.9, ...), custom_call_target="tpu_custom_call" | custom-call | flops 2684354560 | bytes 8388608 | tf_op jit(solution)/shard_map/pallas_call | solution.py:163
  121.3 3.2 %collective-permute-done.21.rest_3_ = bf16[2,2,512,256]{3,2,1,0:T(8,128)(2,1)} collective-permute-done((bf16[2,2,512,256]{3,2,1,0:T(8,128)(2,1)}, bf16[2,2,512,256]{3,2,1,0:T(8,128)(2,1)}, u32[]{:S(2)}, u32[]{:S(2)}) %collective-permute-start.21) | collective-permute-done | bytes 1048608 | tf_op jit(solution)/shard_map/ppermute | solution.py:55
  124.9 3.9 %collective-permute-start.27 = (bf16[1,2,512,256]{3,2,1,0:T(8,128)(2,1)S(1)}, bf16[1,2,512,256]{3,2,1,0:T(8,128)(2,1)S(1)}, u32[]{:S(2)}, u32[]{:S(2)}) collective-permute-start(bf16[1,2,512,256]{3,2,1,0:T(8,128)(2,1)S(1)} %get-tuple-element.159), channel_id=1, source_target_pairs={{0,48},{1,49},{2,50},{3,51},{4,52},{5,53},{6,54},{7,55},{8,56},{9,... | collective-permute-start | bytes 1572872 | tf_op jit(solution)/shard_map/ppermute | solution.py:55
  128.9 4.9 %shard_map.29 = (bf16[2,9,8,2,128,128]{5,4,3,2,1,0:T(8,128)(2,1)}, bf16[2,2,2,2,128,128]{5,4,3,2,1,0:T(8,128)(2,1)S(1)}) custom-call(f32[28]{0:T(128)S(1)} %div.28.inv, bf16[4,512,256]{2,1,0:T(8,128)(2,1)S(1)} %maximum_select_fusion.scales, bf16[8,2,512,256]{3,2,1,0:T(8,128)(2,1)S(1)} %copy-done, ...), custom_call_target="tpu_custom_call", output_to_operand_aliasing={{0}: (6, {})} | custom-call | flops 2684354560 | bytes 8388608 | tf_op jit(solution)/shard_map/pallas_call | solution.py:163
  133.8 5.6 %shard_map.30 = (bf16[2,9,8,2,128,128]{5,4,3,2,1,0:T(8,128)(2,1)}, bf16[2,2,2,2,128,128]{5,4,3,2,1,0:T(8,128)(2,1)S(1)}) custom-call(f32[28]{0:T(128)S(1)} %div.28.inv, bf16[4,512,256]{2,1,0:T(8,128)(2,1)S(1)} %maximum_select_fusion.scales, bf16[8,2,512,256]{3,2,1,0:T(8,128)(2,1)S(1)} %copy-done, ...), custom_call_target="tpu_custom_call", output_to_operand_aliasing={{0}: (6, {})} | custom-call | flops 2684354560 | bytes 8388608 | tf_op jit(solution)/shard_map/pallas_call | solution.py:163
  139.3 1.9 %collective-permute-start.33 = (bf16[2,2,2,2,128,128]{5,4,3,2,1,0:T(8,128)(2,1)S(1)}, bf16[2,2,2,2,128,128]{5,4,3,2,1,0:T(8,128)(2,1)S(1)}, u32[]{:S(2)}, u32[]{:S(2)}) collective-permute-start(bf16[2,2,2,2,128,128]{5,4,3,2,1,0:T(8,128)(2,1)S(1)} %get-tuple-element.145), channel_id=1, source_target_pairs={{0,16},{1,17},{2,18},{3,19},{4,20},{5,21},{6,22},{7,23},{8,24},{9,... | collective-permute-start | bytes 1572872 | tf_op jit(solution)/shard_map/ppermute | solution.py:55
  141.4 3.0 %shard_map.31 = (bf16[2,9,8,2,128,128]{5,4,3,2,1,0:T(8,128)(2,1)}, bf16[2,2,1,2,128,128]{5,4,3,2,1,0:T(8,128)(2,1)S(1)}) custom-call(f32[28]{0:T(128)S(1)} %div.28.inv, bf16[4,512,256]{2,1,0:T(8,128)(2,1)S(1)} %maximum_select_fusion.scales, bf16[8,2,512,256]{3,2,1,0:T(8,128)(2,1)S(1)} %copy-done, ...), custom_call_target="tpu_custom_call", output_to_operand_aliasing={{0}: (5, {})} | custom-call | flops 1342177280 | bytes 4194304 | tf_op jit(solution)/shard_map/pallas_call | solution.py:163
  144.4 3.4 %collective-permute-done.26.rest_1_ = bf16[1,2,512,256]{3,2,1,0:T(8,128)(2,1)S(1)} collective-permute-done((bf16[1,2,512,256]{3,2,1,0:T(8,128)(2,1)S(1)}, bf16[1,2,512,256]{3,2,1,0:T(8,128)(2,1)S(1)}, u32[]{:S(2)}, u32[]{:S(2)}) %collective-permute-start.26) | collective-permute-done | bytes 524320 | tf_op jit(solution)/shard_map/ppermute | solution.py:55
  147.8 0.2 multiply_convert_fusion
  148.0 5.6 %collective-permute-start.32 = (bf16[1,2,512,256]{3,2,1,0:T(8,128)(2,1)S(1)}, bf16[1,2,512,256]{3,2,1,0:T(8,128)(2,1)S(1)}, u32[]{:S(2)}, u32[]{:S(2)}) collective-permute-start(bf16[1,2,512,256]{3,2,1,0:T(8,128)(2,1)S(1)} %get-tuple-element.161), channel_id=1, source_target_pairs={{0,112},{1,113},{2,114},{3,115},{4,116},{5,117},{6,118},{7,119},{8... | collective-permute-start | bytes 1572872 | tf_op jit(solution)/shard_map/ppermute | solution.py:55
  153.7 3.0 %shard_map.32 = (bf16[2,9,8,2,128,128]{5,4,3,2,1,0:T(8,128)(2,1)}, bf16[2,2,1,2,128,128]{5,4,3,2,1,0:T(8,128)(2,1)S(1)}) custom-call(f32[28]{0:T(128)S(1)} %div.28.inv, bf16[4,512,256]{2,1,0:T(8,128)(2,1)S(1)} %maximum_select_fusion.scales, bf16[8,2,512,256]{3,2,1,0:T(8,128)(2,1)S(1)} %copy-done, ...), custom_call_target="tpu_custom_call", output_to_operand_aliasing={{0}: (5, {})} | custom-call | flops 1342177280 | bytes 4194304 | tf_op jit(solution)/shard_map/pallas_call | solution.py:163
  156.7 2.0 %collective-permute-start.31 = (bf16[2,2,1,2,128,128]{5,4,3,2,1,0:T(8,128)(2,1)S(1)}, bf16[2,2,1,2,128,128]{5,4,3,2,1,0:T(8,128)(2,1)S(1)}, u32[]{:S(2)}, u32[]{:S(2)}) collective-permute-start(bf16[2,2,1,2,128,128]{5,4,3,2,1,0:T(8,128)(2,1)S(1)} %get-tuple-element.144), channel_id=1, source_target_pairs={{0,16},{1,17},{2,18},{3,19},{4,20},{5,21},{6,22},{7,23},{8,24},{9,... | collective-permute-start | bytes 786440 | tf_op jit(solution)/shard_map/ppermute | solution.py:55
  158.7 9.6 %collective-permute-done.34.res = bf16[2,2,2,2,128,128]{5,4,3,2,1,0:T(8,128)(2,1)S(1)} collective-permute-done((bf16[2,2,2,2,128,128]{5,4,3,2,1,0:T(8,128)(2,1)S(1)}, bf16[2,2,2,2,128,128]{5,4,3,2,1,0:T(8,128)(2,1)S(1)}, u32[]{:S(2)}, u32[]{:S(2)}) %collective-permute-start.34) | collective-permute-done | bytes 524320 | tf_op jit(solution)/shard_map/ppermute | solution.py:55
  168.3 1.4 shard_map.33.old
  169.6 1.4 shard_map.34.rest_1_
  171.0 1.0 copy-done.1
  172.0 2.0 %shard_map.35.rest_2_ = bf16[2,9,8,2,128,128]{5,4,3,2,1,0:T(8,128)(2,1)} custom-call(f32[28]{0:T(128)S(1)} %div.28.inv, bf16[4,512,256]{2,1,0:T(8,128)(2,1)S(1)} %maximum_select_fusion.scales, bf16[8,2,512,256]{3,2,1,0:T(8,128)(2,1)S(1)} %copy-done.1, bf16[1,2,512,256]{3,2,1,0:T(8,128)(2,1)S(1)} %collective-permute-done.32.far, ...), custom_call_target="tpu_custom_call", output_to_operand_aliasing={{}: (5, {})} | custom-call | flops 268435456 | bytes 4194304 | tf_op jit(solution)/shard_map/pallas_call | solution.py:273
  174.1 4.2 %collective-permute-done.30.rest_0_ = bf16[2,2,1,2,128,128]{5,4,3,2,1,0:T(8,128)(2,1)S(1)} collective-permute-done((bf16[2,2,1,2,128,128]{5,4,3,2,1,0:T(8,128)(2,1)S(1)}, bf16[2,2,1,2,128,128]{5,4,3,2,1,0:T(8,128)(2,1)S(1)}, u32[]{:S(2)}, u32[]{:S(2)}) %collective-permute-start.30) | collective-permute-done | bytes 262176 | tf_op jit(solution)/shard_map/ppermute | solution.py:55
  178.3 2.1 %shard_map.36 = bf16[2,9,8,2,128,128]{5,4,3,2,1,0:T(8,128)(2,1)} custom-call(f32[28]{0:T(128)S(1)} %div.28.inv, bf16[4,512,256]{2,1,0:T(8,128)(2,1)S(1)} %maximum_select_fusion.scales, bf16[8,2,512,256]{3,2,1,0:T(8,128)(2,1)S(1)} %copy-done.1, bf16[1,2,512,256]{3,2,1,0:T(8,128)(2,1)S(1)} %collective-permute-done.29.far, ...), custom_call_target="tpu_custom_call", output_to_operand_aliasing={{}: (6, {})} | custom-call | flops 268435456 | bytes 4194304 | tf_op jit(solution)/shard_map/pallas_call | solution.py:273
  (88 shorter events, 1.7 us)
Async XLA Ops:
  3.4 29.8 %collective-permute-start.1 = (bf16[2,2,512,256]{3,2,1,0:T(8,128)(2,1)S(1)}, bf16[2,2,512,256]{3,2,1,0:T(8,128)(2,1)S(1)}, u32[]{:S(2)}, u32[]{:S(2)}) collective-permute-start(bf16[2,2,512,256]{3,2,1,0:T(8,128)(2,1)S(1)} %get-tuple-element.77), channel_id=1, source_target_pairs={{0,64},{1,65},{2,66},{3,67},{4,68},{5,69},{6,70},{7,71},{8,72},{9,... | collective-permute-start | bytes 3145736 | tf_op jit(solution)/shard_map/ppermute | solution.py:55
  9.7 1.7 copy-start.12
  11.2 1.6 collective-permute-start.2
  11.3 18.7 %collective-permute-start.9 = (s32[2,512]{1,0:T(2,128)S(1)}, s32[2,512]{1,0:T(2,128)S(1)}, u32[]{:S(2)}, u32[]{:S(2)}) collective-permute-start(s32[2,512]{1,0:T(2,128)S(1)} %copy-done.12), channel_id=1, source_target_pairs={{0,64},{1,65},{2,66},{3,67},{4,68},{5,69},{6,70},{7,71},{8,72},{9,... | collective-permute-start | bytes 12296 | tf_op jit(solution)/shard_map/ppermute | solution.py:55
  12.9 4.3 %collective-permute-start.3 = (f32[64,256]{1,0:T(8,128)S(1)}, f32[64,256]{1,0:T(8,128)S(1)}, u32[]{:S(2)}, u32[]{:S(2)}) collective-permute-start(f32[64,256]{1,0:T(8,128)S(1)} %get-tuple-element.163), channel_id=1, source_target_pairs={{0,2},{1,3},{2,4},{3,5},{4,6},{5,7},{6,0},{7,1},{8,10},{9,11},{10,... | collective-permute-start | bytes 196616 | tf_op jit(solution)/shard_map/ppermute | solution.py:55
  13.5 7.2 %collective-permute-start.5 = (f32[64,256]{1,0:T(8,128)S(1)}, f32[64,256]{1,0:T(8,128)S(1)}, u32[]{:S(2)}, u32[]{:S(2)}) collective-permute-start(f32[64,256]{1,0:T(8,128)S(1)} %get-tuple-element.164), channel_id=1, source_target_pairs={{0,6},{1,7},{2,0},{3,1},{4,2},{5,3},{6,4},{7,5},{8,14},{9,15},{10,... | collective-permute-start | bytes 196616 | tf_op jit(solution)/shard_map/ppermute | solution.py:55
  15.0 10.2 %collective-permute-start.4 = (f32[64,256]{1,0:T(8,128)S(1)}, f32[64,256]{1,0:T(8,128)S(1)}, u32[]{:S(2)}, u32[]{:S(2)}) collective-permute-start(f32[64,256]{1,0:T(8,128)S(1)} %get-tuple-element.165), channel_id=1, source_target_pairs={{0,4},{1,5},{2,6},{3,7},{4,0},{5,1},{6,2},{7,3},{8,12},{9,13},{10,... | collective-permute-start | bytes 196616 | tf_op jit(solution)/shard_map/ppermute | solution.py:55
  17.3 15.9 %collective-permute-start.8 = (s32[2,512]{1,0:T(2,128)S(1)}, s32[2,512]{1,0:T(2,128)S(1)}, u32[]{:S(2)}, u32[]{:S(2)}) collective-permute-start(s32[2,512]{1,0:T(2,128)S(1)} %copy-done.12), channel_id=1, source_target_pairs={{0,80},{1,81},{2,82},{3,83},{4,84},{5,85},{6,86},{7,87},{8,88},{9,... | collective-permute-start | bytes 12296 | tf_op jit(solution)/shard_map/ppermute | solution.py:55
  20.7 12.5 %collective-permute-start.7 = (s32[2,512]{1,0:T(2,128)S(1)}, s32[2,512]{1,0:T(2,128)S(1)}, u32[]{:S(2)}, u32[]{:S(2)}) collective-permute-start(s32[2,512]{1,0:T(2,128)S(1)} %copy-done.12), channel_id=1, source_target_pairs={{0,96},{1,97},{2,98},{3,99},{4,100},{5,101},{6,102},{7,103},{8,104... | collective-permute-start | bytes 12296 | tf_op jit(solution)/shard_map/ppermute | solution.py:55
  25.2 8.0 %collective-permute-start.6 = (s32[2,512]{1,0:T(2,128)S(1)}, s32[2,512]{1,0:T(2,128)S(1)}, u32[]{:S(2)}, u32[]{:S(2)}) collective-permute-start(s32[2,512]{1,0:T(2,128)S(1)} %copy-done.12), channel_id=1, source_target_pairs={{0,112},{1,113},{2,114},{3,115},{4,116},{5,117},{6,118},{7,119},{8... | collective-permute-start | bytes 12296 | tf_op jit(solution)/shard_map/ppermute | solution.py:55
  30.0 27.5 %collective-permute-start = (bf16[2,2,512,256]{3,2,1,0:T(8,128)(2,1)}, bf16[2,2,512,256]{3,2,1,0:T(8,128)(2,1)S(1)}, u32[]{:S(2)}, u32[]{:S(2)}) collective-permute-start(bf16[2,2,512,256]{3,2,1,0:T(8,128)(2,1)} %get-tuple-element.154), channel_id=1, source_target_pairs={{0,64},{1,65},{2,66},{3,67},{4,68},{5,69},{6,70},{7,71},{8,72},{9,... | collective-permute-start | bytes 3145736 | tf_op jit(solution)/shard_map/ppermute | solution.py:55
  33.2 33.7 %copy-start.2 = (bf16[2,2,512,256]{3,2,1,0:T(8,128)(2,1)}, bf16[2,2,512,256]{3,2,1,0:T(8,128)(2,1)S(1)}, u32[]{:S(2)}) copy-start(bf16[2,2,512,256]{3,2,1,0:T(8,128)(2,1)S(1)} %collective-permute-done.1.rest_2_) | copy-start | bytes 3145732
  34.9 25.6 %collective-permute-start.10 = (bf16[2,2,512,256]{3,2,1,0:T(8,128)(2,1)}, bf16[2,2,512,256]{3,2,1,0:T(8,128)(2,1)S(1)}, u32[]{:S(2)}, u32[]{:S(2)}) collective-permute-start(bf16[2,2,512,256]{3,2,1,0:T(8,128)(2,1)} %get-tuple-element.87), channel_id=1, source_target_pairs={{0,48},{1,49},{2,50},{3,51},{4,52},{5,53},{6,54},{7,55},{8,56},{9,... | collective-permute-start | bytes 3145736 | tf_op jit(solution)/shard_map/ppermute | solution.py:55
  38.9 25.0 %collective-permute-start.11 = (bf16[2,2,512,256]{3,2,1,0:T(8,128)(2,1)}, bf16[2,2,512,256]{3,2,1,0:T(8,128)(2,1)}, u32[]{:S(2)}, u32[]{:S(2)}) collective-permute-start(bf16[2,2,512,256]{3,2,1,0:T(8,128)(2,1)} %get-tuple-element.88), channel_id=1, source_target_pairs={{0,16},{1,17},{2,18},{3,19},{4,20},{5,21},{6,22},{7,23},{8,24},{9,... | collective-permute-start | bytes 3145736 | tf_op jit(solution)/shard_map/ppermute | solution.py:55
  39.0 18.4 %collective-permute-start.12 = (f32[64,256]{1,0:T(8,128)S(1)}, f32[64,256]{1,0:T(8,128)S(1)}, u32[]{:S(2)}, u32[]{:S(2)}) collective-permute-start(f32[64,256]{1,0:T(8,128)S(1)} %add_add_fusion), channel_id=1, source_target_pairs={{0,8},{1,9},{2,10},{3,11},{4,12},{5,13},{6,14},{7,15},{8,0},{9,1},... | collective-permute-start | bytes 196616 | tf_op jit(solution)/shard_map/ppermute | solution.py:55
  39.9 53.0 %copy-start.10 = (bf16[2,2,512,256]{3,2,1,0:T(8,128)(2,1)S(1)}, bf16[2,2,512,256]{3,2,1,0:T(8,128)(2,1)}, u32[]{:S(2)}) copy-start(bf16[2,2,512,256]{3,2,1,0:T(8,128)(2,1)} %get-tuple-element.97) | copy-start | bytes 3145732
  60.4 1.0 copy-start.8
  63.9 25.0 %collective-permute-start.13 = (bf16[2,2,512,256]{3,2,1,0:T(8,128)(2,1)}, bf16[2,2,512,256]{3,2,1,0:T(8,128)(2,1)S(1)}, u32[]{:S(2)}, u32[]{:S(2)}) collective-permute-start(bf16[2,2,512,256]{3,2,1,0:T(8,128)(2,1)} %get-tuple-element.97), channel_id=1, source_target_pairs={{0,64},{1,65},{2,66},{3,67},{4,68},{5,69},{6,70},{7,71},{8,72},{9,... | collective-permute-start | bytes 3145736 | tf_op jit(solution)/shard_map/ppermute | solution.py:55
  66.9 22.8 %collective-permute-start.14 = (bf16[2,2,512,256]{3,2,1,0:T(8,128)(2,1)S(1)}, bf16[2,2,512,256]{3,2,1,0:T(8,128)(2,1)S(1)}, u32[]{:S(2)}, u32[]{:S(2)}) collective-permute-start(bf16[2,2,512,256]{3,2,1,0:T(8,128)(2,1)S(1)} %get-tuple-element.102), channel_id=1, source_target_pairs={{0,48},{1,49},{2,50},{3,51},{4,52},{5,53},{6,54},{7,55},{8,56},{9,... | collective-permute-start | bytes 3145736 | tf_op jit(solution)/shard_map/ppermute | solution.py:55
  68.1 23.8 %collective-permute-start.15 = (bf16[2,2,512,256]{3,2,1,0:T(8,128)(2,1)S(1)}, bf16[2,2,512,256]{3,2,1,0:T(8,128)(2,1)S(1)}, u32[]{:S(2)}, u32[]{:S(2)}) collective-permute-start(bf16[2,2,512,256]{3,2,1,0:T(8,128)(2,1)S(1)} %get-tuple-element.103), channel_id=1, source_target_pairs={{0,16},{1,17},{2,18},{3,19},{4,20},{5,21},{6,22},{7,23},{8,24},{9,... | collective-permute-start | bytes 3145736 | tf_op jit(solution)/shard_map/ppermute | solution.py:55
  68.9 24.0 %collective-permute-start.18 = (bf16[64,256]{1,0:T(8,128)(2,1)S(1)}, bf16[64,256]{1,0:T(8,128)(2,1)S(1)}, u32[]{:S(2)}, u32[]{:S(2)}) collective-permute-start(bf16[64,256]{1,0:T(8,128)(2,1)S(1)} %fusion.3), channel_id=1, source_target_pairs={{0,64},{1,65},{2,66},{3,67},{4,68},{5,69},{6,70},{7,71},{8,72},{9,... | collective-permute-start | bytes 98312 | tf_op jit(solution)/shard_map/ppermute | solution.py:55
  72.1 20.8 %collective-permute-start.17 = (bf16[64,256]{1,0:T(8,128)(2,1)S(1)}, bf16[64,256]{1,0:T(8,128)(2,1)S(1)}, u32[]{:S(2)}, u32[]{:S(2)}) collective-permute-start(bf16[64,256]{1,0:T(8,128)(2,1)S(1)} %fusion.3), channel_id=1, source_target_pairs={{0,80},{1,81},{2,82},{3,83},{4,84},{5,85},{6,86},{7,87},{8,88},{9,... | collective-permute-start | bytes 98312 | tf_op jit(solution)/shard_map/ppermute | solution.py:55
  88.8 4.1 %collective-permute-start.16 = (bf16[64,256]{1,0:T(8,128)(2,1)S(1)}, bf16[64,256]{1,0:T(8,128)(2,1)S(1)}, u32[]{:S(2)}, u32[]{:S(2)}) collective-permute-start(bf16[64,256]{1,0:T(8,128)(2,1)S(1)} %fusion.3), channel_id=1, source_target_pairs={{0,112},{1,113},{2,114},{3,115},{4,116},{5,117},{6,118},{7,119},{8... | collective-permute-start | bytes 98312 | tf_op jit(solution)/shard_map/ppermute | solution.py:55
  89.7 1.0 copy-start.4
  92.0 1.0 copy-start.6
  95.1 8.6 %collective-permute-start.22 = (bf16[4,64,256]{2,1,0:T(8,128)(2,1)}, bf16[4,64,256]{2,1,0:T(8,128)(2,1)S(1)}, u32[]{:S(2)}, u32[]{:S(2)}) collective-permute-start(bf16[4,64,256]{2,1,0:T(8,128)(2,1)} %pad_maximum_fusion), channel_id=1, source_target_pairs={{0,6},{1,7},{2,0},{3,1},{4,2},{5,3},{6,4},{7,5},{8,14},{9,15},{10,... | collective-permute-start | bytes 393224 | tf_op jit(solution)/shard_map/ppermute | solution.py:55
  95.9 10.2 %collective-permute-start.23 = (bf16[4,64,256]{2,1,0:T(8,128)(2,1)}, bf16[4,64,256]{2,1,0:T(8,128)(2,1)S(1)}, u32[]{:S(2)}, u32[]{:S(2)}) collective-permute-start(bf16[4,64,256]{2,1,0:T(8,128)(2,1)} %pad_maximum_fusion), channel_id=1, source_target_pairs={{0,4},{1,5},{2,6},{3,7},{4,0},{5,1},{6,2},{7,3},{8,12},{9,13},{10,... | collective-permute-start | bytes 393224 | tf_op jit(solution)/shard_map/ppermute | solution.py:55
  97.0 9.1 %collective-permute-start.24 = (bf16[4,64,256]{2,1,0:T(8,128)(2,1)}, bf16[4,64,256]{2,1,0:T(8,128)(2,1)S(1)}, u32[]{:S(2)}, u32[]{:S(2)}) collective-permute-start(bf16[4,64,256]{2,1,0:T(8,128)(2,1)} %pad_maximum_fusion), channel_id=1, source_target_pairs={{0,2},{1,3},{2,4},{3,5},{4,6},{5,7},{6,0},{7,1},{8,10},{9,11},{10,... | collective-permute-start | bytes 393224 | tf_op jit(solution)/shard_map/ppermute | solution.py:55
  99.1 22.2 %collective-permute-start.20 = (bf16[2,2,512,256]{3,2,1,0:T(8,128)(2,1)}, bf16[2,2,512,256]{3,2,1,0:T(8,128)(2,1)}, u32[]{:S(2)}, u32[]{:S(2)}) collective-permute-start(bf16[2,2,512,256]{3,2,1,0:T(8,128)(2,1)} %get-tuple-element.114), channel_id=1, source_target_pairs={{0,48},{1,49},{2,50},{3,51},{4,52},{5,53},{6,54},{7,55},{8,56},{9,... | collective-permute-start | bytes 3145736 | tf_op jit(solution)/shard_map/ppermute | solution.py:55
  103.7 20.8 %collective-permute-start.21 = (bf16[2,2,512,256]{3,2,1,0:T(8,128)(2,1)}, bf16[2,2,512,256]{3,2,1,0:T(8,128)(2,1)}, u32[]{:S(2)}, u32[]{:S(2)}) collective-permute-start(bf16[2,2,512,256]{3,2,1,0:T(8,128)(2,1)} %get-tuple-element.115), channel_id=1, source_target_pairs={{0,16},{1,17},{2,18},{3,19},{4,20},{5,21},{6,22},{7,23},{8,24},{9,... | collective-permute-start | bytes 3145736 | tf_op jit(solution)/shard_map/ppermute | solution.py:55
  103.7 21.0 %collective-permute-start.19 = (bf16[2,2,512,256]{3,2,1,0:T(8,128)(2,1)}, bf16[2,2,512,256]{3,2,1,0:T(8,128)(2,1)S(1)}, u32[]{:S(2)}, u32[]{:S(2)}) collective-permute-start(bf16[2,2,512,256]{3,2,1,0:T(8,128)(2,1)} %get-tuple-element.106), channel_id=1, source_target_pairs={{0,64},{1,65},{2,66},{3,67},{4,68},{5,69},{6,70},{7,71},{8,72},{9,... | collective-permute-start | bytes 3145736 | tf_op jit(solution)/shard_map/ppermute | solution.py:55
  107.1 2.3 %collective-permute-start.25 = (bf16[4,256,256]{2,1,0:T(8,128)(2,1)}, bf16[4,256,256]{2,1,0:T(8,128)(2,1)}, u32[]{:S(2)}, u32[]{:S(2)}) collective-permute-start(bf16[4,256,256]{2,1,0:T(8,128)(2,1)} %constant_dynamic-slice_fusion), channel_id=1, source_target_pairs={{0,1},{1,0},{2,3},{3,2},{4,5},{5,4},{6,7},{7,6},{8,9},{9,8},{10,11... | collective-permute-start | bytes 1572872 | tf_op jit(solution)/shard_map/ppermute | solution.py:55
  111.2 2.2 %copy-start = (bf16[8,2,512,256]{3,2,1,0:T(8,128)(2,1)S(1)}, bf16[8,2,512,256]{3,2,1,0:T(8,128)(2,1)}, u32[]{:S(2)}) copy-start(bf16[8,2,512,256]{3,2,1,0:T(8,128)(2,1)} %x.3) | copy-start | bytes 12582916
  113.4 1.2 copy-start.3
  114.6 1.2 copy-start.9
  115.8 8.9 %copy-start.11 = (bf16[2,2,512,256]{3,2,1,0:T(8,128)(2,1)S(1)}, bf16[2,2,512,256]{3,2,1,0:T(8,128)(2,1)}, u32[]{:S(2)}) copy-start(bf16[2,2,512,256]{3,2,1,0:T(8,128)(2,1)} %get-tuple-element.106) | copy-start | bytes 3145732
  121.3 7.6 %copy-start.5 = (bf16[2,2,512,256]{3,2,1,0:T(8,128)(2,1)S(1)}, bf16[2,2,512,256]{3,2,1,0:T(8,128)(2,1)}, u32[]{:S(2)}) copy-start(bf16[2,2,512,256]{3,2,1,0:T(8,128)(2,1)} %copy-done.4) | copy-start | bytes 3145732
  121.3 7.6 %copy-start.7 = (bf16[2,2,512,256]{3,2,1,0:T(8,128)(2,1)S(1)}, bf16[2,2,512,256]{3,2,1,0:T(8,128)(2,1)}, u32[]{:S(2)}) copy-start(bf16[2,2,512,256]{3,2,1,0:T(8,128)(2,1)} %copy-done.6) | copy-start | bytes 3145732
  121.3 20.1 %collective-permute-start.28 = (bf16[2,2,2,2,128,128]{5,4,3,2,1,0:T(8,128)(2,1)S(1)}, bf16[2,2,2,2,128,128]{5,4,3,2,1,0:T(8,128)(2,1)S(1)}, u32[]{:S(2)}, u32[]{:S(2)}) collective-permute-start(bf16[2,2,2,2,128,128]{5,4,3,2,1,0:T(8,128)(2,1)S(1)} %get-tuple-element.130), channel_id=1, source_target_pairs={{0,16},{1,17},{2,18},{3,19},{4,20},{5,21},{6,22},{7,23},{8,24},{9,... | collective-permute-start | bytes 1572872 | tf_op jit(solution)/shard_map/ppermute | solution.py:55
  124.9 16.5 %collective-permute-start.27 = (bf16[1,2,512,256]{3,2,1,0:T(8,128)(2,1)S(1)}, bf16[1,2,512,256]{3,2,1,0:T(8,128)(2,1)S(1)}, u32[]{:S(2)}, u32[]{:S(2)}) collective-permute-start(bf16[1,2,512,256]{3,2,1,0:T(8,128)(2,1)S(1)} %get-tuple-element.159), channel_id=1, source_target_pairs={{0,48},{1,49},{2,50},{3,51},{4,52},{5,53},{6,54},{7,55},{8,56},{9,... | collective-permute-start | bytes 1572872 | tf_op jit(solution)/shard_map/ppermute | solution.py:55
  128.8 19.0 %collective-permute-start.26 = (bf16[1,2,512,256]{3,2,1,0:T(8,128)(2,1)S(1)}, bf16[1,2,512,256]{3,2,1,0:T(8,128)(2,1)S(1)}, u32[]{:S(2)}, u32[]{:S(2)}) collective-permute-start(bf16[1,2,512,256]{3,2,1,0:T(8,128)(2,1)S(1)} %get-tuple-element.160), channel_id=1, source_target_pairs={{0,48},{1,49},{2,50},{3,51},{4,52},{5,53},{6,54},{7,55},{8,56},{9,... | collective-permute-start | bytes 1572872 | tf_op jit(solution)/shard_map/ppermute | solution.py:55
  139.3 31.7 %collective-permute-start.33 = (bf16[2,2,2,2,128,128]{5,4,3,2,1,0:T(8,128)(2,1)S(1)}, bf16[2,2,2,2,128,128]{5,4,3,2,1,0:T(8,128)(2,1)S(1)}, u32[]{:S(2)}, u32[]{:S(2)}) collective-permute-start(bf16[2,2,2,2,128,128]{5,4,3,2,1,0:T(8,128)(2,1)S(1)} %get-tuple-element.145), channel_id=1, source_target_pairs={{0,16},{1,17},{2,18},{3,19},{4,20},{5,21},{6,22},{7,23},{8,24},{9,... | collective-permute-start | bytes 1572872 | tf_op jit(solution)/shard_map/ppermute | solution.py:55
  141.3 27.0 %collective-permute-start.34 = (bf16[2,2,2,2,128,128]{5,4,3,2,1,0:T(8,128)(2,1)S(1)}, bf16[2,2,2,2,128,128]{5,4,3,2,1,0:T(8,128)(2,1)S(1)}, u32[]{:S(2)}, u32[]{:S(2)}) collective-permute-start(bf16[2,2,2,2,128,128]{5,4,3,2,1,0:T(8,128)(2,1)S(1)} %get-tuple-element.146), channel_id=1, source_target_pairs={{0,16},{1,17},{2,18},{3,19},{4,20},{5,21},{6,22},{7,23},{8,24},{9,... | collective-permute-start | bytes 1572872 | tf_op jit(solution)/shard_map/ppermute | solution.py:55
  148.0 23.0 %collective-permute-start.32 = (bf16[1,2,512,256]{3,2,1,0:T(8,128)(2,1)S(1)}, bf16[1,2,512,256]{3,2,1,0:T(8,128)(2,1)S(1)}, u32[]{:S(2)}, u32[]{:S(2)}) collective-permute-start(bf16[1,2,512,256]{3,2,1,0:T(8,128)(2,1)S(1)} %get-tuple-element.161), channel_id=1, source_target_pairs={{0,112},{1,113},{2,114},{3,115},{4,116},{5,117},{6,118},{7,119},{8... | collective-permute-start | bytes 1572872 | tf_op jit(solution)/shard_map/ppermute | solution.py:55
  153.6 24.6 %collective-permute-start.29 = (bf16[1,2,512,256]{3,2,1,0:T(8,128)(2,1)S(1)}, bf16[1,2,512,256]{3,2,1,0:T(8,128)(2,1)S(1)}, u32[]{:S(2)}, u32[]{:S(2)}) collective-permute-start(bf16[1,2,512,256]{3,2,1,0:T(8,128)(2,1)S(1)} %get-tuple-element.162), channel_id=1, source_target_pairs={{0,112},{1,113},{2,114},{3,115},{4,116},{5,117},{6,118},{7,119},{8... | collective-permute-start | bytes 1572872 | tf_op jit(solution)/shard_map/ppermute | solution.py:55
  156.7 17.3 %collective-permute-start.31 = (bf16[2,2,1,2,128,128]{5,4,3,2,1,0:T(8,128)(2,1)S(1)}, bf16[2,2,1,2,128,128]{5,4,3,2,1,0:T(8,128)(2,1)S(1)}, u32[]{:S(2)}, u32[]{:S(2)}) collective-permute-start(bf16[2,2,1,2,128,128]{5,4,3,2,1,0:T(8,128)(2,1)S(1)} %get-tuple-element.144), channel_id=1, source_target_pairs={{0,16},{1,17},{2,18},{3,19},{4,20},{5,21},{6,22},{7,23},{8,24},{9,... | collective-permute-start | bytes 786440 | tf_op jit(solution)/shard_map/ppermute | solution.py:55
  168.3 10.0 %collective-permute-start.30 = (bf16[2,2,1,2,128,128]{5,4,3,2,1,0:T(8,128)(2,1)S(1)}, bf16[2,2,1,2,128,128]{5,4,3,2,1,0:T(8,128)(2,1)S(1)}, u32[]{:S(2)}, u32[]{:S(2)}) collective-permute-start(bf16[2,2,1,2,128,128]{5,4,3,2,1,0:T(8,128)(2,1)S(1)} %get-tuple-element.142), channel_id=1, source_target_pairs={{0,16},{1,17},{2,18},{3,19},{4,20},{5,21},{6,22},{7,23},{8,24},{9,... | collective-permute-start | bytes 786440 | tf_op jit(solution)/shard_map/ppermute | solution.py:55
  169.6 2.4 %copy-start.1 = (bf16[8,2,512,256]{3,2,1,0:T(8,128)(2,1)S(1)}, bf16[8,2,512,256]{3,2,1,0:T(8,128)(2,1)}, u32[]{:S(2)}) copy-start(bf16[8,2,512,256]{3,2,1,0:T(8,128)(2,1)} %x.3) | copy-start | bytes 12582916
